TPU v7x, 128 devices: a whole 4x4x4 slice. The times are simulated.
128 devices in a mesh: expert: 32 (over z, x, core), wshard: 4 (over y).
Axes of the slice: x: 4, y: 4, z: 4, core: 2. Of those that a mesh axis runs over, the one named last changes fastest.
Arguments:
- tokens: bfloat16 [25216, 768], P(('expert', 'wshard')), may hold values from -6 to 6
- ln1_gain: bfloat16 [768], P('wshard'), may hold values from 0.5 to 1.5
- ln1_bias: bfloat16 [768], P('wshard'), may hold values from -2 to 2
- w_qkv: bfloat16 [768, 2304], P('wshard'), may hold values from -0.21875 to 0.21875
- w_proj: bfloat16 [768, 768], P('wshard'), may hold values from -0.875 to 0.875
- ln2_gain: bfloat16 [768], P('wshard'), may hold values from 0.5 to 1.5
- ln2_bias: bfloat16 [768], P('wshard'), may hold values from -2 to 2
- w_router: bfloat16 [768, 32], P('wshard'), may hold values from -0.15625 to 0.15625
- expert_in: bfloat16 [32, 768, 3072], P('expert'), may hold values from -0.21875 to 0.21875
- expert_out: bfloat16 [32, 3072, 768], P('expert'), may hold values from -1.75 to 1.75
- routes: int32 [25216, 2], P(('expert', 'wshard')), may hold values from 0 to 31, all different within a row; in each aligned block of 197 rows (0 to 196, 197 to 393, ...) at most 16 rows name the same one
- cotangent: bfloat16 [25216, 768], P(('expert', 'wshard')), may hold values from -6 to 6
Outputs:
- mixed: bfloat16 [25216, 768], P(('expert', 'wshard'))
- grad_tokens: float32 [25216, 768], P(('expert', 'wshard'))
- grad_ln1_gain: float32 [768], P('wshard')
- grad_ln1_bias: float32 [768], P('wshard')
- grad_w_qkv: float32 [768, 2304], P('wshard')
- grad_w_proj: float32 [768, 768], P('wshard')
- grad_ln2_gain: float32 [768], P('wshard')
- grad_ln2_bias: float32 [768], P('wshard')
- grad_w_router: float32 [768, 32], P('wshard')
- grad_expert_in: float32 [32, 768, 3072], P('expert', 'wshard')
- grad_expert_out: float32 [32, 3072, 768], P('expert', 'wshard')
Inputs may be any that keep to these rules, and one draw needn't show every extreme that they name: `routes`: each token names two different experts; among the 197 tokens of one device no expert is named more than 16 times, a bound that some block reaches.
All inputs are finite; a program needn't handle non-finite values.
Results may differ from a plain program's by a relative error of at most 0.025.
Values may be sent and summed in bfloat16 or wider, within the bound.
A program may use at most 128 MiB of HBM per device.

v0:
```python
import jax
import jax.numpy as jnp
from jax import lax
from jax.sharding import PartitionSpec as P

HEAD_DIM = 64
LENGTH = 197


epsilon = 1e-06


def normalize(values):
    centered = values - jnp.mean(values, -1, keepdims=True)
    inverse = lax.rsqrt(jnp.mean(centered * centered, -1, keepdims=True) + epsilon)
    return (centered * inverse, inverse)


def norm_back(upstream, normed, inverse, gain_vec):
    scaled = upstream * gain_vec
    return inverse * (
        scaled
        - jnp.mean(scaled, -1, keepdims=True)
        - normed * jnp.mean(scaled * normed, -1, keepdims=True)
    )


def exact_gelu(values):
    return jax.nn.gelu(values, approximate=False)


def outer_sum(left, right):
    return lax.dot_general(
        left, right, (((0,), (0,)), ((), ())), preferred_element_type=jnp.float32
    )


def back_project(upstream, weight):
    return lax.dot_general(
        upstream, weight, (((1,), (1,)), ((), ())), preferred_element_type=jnp.float32
    )


def on_device(
    tokens,
    ln1_gain,
    ln1_bias,
    w_qkv,
    w_proj,
    ln2_gain,
    ln2_bias,
    w_router,
    expert_in,
    expert_out,
    routes,
    cotangent,
):
    gathered = (
        lax.all_gather(w_qkv, "wshard", axis=0, tiled=True),
        lax.all_gather(w_proj, "wshard", axis=0, tiled=True),
        lax.all_gather(w_router, "wshard", axis=0, tiled=True),
        lax.all_gather(ln1_gain, "wshard", axis=0, tiled=True),
        lax.all_gather(ln1_bias, "wshard", axis=0, tiled=True),
        lax.all_gather(ln2_gain, "wshard", axis=0, tiled=True),
        lax.all_gather(ln2_bias, "wshard", axis=0, tiled=True),
    )
    full_qkv, full_proj, full_router = (gathered[0], gathered[1], gathered[2])
    gain_one = gathered[3].astype(jnp.float32)
    shift_one = gathered[4].astype(jnp.float32)
    gain_two = gathered[5].astype(jnp.float32)
    shift_two = gathered[6].astype(jnp.float32)
    inputs = tokens.astype(jnp.float32)
    rows_dev, model_width = inputs.shape
    images = rows_dev // LENGTH
    head_count = model_width // HEAD_DIM
    num_experts = full_router.shape[1]
    capacity = (5 * rows_dev // 2 + 8 * num_experts - 1) // (8 * num_experts) * 8
    score_scale = HEAD_DIM ** (-0.5)

    def split_heads(block_cols):
        return block_cols.reshape(images, LENGTH, head_count, HEAD_DIM)

    normed_one, inverse_one = normalize(inputs)
    first_in = (normed_one * gain_one + shift_one).astype(jnp.bfloat16)
    packed = jnp.dot(first_in, full_qkv, preferred_element_type=jnp.float32).astype(jnp.bfloat16)
    query_heads = split_heads(packed[:, :model_width])
    key_heads = split_heads(packed[:, model_width : 2 * model_width])
    value_heads = split_heads(packed[:, 2 * model_width :])
    scores = (
        jnp.einsum("iqhc,ikhc->ihqk", query_heads, key_heads, preferred_element_type=jnp.float32)
        * score_scale
    )
    row_top = jnp.max(scores, -1, keepdims=True)
    exp_scores = jnp.exp(scores - row_top)
    row_total = jnp.sum(exp_scores, -1, keepdims=True)
    probs = exp_scores / row_total
    log_total = row_top + jnp.log(row_total)
    attended = jnp.einsum(
        "ihqk,ikhc->iqhc",
        probs.astype(jnp.bfloat16),
        value_heads,
        preferred_element_type=jnp.float32,
    )
    attended = attended.astype(jnp.bfloat16).reshape(rows_dev, model_width)
    residual = inputs + jnp.dot(attended, full_proj, preferred_element_type=jnp.float32)
    normed_two, inverse_two = normalize(residual)
    second_in = (normed_two * gain_two + shift_two).astype(jnp.bfloat16)
    gate_probs = jax.nn.softmax(
        jnp.dot(second_in, full_router, preferred_element_type=jnp.float32), axis=-1
    )
    route_flat = routes.reshape(-1)
    expert_ids = jnp.arange(num_experts, dtype=jnp.int32)
    matches = (routes[:, :, None] == expert_ids).astype(jnp.float32)
    chosen = jnp.sum(matches * gate_probs[:, None, :], -1)
    hit_table = (route_flat[:, None] == expert_ids).astype(jnp.int32)
    slot_index = jnp.sum((jnp.cumsum(hit_table, 0) - hit_table) * hit_table, 1)
    outgoing = jnp.zeros((capacity, num_experts, model_width), jnp.bfloat16)
    outgoing = outgoing.at[slot_index, route_flat].set(jnp.repeat(second_in, 2, axis=0))
    arrived = lax.all_to_all(outgoing, "expert", split_axis=1, concat_axis=0, tiled=True)
    hidden = jnp.einsum("rld,ldf->rlf", arrived, expert_in, preferred_element_type=jnp.float32)
    active = exact_gelu(hidden).astype(jnp.bfloat16)
    produced_terms = jnp.einsum(
        "rlf,lfd->rld", active, expert_out, preferred_element_type=jnp.float32
    )
    produced = produced_terms.astype(jnp.bfloat16)
    returned = lax.all_to_all(produced, "expert", split_axis=0, concat_axis=1, tiled=True)
    picked = returned[slot_index, route_flat].astype(jnp.float32).reshape(rows_dev, 2, model_width)
    output = residual + jnp.sum(chosen[..., None] * picked, 1)
    mixed = output.astype(jnp.bfloat16)
    upstream = cotangent.astype(jnp.float32)
    grad_chosen = jnp.sum(upstream[:, None, :] * picked, -1)
    grad_rows = (
        (chosen[..., None] * upstream[:, None, :])
        .astype(jnp.bfloat16)
        .reshape(2 * rows_dev, model_width)
    )
    grad_outgoing = jnp.zeros((capacity, num_experts, model_width), jnp.bfloat16)
    grad_outgoing = grad_outgoing.at[slot_index, route_flat].set(grad_rows)
    grad_arrived = lax.all_to_all(grad_outgoing, "expert", split_axis=1, concat_axis=0, tiled=True)
    grad_active = jnp.einsum(
        "rld,lfd->rlf", grad_arrived, expert_out, preferred_element_type=jnp.float32
    )
    grad_second_layer = jnp.einsum(
        "rlf,rld->lfd", active, grad_arrived, preferred_element_type=jnp.float32
    )
    gelu_value, gelu_pull = jax.vjp(exact_gelu, hidden)
    grad_hidden = gelu_pull(grad_active)[0].astype(jnp.bfloat16)
    grad_first_layer = jnp.einsum(
        "rld,rlf->ldf", arrived, grad_hidden, preferred_element_type=jnp.float32
    )
    grad_in_terms = jnp.einsum(
        "rlf,ldf->rld", grad_hidden, expert_in, preferred_element_type=jnp.float32
    )
    grad_arrived_in = grad_in_terms.astype(jnp.bfloat16)
    expert_sums = (
        lax.psum_scatter(
            grad_first_layer.astype(jnp.bfloat16), "wshard", scatter_dimension=1, tiled=True
        ).astype(jnp.float32),
        lax.psum_scatter(
            grad_second_layer.astype(jnp.bfloat16), "wshard", scatter_dimension=1, tiled=True
        ).astype(jnp.float32),
    )
    first_owned = expert_sums[0]
    second_owned = expert_sums[1]
    grad_returned = lax.all_to_all(
        grad_arrived_in, "expert", split_axis=0, concat_axis=1, tiled=True
    )
    grad_second_expert = jnp.sum(
        grad_returned[slot_index, route_flat].astype(jnp.float32).reshape(rows_dev, 2, model_width),
        1,
    )
    grad_gates = jnp.sum(matches * grad_chosen[..., None], 1)
    grad_logits = (
        gate_probs * (grad_gates - jnp.sum(gate_probs * grad_gates, -1, keepdims=True))
    ).astype(jnp.bfloat16)
    grad_router = outer_sum(second_in, grad_logits)
    grad_second = grad_second_expert + back_project(grad_logits, full_router)
    grad_gain_two = jnp.sum(grad_second * normed_two, 0)
    grad_shift_two = jnp.sum(grad_second, 0)
    grad_residual = upstream + norm_back(grad_second, normed_two, inverse_two, gain_two)
    grad_branch = grad_residual.astype(jnp.bfloat16)
    grad_proj = outer_sum(attended, grad_branch)
    grad_attended = (
        back_project(grad_branch, full_proj)
        .astype(jnp.bfloat16)
        .reshape(images, LENGTH, head_count, HEAD_DIM)
    )
    scores_again = (
        jnp.einsum("iqhc,ikhc->ihqk", query_heads, key_heads, preferred_element_type=jnp.float32)
        * score_scale
    )
    probs_again = jnp.exp(scores_again - log_total)
    grad_value = jnp.einsum(
        "ihqk,iqhc->ikhc",
        probs_again.astype(jnp.bfloat16),
        grad_attended,
        preferred_element_type=jnp.float32,
    )
    grad_probs = jnp.einsum(
        "iqhc,ikhc->ihqk", grad_attended, value_heads, preferred_element_type=jnp.float32
    )
    grad_scores = (
        probs_again * (grad_probs - jnp.sum(grad_probs * probs_again, -1, keepdims=True))
    ).astype(jnp.bfloat16)
    grad_query = (
        jnp.einsum("ihqk,ikhc->iqhc", grad_scores, key_heads, preferred_element_type=jnp.float32)
        * score_scale
    )
    grad_key = (
        jnp.einsum("ihqk,iqhc->ikhc", grad_scores, query_heads, preferred_element_type=jnp.float32)
        * score_scale
    )
    grad_packed = jnp.concatenate(
        [
            grad_query.reshape(rows_dev, model_width),
            grad_key.reshape(rows_dev, model_width),
            grad_value.reshape(rows_dev, model_width),
        ],
        1,
    ).astype(jnp.bfloat16)
    grad_qkv = outer_sum(first_in, grad_packed)
    grad_first = back_project(grad_packed, full_qkv)
    grad_gain_one = jnp.sum(grad_first * normed_one, 0)
    grad_shift_one = jnp.sum(grad_first, 0)
    grad_inputs = grad_residual + norm_back(grad_first, normed_one, inverse_one, gain_one)
    summed = (
        lax.psum(grad_qkv.astype(jnp.bfloat16), "expert").astype(jnp.float32),
        lax.psum(grad_proj.astype(jnp.bfloat16), "expert").astype(jnp.float32),
        lax.psum(grad_router.astype(jnp.bfloat16), "expert").astype(jnp.float32),
        lax.psum(grad_gain_one.astype(jnp.bfloat16), "expert").astype(jnp.float32),
        lax.psum(grad_shift_one.astype(jnp.bfloat16), "expert").astype(jnp.float32),
        lax.psum(grad_gain_two.astype(jnp.bfloat16), "expert").astype(jnp.float32),
        lax.psum(grad_shift_two.astype(jnp.bfloat16), "expert").astype(jnp.float32),
    )
    owned = (
        lax.psum_scatter(
            summed[0].astype(jnp.bfloat16), "wshard", scatter_dimension=0, tiled=True
        ).astype(jnp.float32),
        lax.psum_scatter(
            summed[1].astype(jnp.bfloat16), "wshard", scatter_dimension=0, tiled=True
        ).astype(jnp.float32),
        lax.psum_scatter(
            summed[2].astype(jnp.bfloat16), "wshard", scatter_dimension=0, tiled=True
        ).astype(jnp.float32),
        lax.psum_scatter(
            summed[3].astype(jnp.bfloat16), "wshard", scatter_dimension=0, tiled=True
        ).astype(jnp.float32),
        lax.psum_scatter(
            summed[4].astype(jnp.bfloat16), "wshard", scatter_dimension=0, tiled=True
        ).astype(jnp.float32),
        lax.psum_scatter(
            summed[5].astype(jnp.bfloat16), "wshard", scatter_dimension=0, tiled=True
        ).astype(jnp.float32),
        lax.psum_scatter(
            summed[6].astype(jnp.bfloat16), "wshard", scatter_dimension=0, tiled=True
        ).astype(jnp.float32),
    )
    return (
        mixed,
        grad_inputs,
        owned[3],
        owned[4],
        owned[0],
        owned[1],
        owned[5],
        owned[6],
        owned[2],
        first_owned,
        second_owned,
    )


def solution(mesh):
    in_specs = (
        P(("expert", "wshard"), None),
        P("wshard"),
        P("wshard"),
        P("wshard", None),
        P("wshard", None),
        P("wshard"),
        P("wshard"),
        P("wshard", None),
        P("expert", None, None),
        P("expert", None, None),
        P(("expert", "wshard"), None),
        P(("expert", "wshard"), None),
    )
    out_specs = (
        P(("expert", "wshard"), None),
        P(("expert", "wshard"), None),
        P("wshard"),
        P("wshard"),
        P("wshard", None),
        P("wshard", None),
        P("wshard"),
        P("wshard"),
        P("wshard", None),
        P("expert", "wshard", None),
        P("expert", "wshard", None),
    )
    return jax.shard_map(
        on_device, mesh=mesh, in_specs=in_specs, out_specs=out_specs, check_vma=False
    )
```

profile of v0, /device:TPU:1, one launch (start us, length us, event | category | flops | bytes accessed | tf_op | source)
XLA Modules:
  0.0 574.9 jit_solution(14656040948970666705)
XLA Ops:
  15.2 9.6 %all-reduce.12 = (bf16[768]{0:T(1024)(128)(2,1)S(1)}, bf16[768]{0:T(1024)(128)(2,1)S(1)}, bf16[768]{0:T(1024)(128)(2,1)S(1)}, bf16[768]{0:T(1024)(128)(2,1)S(1)}) all-reduce(bf16[768]{0:T(1024)(128)(2,1)S(1)} %dynamic-update-slice.1, bf16[768]{0:T(1024)(128)(2,1)S(1)} %dynamic-update-slice, ...), channel_id=1, replica_groups=mesh['expert'=32,'wshard'=4] {'wshard'}, use_global_device_ids=true, to_apply=%add.2 | all-reduce | flops 3072 | bytes 12288
  28.8 10.6 %all-gather = bf16[4,192,32]{1,2,0:T(8,128)(2,1)S(1)} all-gather(bf16[1,192,32]{1,2,0:T(8,128)(2,1)} %bitcast.261), channel_id=1, replica_groups=mesh['expert'=32,'wshard'=4] {'wshard'}, dimensions={0}, use_global_device_ids=true | all-gather | bytes 61440 | tf_op jit(solution)/shard_map/all_gather | solution.py:61
  42.3 14.0 %all-gather.4.cloned.1.call-done = bf16[768,2304]{1,0:T(8,128)(2,1)} async-done(((bf16[192,2304]{1,0:T(8,128)(2,1)}), bf16[768,2304]{1,0:T(8,128)(2,1)}) %all-gather.4.cloned.1.call-update) | async-done | bytes 3538960 | tf_op jit(solution)/shard_map/all_gather | solution.py:59
  56.3 3.0 convolution_convert_fusion.3
  62.7 19.0 %all-gather.6.cloned.1.call-done = bf16[768,768]{1,0:T(8,128)(2,1)} async-done(((bf16[192,768]{1,0:T(8,128)(2,1)}), bf16[768,768]{1,0:T(8,128)(2,1)}) %all-gather.6.cloned.1.call-update) | async-done | bytes 1179664 | tf_op jit(solution)/shard_map/all_gather | solution.py:60
  86.4 24.0 %scatter_fusion = bf16[16,32,768]{2,1,0:T(8,128)(2,1)S(1)} fusion(bf16[16,32,768]{2,1,0:T(8,128)(2,1)S(1)} %broadcast.271.clone, s32[394]{0:T(512)S(1)} %bitcast.233, bf16[394,768]{1,0:T(8,128)(2,1)S(1)} %reshape.339), kind=kCustom, calls=%fused_computation.2 | custom fusion | bytes 1818704 | tf_op jit(solution)/shard_map/scatter | solution.py:118
  111.7 8.9 %all-to-all-start = ((bf16[16,32,768]{2,0,1:T(8,128)(2,1)}), bf16[16,32,768]{2,0,1:T(8,128)(2,1)S(1)}, u32[]{:S(2)}, u32[]{:S(2)}) async-start(bf16[16,32,768]{2,0,1:T(8,128)(2,1)} %copy.146), calls=%async_computation | async-start | bytes 1572864 | tf_op jit(solution)/shard_map/all_to_all | solution.py:119
  121.5 24.0 %scatter_fusion.1 = bf16[16,32,768]{2,1,0:T(8,128)(2,1)S(1)} fusion(bf16[16,32,768]{2,1,0:T(8,128)(2,1)S(1)} %broadcast.271.clone.1, s32[394]{0:T(512)S(1)} %bitcast.234, bf16[394,768]{1,0:T(8,128)(2,1)S(1)} %multiply_convert_fusion.1), kind=kCustom, calls=%fused_computation.3 | custom fusion | bytes 1818704 | tf_op jit(solution)/shard_map/scatter | solution.py:138
  146.9 7.4 %all-to-all-start.2 = ((bf16[16,32,768]{2,0,1:T(8,128)(2,1)}), bf16[16,32,768]{2,0,1:T(8,128)(2,1)S(1)}, u32[]{:S(2)}, u32[]{:S(2)}) async-start(bf16[16,32,768]{2,0,1:T(8,128)(2,1)} %copy.150), calls=%async_computation.2 | async-start | bytes 1572864 | tf_op jit(solution)/shard_map/all_to_all | solution.py:139
  154.3 4.6 fusion.24
  159.0 2.7 copy-done.7
  161.6 16.8 %fusion.43 = bf16[512,1,768]{2,0,1:T(8,128)(2,1)} fusion(bf16[1,3072,768]{2,1,0:T(8,128)(2,1)S(1)} %bitcast.264, f32[512,3072]{1,0:T(8,128)S(1)} %fusion.24), kind=kOutput, calls=%fused_computation.59 | convolution fusion | flops 2518548480 | bytes 11796480 | tf_op jit(solution)/shard_map/rlf,lfd->rld/dot_general | solution.py:122
  183.2 7.7 %all-to-all-start.1 = ((bf16[32,2,6144]{2,1,0:T(2,128)(2,1)}), bf16[32,2,6144]{2,1,0:T(2,128)(2,1)S(1)}, u32[]{:S(2)}, u32[]{:S(2)}) async-start(bf16[32,2,6144]{2,1,0:T(2,128)(2,1)} %reshape.378), calls=%async_computation.1 | async-start | bytes 1572864 | tf_op jit(solution)/shard_map/all_to_all | solution.py:126
  191.0 18.5 %fusion.6 = bf16[512,1,3072]{2,0,1:T(8,128)(2,1)S(1)} fusion(f32[512,3072]{1,0:T(8,128)} %copy-done.7, bf16[512,768]{1,0:T(8,128)(2,1)} %bitcast.253, bf16[1,3072,768]{2,1,0:T(8,128)(2,1)} %param.21), kind=kOutput, calls=%fused_computation.13 | convolution fusion | flops 2529165312 | bytes 14942208 | tf_op jit(solution)/shard_map/rld,lfd->rlf/dot_general | solution.py:140
  211.1 2.7 fusion.46
  216.0 7.4 %all-to-all-start.3 = ((bf16[32,2,6144]{2,1,0:T(2,128)(2,1)}), bf16[32,2,6144]{2,1,0:T(2,128)(2,1)S(1)}, u32[]{:S(2)}, u32[]{:S(2)}) async-start(bf16[32,2,6144]{2,1,0:T(2,128)(2,1)} %reshape.380), calls=%async_computation.3 | async-start | bytes 1572864 | tf_op jit(solution)/shard_map/all_to_all | solution.py:165
  225.9 7.4 %gather_fusion = bf16[394,768]{1,0:T(8,128)(2,1)} fusion(bf16[16,32,768]{2,1,0:T(8,128)(2,1)S(1)} %bitcast.235, s32[394]{0:T(512)S(1)} %bitcast.231), kind=kCustom, calls=%fused_computation | custom fusion | bytes 1213520 | tf_op jit(solution)/shard_map/gather | solution.py:127
  235.3 3.5 multiply_reduce_fusion.2
  240.2 6.4 %gather_fusion.1 = bf16[394,768]{1,0:T(8,128)(2,1)S(1)} fusion(bf16[16,32,768]{2,1,0:T(8,128)(2,1)S(1)} %bitcast.236, s32[394]{0:T(512)S(1)} %bitcast.232), kind=kCustom, calls=%fused_computation.1 | custom fusion | bytes 1213520 | tf_op jit(solution)/shard_map/gather | solution.py:169
  248.4 3.7 reduce_sum.210
  266.3 3.1 convolution_convert_fusion.2
  270.6 11.8 %reduce-scatter.14.cloned.1.call-done = bf16[192,768]{1,0:T(8,128)(2,1)} async-done(((bf16[768,768]{1,0:T(8,128)(2,1)}), bf16[192,768]{1,0:T(8,128)(2,1)}) %reduce-scatter.14.cloned.1.call-update) | async-done | bytes 294928 | tf_op jit(solution)/shard_map/reduce_scatter | solution.py:239
  282.4 44.8 %reduce-scatter.12.cloned.1.call-done = bf16[192,2304]{1,0:T(8,128)(2,1)} async-done(((bf16[768,2304]{1,0:T(8,128)(2,1)}), bf16[192,2304]{1,0:T(8,128)(2,1)}) %reduce-scatter.12.cloned.1.call-update) | async-done | bytes 884752 | tf_op jit(solution)/shard_map/reduce_scatter | solution.py:236
  327.3 18.6 %fusion.27 = bf16[1,3072,768]{2,1,0:T(8,128)(2,1)} fusion(bf16[512,768]{1,0:T(8,128)(2,1)S(1)} %bitcast.254, f32[512,3072]{1,0:T(8,128)} %copy-done.7), kind=kOutput, calls=%fused_computation.43 | convolution fusion | flops 2520514560 | bytes 11796480 | tf_op jit(solution)/shard_map/rlf,rld->lfd/dot_general | solution.py:143
  346.0 6.3 %fusion.26 = bf16[1,768,3072]{2,1,0:T(8,128)(2,1)} fusion(bf16[512,768]{1,0:T(8,128)(2,1)S(1)} %bitcast.246, bf16[512,1,3072]{2,0,1:T(8,128)(2,1)} %copy-done.51), kind=kOutput, calls=%fused_computation.42 | convolution fusion | flops 2418278400 | bytes 8650752 | tf_op jit(solution)/shard_map/rld,rlf->ldf/dot_general | solution.py:148
  353.0 3.5 fusion.68
  356.6 6.6 %all-reduce.11 = (bf16[768]{0:T(1024)(128)(2,1)S(1)}, bf16[768]{0:T(1024)(128)(2,1)S(1)}, bf16[768]{0:T(1024)(128)(2,1)S(1)}, bf16[768]{0:T(1024)(128)(2,1)S(1)}) all-reduce(bf16[768]{0:T(1024)(128)(2,1)S(1)} %get-tuple-element.15, ...), channel_id=2, replica_groups=mesh['expert'=32,'wshard'=4] {'wshard'}, use_global_device_ids=true, to_apply=%region_26.27.clone | all-reduce | flops 3072 | bytes 12288
  365.5 123.5 %all-reduce.9 = (bf16[192]{0:T(256)(128)(2,1)S(1)}, bf16[192]{0:T(256)(128)(2,1)S(1)}, bf16[192]{0:T(256)(128)(2,1)S(1)}, bf16[192]{0:T(256)(128)(2,1)S(1)}, bf16[192,32]{0,1:T(8,128)(2,1)S(1)}) all-reduce(bf16[192]{0:T(256)(128)(2,1)S(1)} %dynamic-slice.5, ...), channel_id=1, replica_groups=mesh['expert'=32,'wshard'=4] {'expert'}, use_global_device_ids=true, to_apply=%region_25.26 | all-reduce | flops 6912 | bytes 27648 | tf_op jit(solution)/shard_map/psum | solution.py:230
  496.2 15.3 %reduce-scatter.10.cloned.1.call-done = bf16[1,768,768]{2,1,0:T(8,128)(2,1)} async-done(((bf16[1,3072,768]{2,1,0:T(8,128)(2,1)}), bf16[1,768,768]{2,1,0:T(8,128)(2,1)}) %reduce-scatter.10.cloned.1.call-update) | async-done | bytes 1179664 | tf_op jit(solution)/shard_map/reduce_scatter | solution.py:159
  511.5 2.8 convert_element_type.246
  514.3 50.6 %reduce-scatter.8.cloned.1.call-done = bf16[1,192,3072]{2,1,0:T(8,128)(2,1)} async-done(((bf16[1,768,3072]{2,1,0:T(8,128)(2,1)}), bf16[1,192,3072]{2,1,0:T(8,128)(2,1)}) %reduce-scatter.8.cloned.1.call-update) | async-done | bytes 1179664 | tf_op jit(solution)/shard_map/reduce_scatter | solution.py:156
  564.9 2.9 convert_element_type.243
  (240 shorter events, 66.3 us)
Async XLA Ops:
  7.2 49.1 %copy-start.10 = (bf16[197,768]{1,0:T(8,128)(2,1)S(1)}, bf16[197,768]{1,0:T(8,128)(2,1)}, u32[]{:S(2)}) copy-start(bf16[197,768]{1,0:T(8,128)(2,1)} %param.12) | copy-start | bytes 907780
  7.2 49.1 %all-gather.4.cloned.1.call-start = ((), (), s32[]{:S(2)}) async-start(), calls=%async_computation.9 | async-start | bytes 4423680 | tf_op jit(solution)/shard_map/all_gather | solution.py:59
  7.9 73.7 %all-gather.6.cloned.1.call-start = ((), (), s32[]{:S(2)}) async-start(), calls=%async_computation.10 | async-start | bytes 1474560 | tf_op jit(solution)/shard_map/all_gather | solution.py:60
  24.8 31.5 %copy-start.43 = (f32[768]{0:T(1024)}, f32[768]{0:T(1024)S(1)}, u32[]{:S(2)}) copy-start(f32[768]{0:T(1024)S(1)} %convert_element_type.193) | copy-start | bytes 9220
  24.9 31.4 %copy-start.49 = (f32[768]{0:T(1024)}, f32[768]{0:T(1024)S(1)}, u32[]{:S(2)}) copy-start(f32[768]{0:T(1024)S(1)} %convert_element_type.194) | copy-start | bytes 9220
  26.0 30.3 %copy-start.45 = (f32[197]{0:T(256)}, f32[197]{0:T(256)S(1)}, u32[]{:S(2)}) copy-start(f32[197]{0:T(256)S(1)} %broadcast_multiply_fusion.5) | copy-start | bytes 2368
  27.2 56.5 %copy-start.34 = (f32[768]{0:T(1024)}, f32[768]{0:T(1024)S(1)}, u32[]{:S(2)}) copy-start(f32[768]{0:T(1024)S(1)} %convert_element_type.201) | copy-start | bytes 9220
  39.6 81.1 %copy-start.24 = (bf16[768,32]{0,1:T(8,128)(2,1)}, bf16[768,32]{0,1:T(8,128)(2,1)S(1)}, u32[]{:S(2)}) copy-start(bf16[768,32]{0,1:T(8,128)(2,1)S(1)} %reshape.362) | copy-start | bytes 147460
  42.3 14.0 %copy-start.47 = (f32[197]{0:T(256)}, f32[197]{0:T(256)S(1)}, u32[]{:S(2)}) copy-start(f32[197]{0:T(256)S(1)} %add_rsqrt_fusion.1) | copy-start | bytes 2368
  62.7 22.4 %copy-start.21 = (bf16[12,64,197]{2,1,0:T(8,128)(2,1)}, bf16[12,64,197]{2,1,0:T(8,128)(2,1)S(1)}, u32[]{:S(2)}) copy-start(bf16[12,64,197]{2,1,0:T(8,128)(2,1)S(1)} %convolution_convert_fusion.6) | copy-start | bytes 907780
  85.0 35.6 %copy-start.8 = (bf16[197,768]{1,0:T(8,128)(2,1)}, bf16[197,768]{1,0:T(8,128)(2,1)S(1)}, u32[]{:S(2)}) copy-start(bf16[197,768]{1,0:T(8,128)(2,1)S(1)} %add_convert_fusion.1) | copy-start | bytes 907780
  86.4 34.6 %copy-start.40 = (s32[197,2]{0,1:T(2,128)S(1)}, s32[197,2]{0,1:T(2,128)}, u32[]{:S(2)}) copy-start(s32[197,2]{0,1:T(2,128)} %param.22) | copy-start | bytes 4732
  111.7 35.2 %all-to-all-start = ((bf16[16,32,768]{2,0,1:T(8,128)(2,1)}), bf16[16,32,768]{2,0,1:T(8,128)(2,1)S(1)}, u32[]{:S(2)}, u32[]{:S(2)}) async-start(bf16[16,32,768]{2,0,1:T(8,128)(2,1)} %copy.146), calls=%async_computation | async-start | bytes 1572864 | tf_op jit(solution)/shard_map/all_to_all | solution.py:119
  146.9 35.4 %all-to-all-start.2 = ((bf16[16,32,768]{2,0,1:T(8,128)(2,1)}), bf16[16,32,768]{2,0,1:T(8,128)(2,1)S(1)}, u32[]{:S(2)}, u32[]{:S(2)}) async-start(bf16[16,32,768]{2,0,1:T(8,128)(2,1)} %copy.150), calls=%async_computation.2 | async-start | bytes 1572864 | tf_op jit(solution)/shard_map/all_to_all | solution.py:139
  161.6 49.5 %slice-start = ((s8[4718592]{0:T(1024)(128)(4,1)}), s8[524288]{0:T(1024)(128)(4,1)S(1)}, s32[]{:S(2)}) async-start(s8[4718592]{0:T(1024)(128)(4,1)} %bitcast.237), calls=%async_computation.17 | async-start | bytes 1048576
  183.2 32.8 %all-to-all-start.1 = ((bf16[32,2,6144]{2,1,0:T(2,128)(2,1)}), bf16[32,2,6144]{2,1,0:T(2,128)(2,1)S(1)}, u32[]{:S(2)}, u32[]{:S(2)}) async-start(bf16[32,2,6144]{2,1,0:T(2,128)(2,1)} %reshape.378), calls=%async_computation.1 | async-start | bytes 1572864 | tf_op jit(solution)/shard_map/all_to_all | solution.py:126
  191.0 20.1 %slice-start.1 = ((s8[4718592]{0:T(1024)(128)(4,1)}), s8[4194304]{0:T(1024)(128)(4,1)S(1)}, s32[]{:S(2)}) async-start(s8[4718592]{0:T(1024)(128)(4,1)} %bitcast.237), calls=%async_computation.18 | async-start | bytes 8388608
  211.1 12.8 %copy-start.18 = (bf16[197,768]{1,0:T(8,128)(2,1)S(1)}, bf16[197,768]{1,0:T(8,128)(2,1)}, u32[]{:S(2)}) copy-start(bf16[197,768]{1,0:T(8,128)(2,1)} %param.23) | copy-start | bytes 907780
  216.0 22.9 %all-to-all-start.3 = ((bf16[32,2,6144]{2,1,0:T(2,128)(2,1)}), bf16[32,2,6144]{2,1,0:T(2,128)(2,1)S(1)}, u32[]{:S(2)}, u32[]{:S(2)}) async-start(bf16[32,2,6144]{2,1,0:T(2,128)(2,1)} %reshape.380), calls=%async_computation.3 | async-start | bytes 1572864 | tf_op jit(solution)/shard_map/all_to_all | solution.py:165
  223.4 59.0 %reduce-scatter.14.cloned.1.call-start = ((), (), s32[]{:S(2)}) async-start(), calls=%async_computation.14 | async-start | bytes 1474560 | tf_op jit(solution)/shard_map/reduce_scatter | solution.py:239
  239.7 12.3 %copy-start.4 = (f32[197,768]{1,0:T(8,128)S(1)}, f32[197,768]{1,0:T(8,128)}, u32[]{:S(2)}) copy-start(f32[197,768]{1,0:T(8,128)} %copy-done.3) | copy-start | bytes 1815556
  239.8 12.3 %copy-start.25 = (bf16[768,32]{0,1:T(8,128)(2,1)S(1)}, bf16[768,32]{0,1:T(8,128)(2,1)}, u32[]{:S(2)}) copy-start(bf16[768,32]{0,1:T(8,128)(2,1)} %copy-done.24) | copy-start | bytes 147460
  246.5 12.6 %copy-start.33 = (f32[12,197]{1,0:T(8,128)S(1)}, f32[12,197]{1,0:T(8,128)}, u32[]{:S(2)}) copy-start(f32[12,197]{1,0:T(8,128)} %copy-done.32) | copy-start | bytes 28372
  246.6 12.6 %copy-start.37 = (f32[12,197]{1,0:T(8,128)S(1)}, f32[12,197]{1,0:T(8,128)}, u32[]{:S(2)}) copy-start(f32[12,197]{1,0:T(8,128)} %copy-done.36) | copy-start | bytes 28372
  248.4 13.0 %copy-start.2 = (f32[12,197,197]{1,2,0:T(8,128)S(1)}, f32[12,197,197]{1,2,0:T(8,128)}, u32[]{:S(2)}) copy-start(f32[12,197,197]{1,2,0:T(8,128)} %copy-done.1) | copy-start | bytes 5588500
  259.1 68.1 %reduce-scatter.12.cloned.1.call-start = ((), (), s32[]{:S(2)}) async-start(), calls=%async_computation.13 | async-start | bytes 4423680 | tf_op jit(solution)/shard_map/reduce_scatter | solution.py:236
  266.3 61.0 %copy-start.23 = (bf16[16,32,768]{2,0,1:T(8,128)(2,1)S(1)}, bf16[16,32,768]{2,0,1:T(8,128)(2,1)}, u32[]{:S(2)}) copy-start(bf16[16,32,768]{2,0,1:T(8,128)(2,1)} %copy-done.22) | copy-start | bytes 2359300
  269.5 95.1 %reduce-scatter.16.cloned.1.call-start = ((), (), s32[]{:S(2)}) async-start(), calls=%async_computation.15 | async-start | bytes 245760
  270.6 221.3 %all-reduce.15.cloned.1.call-start = ((), (), s32[]{:S(2)}) async-start(), calls=%async_computation.16 | async-start | bytes 2359296 | tf_op jit(solution)/shard_map/psum | solution.py:227
  327.2 18.8 %copy-start.17 = (bf16[16,32,768]{2,0,1:T(8,128)(2,1)S(1)}, bf16[16,32,768]{2,0,1:T(8,128)(2,1)}, u32[]{:S(2)}) copy-start(bf16[16,32,768]{2,0,1:T(8,128)(2,1)} %copy-done.16) | copy-start | bytes 2359300
  327.3 184.2 %reduce-scatter.10.cloned.1.call-start = ((), (), s32[]{:S(2)}) async-start(), calls=%async_computation.12 | async-start | bytes 5898240 | tf_op jit(solution)/shard_map/reduce_scatter | solution.py:159
  346.0 218.9 %reduce-scatter.8.cloned.1.call-start = ((), (), s32[]{:S(2)}) async-start(), calls=%async_computation.11 | async-start | bytes 5898240 | tf_op jit(solution)/shard_map/reduce_scatter | solution.py:156
  (36 other events, 166.6 us)
Sparse Core Ops, SparseCore 0:
  9.7 46.5 all-gather.3
  58.0 23.6 all-gather.5
  259.2 23.1 reduce-scatter.13
  284.7 42.4 reduce-scatter.11
  329.4 17.9 reduce-scatter.15
  351.0 106.9 all-reduce.14
  460.5 50.9 reduce-scatter.9
  514.0 50.8 reduce-scatter.7
where the time goes:
time: 584 us; the launch traced here: 575 us
  waiting for transfers between devices  157 us (27%)
  blocking collectives  150 us (26%)
  local copies, waits for them, and re-layouts  94.8 us (16%)
  matrix products  89.8 us (15%)
  other arithmetic  33.9 us (6%)
  starting transfers between devices  32.2 us (6%)
  between operations  16.8 us (3%)
    psum x1, blocking collectives, on_device(): lax.psum(grad_gain_one.astype(jnp.bfloat16), 'expert').astype(jnp.float32)  124 us
    reduce_scatter x1, waiting for transfers between devices, on_device(): lax.psum_scatter(grad_first_layer.astype(jnp.bfloat16), 'wshard', scatter...  50.6 us
    reduce_scatter x1, waiting for transfers between devices, on_device(): lax.psum_scatter(summed[0].astype(jnp.bfloat16), 'wshard', scatter_dimens...  44.8 us
    scatter x2, local copies, waits for them, and re-layouts, on_device(): outgoing.at[slot_index, route_flat].set(jnp.repeat(second_in, 2, axis=0))  25.3 us
    scatter x2, local copies, waits for them, and re-layouts, on_device(): grad_outgoing = grad_outgoing.at[slot_index, route_flat].set(grad_rows)  25.3 us
    unnamed x135, local copies, waits for them, and re-layouts  20.5 us
    all_gather x1, waiting for transfers between devices, on_device(): lax.all_gather(w_proj, 'wshard', axis=0, tiled=True)  19 us
    dot_general x1, matrix products, on_device(): jnp.einsum('rlf,rld->lfd', active, grad_arrived, preferred_element_type=j...  18.6 us
  transfers between devices with their start and end apart: 12, of which 6 were waited for; matrix products, arithmetic and copies ran while one was open for 28% of the time, Pallas kernels for 0%

commit v1 on v0

v1 whole, which is shorter than its diff:
```python
import functools

import jax
import jax.numpy as jnp
from jax import lax
from jax.experimental import pallas as pl
from jax.experimental.pallas import tpu as pltpu
from jax.sharding import PartitionSpec as P

HEAD_DIM = 64
EPSILON = 1e-06
F32 = jnp.float32
BF16 = jnp.bfloat16
LANES = 128
MIB = 1 << 20


def mm(left, right, left_dim=1, right_dim=0):
    return lax.dot_general(
        left, right, (((left_dim,), (right_dim,)), ((), ())), preferred_element_type=F32
    )


def normalize(values):
    centered = values - jnp.mean(values, -1, keepdims=True)
    inverse = lax.rsqrt(jnp.mean(centered * centered, -1, keepdims=True) + EPSILON)
    return centered * inverse, inverse


def norm_back(upstream, normed, inverse, gain):
    scaled = upstream * gain
    return inverse * (
        scaled
        - jnp.mean(scaled, -1, keepdims=True)
        - normed * jnp.mean(scaled * normed, -1, keepdims=True)
    )


def lane_iota(rows, columns=LANES):
    return lax.broadcasted_iota(jnp.int32, (rows, columns), 1)


MESH = pl.DeviceIdType.MESH
SIDE = 4


def remote(source, target, send, receive, expert, shard):
    return pltpu.make_async_remote_copy(
        src_ref=source, dst_ref=target, send_sem=send, recv_sem=receive,
        device_id=(expert, shard), device_id_type=MESH,
    )


def greet(devices):
    barrier = pltpu.get_barrier_semaphore()
    for expert, shard in devices:
        pl.semaphore_signal(barrier, inc=1, device_id=(expert, shard), device_id_type=MESH)
    pl.semaphore_wait(barrier, len(devices))


class RowGather:
    def __init__(self, shard_ref, full_ref, split, send, receive, expert, shard):
        self.rows, columns = shard_ref.shape
        self.shard_ref, self.full_ref = shard_ref, full_ref
        self.send, self.receive = send, receive
        self.expert, self.shard = expert, shard
        core = lax.rem(expert, 2)
        self.split = split
        self.sibling = expert + 1 - 2 * core
        self.after, self.before = lax.rem(shard + 1, SIDE), lax.rem(shard + 3, SIDE)
        self.across = lax.rem(shard + 2, SIDE)
        if split:
            half = columns // 2
            self.columns = pl.ds(pl.multiple_of(core * half, LANES), half)
            self.others = pl.ds(pl.multiple_of((1 - core) * half, LANES), half)
        else:
            self.columns = self.others = pl.ds(0, columns)

    def at(self, shard, start, count, columns):
        place = pl.multiple_of(shard * self.rows + start, 16)
        return self.full_ref.at[pl.ds(place, count), columns]

    def ring(self, number, source, target, shard):
        return remote(
            source, target, self.send.at[number], self.receive.at[number], self.expert, shard
        )

    def first(self):
        target = self.at(self.shard, 0, self.rows, self.columns)
        source = self.shard_ref.at[:, self.columns]
        self.to_after = self.ring(0, source, target, self.after)
        self.to_before = self.ring(1, source, target, self.before)
        self.own = pltpu.make_async_copy(
            self.shard_ref, self.at(self.shard, 0, self.rows, pl.ds(0, self.shard_ref.shape[1])),
            self.send.at[8],
        )
        self.to_after.start()
        self.to_before.start()
        self.own.start()

    def hand(self, number, shard, start, count):
        if not self.split:
            return None
        block = self.at(shard, start, count, self.columns)
        copy = remote(
            block, block, self.send.at[number], self.receive.at[number], self.sibling, self.shard
        )
        copy.start()
        return copy

    def second(self):
        half = self.rows // 2
        self.to_after.wait_recv()
        top = self.at(self.before, 0, half, self.columns)
        self.pass_after = self.ring(2, top, top, self.after)
        self.pass_after.start()
        self.to_before.wait_recv()
        bottom = self.at(self.after, half, half, self.columns)
        self.pass_before = self.ring(3, bottom, bottom, self.before)
        self.pass_before.start()
        self.handed = [
            self.hand(4, self.before, 0, self.rows),
            self.hand(5, self.after, 0, self.rows),
        ]

    def third(self):
        half = self.rows // 2
        self.pass_after.wait_recv()
        self.handed.append(self.hand(6, self.across, 0, half))
        self.pass_before.wait_recv()
        self.handed.append(self.hand(7, self.across, half, half))

    def finish(self):
        self.own.wait()
        for copy in self.handed:
            if copy is not None:
                copy.wait_recv()

    def drain(self):
        for copy in (self.to_after, self.to_before, self.pass_after, self.pass_before, *self.handed):
            if copy is not None:
                copy.wait_send()


def exchange_peers(expert):
    return [
        lax.rem(expert // 8 + dz, SIDE) * 8 + lax.rem(lax.rem(expert // 2, SIDE) + dx, SIDE) * 2
        + lax.rem(expert + dc, 2)
        for dz, dx, dc in exchange_order()
    ]


def exchange_order():
    reach = [0, 1, 2, 1]
    steps = [(dz, dx, dc) for dz in range(SIDE) for dx in range(SIDE) for dc in range(2)]
    return sorted(steps[1:], key=lambda step: -reach[step[0]] - reach[step[1]])


def exchange_start(source_ref, target_ref, send, receive, local, expert, shard, capacity):
    own = pl.ds(pl.multiple_of(expert * capacity, 16), capacity)
    copies = []
    for number, peer in enumerate(exchange_peers(expert)):
        block = pl.ds(pl.multiple_of(peer * capacity, 16), capacity)
        copy = remote(
            source_ref.at[block, :], target_ref.at[own, :], send.at[number], receive.at[number], peer, shard
        )
        copy.start()
        copies.append(copy)
    keep = pltpu.make_async_copy(source_ref.at[own, :], target_ref.at[own, :], local)
    keep.start()
    return copies, keep


def exchange_wait(copies, keep):
    keep.wait()
    for copy in copies:
        copy.wait()


def exchange_kernel(capacity, source_ref, target_ref, send, receive, local):
    expert, shard = lax.axis_index("expert"), lax.axis_index("wshard")
    greet([(peer, shard) for peer in exchange_peers(expert)])
    exchange_wait(*exchange_start(source_ref, target_ref, send, receive, local, expert, shard, capacity))


def exchange(rows, capacity, collective_id):
    return pl.pallas_call(
        functools.partial(exchange_kernel, capacity),
        out_shape=jax.ShapeDtypeStruct(rows.shape, rows.dtype),
        in_specs=[pl.BlockSpec(memory_space=pl.ANY)],
        out_specs=pl.BlockSpec(memory_space=pl.ANY),
        scratch_shapes=[
            pltpu.SemaphoreType.DMA((31,)), pltpu.SemaphoreType.DMA((31,)), pltpu.SemaphoreType.DMA,
        ],
        compiler_params=pltpu.CompilerParams(collective_id=collective_id, has_side_effects=True),
        cost_estimate=pl.CostEstimate(flops=0, bytes_accessed=4 * MIB, transcendentals=0),
        name="exchange_rows",
    )(rows)


def reduce_kernel(
    g_ref, s_ref, wide_ref, small_ref,
    paired, summed, side, first_in, second, second_in, third_in, piece, line, plane, gathered,
    s_pair, s_sum, s_in, s_out, s_other, send, receive, s_send, s_receive,
):
    expert, shard = lax.axis_index("expert"), lax.axis_index("wshard")
    core = lax.rem(expert, 2)
    x, z = lax.rem(expert // 2, SIDE), expert // 8
    sibling = expert + 1 - 2 * core
    first, second_at = x * (1 - core) + z * core, z * (1 - core) + x * core
    first_step, second_step = 2 + 6 * core, 8 - 6 * core

    def turn(place, by):
        return lax.rem(place + by, SIDE)

    def on_first(by):
        return expert + (turn(first, by) - first) * first_step

    def on_second(by):
        return expert + (turn(second_at, by) - second_at) * second_step

    greet(
        [(sibling, shard)]
        + [(on_first(by), shard) for by in (1, 2, 3)]
        + [(on_second(by), shard) for by in (1, 2, 3)]
        + [(expert, turn(shard, by)) for by in (1, 2, 3)]
    )
    rows = s_ref.shape[1]
    part = rows // 2
    quarter = rows // 4
    count = [0]
    small_count = [0]
    started = []

    def go(source, target, to_expert, to_shard, small=False):
        number = small_count if small else count
        sends, receives = (s_send, s_receive) if small else (send, receive)
        copy = remote(
            source, target, sends.at[number[0]], receives.at[number[0]], to_expert, to_shard
        )
        number[0] += 1
        copy.start()
        started.append(copy)
        return copy

    order = (2, 1, 3, 0)
    theirs = second_at
    pair = [
        go(g_ref.at[(1 - core) * SIDE + turn(theirs, by)], paired.at[number], sibling, shard)
        for number, by in enumerate(order)
    ]
    small_pair = go(s_ref, s_pair, sibling, shard, True)

    def add_pair(number):
        pair[number].wait_recv()
        own = g_ref[core * SIDE + turn(first, order[number])]
        summed[number] = (own.astype(F32) + paired[number].astype(F32)).astype(BF16)

    half = 2 * rows
    add_pair(0)
    relay_up = go(summed.at[0, pl.ds(0, half)], side.at[0], on_first(1), shard)
    relay_down = go(summed.at[0, pl.ds(half, half)], side.at[1], on_first(3), shard)
    add_pair(1)
    add_pair(2)
    small_pair.wait_recv()
    s_sum[...] = (s_ref[...].astype(F32) + s_pair[...].astype(F32)).astype(BF16)
    mine = pl.ds(pl.multiple_of(core * part, 16), part)
    others = pl.ds(pl.multiple_of((1 - core) * part, 16), part)
    small_along = [
        go(s_sum.at[turn(shard, by), mine, :], s_in.at[by - 1], expert, turn(shard, by), True)
        for by in (1, 2, 3)
    ]
    relay_up.wait_recv()
    summed[1, :half] = (summed[1, :half].astype(F32) + side[0].astype(F32)).astype(BF16)
    up = go(summed.at[1], first_in.at[0], on_first(1), shard)
    relay_down.wait_recv()
    summed[2, half:] = (summed[2, half:].astype(F32) + side[1].astype(F32)).astype(BF16)
    down = go(summed.at[2], first_in.at[1], on_first(3), shard)
    add_pair(3)

    for copy in small_along:
        copy.wait_recv()
    s_out[0] = (
        s_sum[shard, mine, :].astype(F32) + s_in[0].astype(F32) + s_in[1].astype(F32) + s_in[2].astype(F32)
    ).astype(BF16)
    small_first = [
        go(s_out.at[0], s_in.at[2 + by], on_first(by), shard, True) for by in (1, 2, 3)
    ]

    up.wait_recv()
    down.wait_recv()
    for own_shard in range(SIDE):
        for place in range(SIDE):
            at = pl.ds(own_shard * rows + place * quarter, quarter)
            second[place, own_shard] = (
                summed[3, at, :].astype(F32) + first_in[0, at, :].astype(F32) + first_in[1, at, :].astype(F32)
            ).astype(BF16)
    along_second = [
        go(second.at[turn(second_at, by)], second_in.at[by - 1], on_second(by), shard) for by in (2, 1, 3)
    ]
    for copy in small_first:
        copy.wait_recv()
    s_out[1] = (
        s_out[0].astype(F32) + s_in[3].astype(F32) + s_in[4].astype(F32) + s_in[5].astype(F32)
    ).astype(BF16)
    small_second = [
        go(s_out.at[1], s_in.at[5 + by], on_second(by), shard, True) for by in (1, 2, 3)
    ]
    for copy in along_second:
        copy.wait_recv()
    piece[...] = (
        second[second_at].astype(F32) + second_in[0].astype(F32) + second_in[1].astype(F32)
        + second_in[2].astype(F32)
    ).astype(BF16)
    along_shard = [
        go(piece.at[turn(shard, by)], third_in.at[by - 1], expert, turn(shard, by)) for by in (2, 1, 3)
    ]
    for copy in small_second:
        copy.wait_recv()
    s_out[2] = (
        s_out[1].astype(F32) + s_in[6].astype(F32) + s_in[7].astype(F32) + s_in[8].astype(F32)
    ).astype(BF16)
    small_back = go(s_out.at[2], s_other, sibling, shard, True)
    for copy in along_shard:
        copy.wait_recv()
    line[second_at] = (
        piece[shard].astype(F32) + third_in[0].astype(F32) + third_in[1].astype(F32) + third_in[2].astype(F32)
    ).astype(BF16)
    back_second = [
        go(line.at[second_at], line.at[second_at], on_second(by), shard) for by in (2, 1, 3)
    ]
    small_back.wait_recv()
    small_ref[mine, :] = s_out[2].astype(F32)
    small_ref[others, :] = s_other[...].astype(F32)
    for copy in back_second:
        copy.wait_recv()
    plane[first] = line[...].reshape(rows, line.shape[-1])
    back_first = [
        go(plane.at[first], plane.at[first], on_first(by), shard) for by in (2, 1, 3)
    ]
    own_back = go(plane.at[first], gathered.at[first], sibling, shard)
    hands = []
    for copy, by in zip(back_first, (2, 1, 3)):
        copy.wait_recv()
        came = turn(first, SIDE - by)
        hands.append(go(plane.at[came], gathered.at[came], sibling, shard))
    wide_ref[pl.ds(core * SIDE, SIDE)] = plane[...].astype(F32)
    own_back.wait_recv()
    for copy in hands:
        copy.wait_recv()
    wide_ref[pl.ds((1 - core) * SIDE, SIDE)] = gathered[...].astype(F32)
    for copy in started:
        copy.wait_send()


def reduce_all(blocks, small, collective_id):
    _, total_rows, columns = blocks.shape
    rows = total_rows // SIDE
    quarter, part = rows // 4, rows // 2
    vmem = pltpu.VMEM
    return pl.pallas_call(
        reduce_kernel,
        out_shape=(
            jax.ShapeDtypeStruct((2 * SIDE, rows, columns), F32),
            jax.ShapeDtypeStruct((rows, LANES), F32),
        ),
        in_specs=[pl.BlockSpec(memory_space=vmem)] * 2,
        out_specs=[pl.BlockSpec(memory_space=vmem)] * 2,
        scratch_shapes=[
            vmem((SIDE, total_rows, columns), BF16),
            vmem((SIDE, total_rows, columns), BF16),
            vmem((2, 2 * rows, columns), BF16),
            vmem((2, total_rows, columns), BF16),
            vmem((SIDE, SIDE, quarter, columns), BF16),
            vmem((3, SIDE, quarter, columns), BF16),
            vmem((3, quarter, columns), BF16),
            vmem((SIDE, quarter, columns), BF16),
            vmem((SIDE, quarter, columns), BF16),
            vmem((SIDE, rows, columns), BF16),
            vmem((SIDE, rows, columns), BF16),
            vmem((SIDE, rows, LANES), BF16),
            vmem((SIDE, rows, LANES), BF16),
            vmem((9, part, LANES), BF16),
            vmem((3, part, LANES), BF16),
            vmem((part, LANES), BF16),
            pltpu.SemaphoreType.DMA((28,)),
            pltpu.SemaphoreType.DMA((28,)),
            pltpu.SemaphoreType.DMA((11,)),
            pltpu.SemaphoreType.DMA((11,)),
        ],
        compiler_params=pltpu.CompilerParams(
            vmem_limit_bytes=48 * MIB, collective_id=collective_id, has_side_effects=True
        ),
        cost_estimate=pl.CostEstimate(flops=0, bytes_accessed=32 * MIB, transcendentals=0),
        name="reduce_all",
    )(blocks, small.reshape(SIDE, rows, LANES))


def forward_kernel(
    experts, capacity, x_ref, g_ref, routes_ref, wq_shard, wp_shard, ws_shard,
    wq_out, wp_out, ws_ref, ln_ref, qkv_ref, lse_ref, o_ref, x2_ref, gates_ref, pick0_ref, pick1_ref, arrived_ref,
    wq_ref, wp_ref, small_ref, send_ref, sends, receives, ex_send, ex_receive, local,
):
    rows, width = x_ref.shape
    expert, shard = lax.axis_index("expert"), lax.axis_index("wshard")
    core = lax.rem(expert, 2)
    greet(
        [(expert, lax.rem(shard + 1, SIDE)), (expert, lax.rem(shard + 3, SIDE))]
        + [(peer, shard) for peer in exchange_peers(expert)]
    )
    small, first_w, second_w = [
        RowGather(shard_ref, full_ref, split, sends.at[number], receives.at[number], expert, shard)
        for number, (shard_ref, full_ref, split) in enumerate(
            ((ws_shard, small_ref, False), (wq_shard, wq_ref, True), (wp_shard, wp_ref, True))
        )
    ]
    small.first()
    first_w.first()
    x = x_ref[...].astype(F32)
    normed, _ = normalize(x)
    small.second()
    first_w.second()
    second_w.first()
    small.third()
    small.finish()
    lane = lane_iota(rows)
    both = small_ref[...].astype(F32)
    vectors = both.T[experts : experts + 8, :]
    ln_ref[...] = vectors
    ws_ref[...] = jnp.where(lane_iota(width) < experts, both, 0.0).astype(BF16)
    h1 = (normed * vectors[0:1, :] + vectors[1:2, :]).astype(BF16)
    first_w.third()
    second_w.second()
    first_w.finish()
    keep_first = pltpu.make_async_copy(wq_ref, wq_out, local.at[1])
    keep_first.start()
    qkv_ref[...] = mm(h1, wq_ref[...]).astype(BF16)
    scale = HEAD_DIM ** (-0.5)
    lse_all = jnp.zeros((rows, LANES), F32)
    for pair in range(width // LANES):
        if pair == 2:
            second_w.third()
        at = pair * LANES
        q = qkv_ref[:, at : at + LANES]
        k = qkv_ref[:, width + at : width + at + LANES]
        v = qkv_ref[:, 2 * width + at : 2 * width + at + LANES]
        halves = []
        for half in range(2):
            own = (lane // HEAD_DIM) == half
            s = mm(jnp.where(own, q, jnp.zeros_like(q)), k, 1, 1) * scale
            top = jnp.max(s, -1, keepdims=True)
            e = jnp.exp(s - top)
            total = jnp.sum(e, -1, keepdims=True)
            lse_all = jnp.where(lane == 2 * pair + half, top + jnp.log(total), lse_all)
            halves.append(mm((e / total).astype(BF16), v))
        o_ref[:, at : at + LANES] = jnp.where(lane < HEAD_DIM, halves[0], halves[1]).astype(BF16)
    lse_ref[...] = lse_all
    second_w.finish()
    keep_second = pltpu.make_async_copy(wp_ref, wp_out, local.at[2])
    keep_second.start()
    x2 = x + mm(o_ref[...], wp_ref[...])
    x2_ref[...] = x2
    normed2, _ = normalize(x2)
    h2 = (normed2 * vectors[2:3, :] + vectors[3:4, :]).astype(BF16)
    logits = jnp.where(lane < experts, mm(h2, ws_ref[...]), -jnp.inf)
    e = jnp.exp(logits - jnp.max(logits, -1, keepdims=True))
    gates = e / jnp.sum(e, -1, keepdims=True)
    gates_ref[...] = gates
    routes = routes_ref[...]
    match = [lane == routes[:, k : k + 1] for k in range(2)]
    hits = (match[0] | match[1]).astype(F32).astype(BF16)
    earlier = lax.broadcasted_iota(jnp.int32, (rows, rows), 0) > lane_iota(rows, rows)
    before = mm(earlier.astype(F32).astype(BF16), hits)
    slots = lane_iota(rows, experts * capacity).astype(F32)
    g = g_ref[...].astype(F32)
    picks, grads = [], []
    for k in range(2):
        slot = jnp.sum(jnp.where(match[k], before, 0.0), -1, keepdims=True)
        place = (routes[:, k : k + 1] * capacity).astype(F32) + slot
        picks.append((slots == place).astype(F32).astype(BF16))
        chosen = jnp.sum(jnp.where(match[k], gates, 0.0), -1, keepdims=True)
        grads.append((chosen * g).astype(BF16))
    pick0_ref[...] = picks[0]
    pick1_ref[...] = picks[1]
    send_ref[:, :width] = mm(picks[0] + picks[1], h2, 0, 0).astype(BF16)
    send_ref[:, width:] = (mm(picks[0], grads[0], 0, 0) + mm(picks[1], grads[1], 0, 0)).astype(BF16)
    copies, keep = exchange_start(
        send_ref, arrived_ref, ex_send, ex_receive, local.at[0], expert, shard, capacity
    )
    for gather in (small, first_w, second_w):
        gather.drain()
    keep_first.wait()
    keep_second.wait()
    exchange_wait(copies, keep)


def forward(tokens, cotangent, routes, wq, wp, ws, experts, capacity):
    rows, width = tokens.shape
    slots = experts * capacity
    vmem, anywhere = pl.BlockSpec(memory_space=pltpu.VMEM), pl.BlockSpec(memory_space=pl.ANY)
    return pl.pallas_call(
        functools.partial(forward_kernel, experts, capacity),
        out_shape=(
            jax.ShapeDtypeStruct((width, 3 * width), BF16),
            jax.ShapeDtypeStruct((width, width), BF16),
            jax.ShapeDtypeStruct((width, LANES), BF16),
            jax.ShapeDtypeStruct((8, width), F32),
            jax.ShapeDtypeStruct((rows, 3 * width), BF16),
            jax.ShapeDtypeStruct((rows, LANES), F32),
            jax.ShapeDtypeStruct((rows, width), BF16),
            jax.ShapeDtypeStruct((rows, width), F32),
            jax.ShapeDtypeStruct((rows, LANES), F32),
            jax.ShapeDtypeStruct((rows, slots), BF16),
            jax.ShapeDtypeStruct((rows, slots), BF16),
            jax.ShapeDtypeStruct((slots, 2 * width), BF16),
        ),
        in_specs=[vmem] * 6,
        out_specs=[anywhere] * 2 + [vmem] * 9 + [anywhere],
        scratch_shapes=[
            pltpu.VMEM((width, 3 * width), BF16),
            pltpu.VMEM((width, width), BF16),
            pltpu.VMEM((width, LANES), BF16),
            pltpu.VMEM((slots, 2 * width), BF16),
            pltpu.SemaphoreType.DMA((3, 9)),
            pltpu.SemaphoreType.DMA((3, 8)),
            pltpu.SemaphoreType.DMA((31,)),
            pltpu.SemaphoreType.DMA((31,)),
            pltpu.SemaphoreType.DMA((3,)),
        ],
        compiler_params=pltpu.CompilerParams(
            vmem_limit_bytes=48 * MIB, collective_id=1, has_side_effects=True
        ),
        cost_estimate=pl.CostEstimate(
            flops=2 * rows * width * 6 * width, bytes_accessed=16 * MIB, transcendentals=rows * rows * 12
        ),
        name="attention_forward",
    )(tokens, cotangent, routes, wq, wp, ws)


def expert_kernel(arrived_ref, w1_ref, w2_ref, a_ref, du_ref, gw1_ref, gw2_ref):
    width = w1_ref.shape[0]
    z = arrived_ref[:, :width]
    dy = arrived_ref[:, width:]
    u = mm(z, w1_ref[...])
    da = mm(dy, w2_ref[...], 1, 1)
    phi = 0.5 * (1.0 + lax.erf(u * (2.0**-0.5)))
    density = jnp.exp(-0.5 * u * u) * 0.3989422804014327
    a = (u * phi).astype(BF16)
    du = (da * (phi + u * density)).astype(BF16)
    a_ref[...] = a
    du_ref[...] = du
    gw2_ref[...] = mm(a, dy, 0, 0).astype(BF16)
    gw1_ref[...] = mm(z, du, 0, 0).astype(BF16)


def expert_grads(arrived, w1, w2):
    rows = arrived.shape[0]
    width, hidden = w1.shape
    block = 512
    return pl.pallas_call(
        expert_kernel,
        grid=(hidden // block,),
        in_specs=[
            pl.BlockSpec((rows, 2 * width), lambda f: (0, 0)),
            pl.BlockSpec((width, block), lambda f: (0, f)),
            pl.BlockSpec((block, width), lambda f: (f, 0)),
        ],
        out_specs=[
            pl.BlockSpec((rows, block), lambda f: (0, f)),
            pl.BlockSpec((rows, block), lambda f: (0, f)),
            pl.BlockSpec((width, block), lambda f: (0, f)),
            pl.BlockSpec((block, width), lambda f: (f, 0)),
        ],
        out_shape=(
            jax.ShapeDtypeStruct((rows, hidden), BF16),
            jax.ShapeDtypeStruct((rows, hidden), BF16),
            jax.ShapeDtypeStruct((width, hidden), BF16),
            jax.ShapeDtypeStruct((hidden, width), BF16),
        ),
        compiler_params=pltpu.CompilerParams(vmem_limit_bytes=48 * MIB),
        cost_estimate=pl.CostEstimate(
            flops=8 * rows * width * hidden, bytes_accessed=24 * MIB, transcendentals=2 * rows * hidden
        ),
        name="expert_grads",
    )(arrived, w1, w2)


def expert_out_kernel(a_ref, du_ref, w1_ref, w2_ref, back_ref, total_ref):
    width = w1_ref.shape[0]
    step = pl.program_id(0)

    @pl.when(step == 0)
    def _():
        total_ref[...] = jnp.zeros_like(total_ref)

    total_ref[:, :width] += mm(a_ref[...], w2_ref[...])
    total_ref[:, width:] += mm(du_ref[...], w1_ref[...], 1, 1)

    @pl.when(step == pl.num_programs(0) - 1)
    def _():
        back_ref[...] = total_ref[...].astype(BF16)


def expert_rows(a, du, w1, w2):
    rows, hidden = a.shape
    width = w1.shape[0]
    block = 768
    return pl.pallas_call(
        expert_out_kernel,
        grid=(hidden // block,),
        in_specs=[
            pl.BlockSpec((rows, block), lambda f: (0, f)),
            pl.BlockSpec((rows, block), lambda f: (0, f)),
            pl.BlockSpec((width, block), lambda f: (0, f)),
            pl.BlockSpec((block, width), lambda f: (f, 0)),
        ],
        out_specs=pl.BlockSpec((rows, 2 * width), lambda f: (0, 0)),
        out_shape=jax.ShapeDtypeStruct((rows, 2 * width), BF16),
        scratch_shapes=[pltpu.VMEM((rows, 2 * width), F32)],
        compiler_params=pltpu.CompilerParams(vmem_limit_bytes=48 * MIB),
        cost_estimate=pl.CostEstimate(
            flops=4 * rows * width * hidden, bytes_accessed=18 * MIB, transcendentals=0
        ),
        name="expert_rows",
    )(a, du, w1, w2)


def backward_kernel(
    x_ref, g_ref, routes_ref, wq_ref, wp_ref, ws_ref, ln_ref,
    qkv_ref, lse_ref, o_ref, x2_ref, gates_ref, pick0_ref, pick1_ref, ret_ref,
    mixed_ref, dx_ref, gw_ref, gws_ref, dqkv_ref,
):
    rows, width = x_ref.shape
    lane = lane_iota(rows)
    g = g_ref[...].astype(F32)
    x2 = x2_ref[...]
    gates = gates_ref[...]
    routes = routes_ref[...]
    out = x2
    dgates = jnp.zeros((rows, LANES), F32)
    for k, pick_ref in enumerate((pick0_ref, pick1_ref)):
        match = lane == routes[:, k : k + 1]
        picked = mm(pick_ref[...], ret_ref[:, :width])
        chosen = jnp.sum(jnp.where(match, gates, 0.0), -1, keepdims=True)
        out = out + chosen * picked
        dgates = jnp.where(match, jnp.sum(g * picked, -1, keepdims=True), dgates)
    mixed_ref[...] = out.astype(BF16)
    dl = (gates * (dgates - jnp.sum(gates * dgates, -1, keepdims=True))).astype(BF16)
    dh2 = mm(pick0_ref[...] + pick1_ref[...], ret_ref[:, width:]) + mm(dl, ws_ref[...], 1, 1)
    gain1, bias1 = ln_ref[0:1, :], ln_ref[1:2, :]
    gain2, bias2 = ln_ref[2:3, :], ln_ref[3:4, :]
    n2, r2 = normalize(x2)
    h2 = (n2 * gain2 + bias2).astype(BF16)
    g_router = mm(h2, dl, 0, 0)
    g_gain2 = jnp.sum(dh2 * n2, 0, keepdims=True)
    g_bias2 = jnp.sum(dh2, 0, keepdims=True)
    dx2 = g + norm_back(dh2, n2, r2, gain2)
    dx2b = dx2.astype(BF16)
    block = gw_ref.shape[2]
    for core in range(2):
        columns = dx2b[:, core * block : (core + 1) * block]
        gw_ref[core * SIDE + 3] = mm(o_ref[...], columns, 0, 0).astype(BF16)
    do_all = mm(dx2b, wp_ref[...], 1, 1).astype(BF16)
    scale = HEAD_DIM ** (-0.5)
    for pair in range(width // LANES):
        at = pair * LANES
        q = qkv_ref[:, at : at + LANES]
        k = qkv_ref[:, width + at : width + at + LANES]
        v = qkv_ref[:, 2 * width + at : 2 * width + at + LANES]
        do = do_all[:, at : at + LANES]
        parts = []
        for half in range(2):
            own = (lane // HEAD_DIM) == half
            head = 2 * pair + half
            s = mm(jnp.where(own, q, jnp.zeros_like(q)), k, 1, 1) * scale
            p = jnp.exp(s - lse_ref[:, head : head + 1])
            dp = mm(jnp.where(own, do, jnp.zeros_like(do)), v, 1, 1)
            ds = (p * (dp - jnp.sum(dp * p, -1, keepdims=True))).astype(BF16)
            parts.append((mm(ds, k) * scale, mm(ds, q, 0, 0) * scale, mm(p.astype(BF16), do, 0, 0)))
        low = lane < HEAD_DIM
        for third, (first, second) in enumerate(zip(*parts)):
            start = third * width + at
            dqkv_ref[:, start : start + LANES] = jnp.where(low, first, second).astype(BF16)
    n1, r1 = normalize(x_ref[...].astype(F32))
    h1 = (n1 * gain1 + bias1).astype(BF16)
    for number in range(6):
        columns = dqkv_ref[:, number * block : (number + 1) * block]
        gw_ref[number // 3 * SIDE + number % 3] = mm(h1, columns, 0, 0).astype(BF16)
    dh1 = mm(dqkv_ref[...], wq_ref[...], 1, 1)
    g_gain1 = jnp.sum(dh1 * n1, 0, keepdims=True)
    g_bias1 = jnp.sum(dh1, 0, keepdims=True)
    dx_ref[...] = dx2 + norm_back(dh1, n1, r1, gain1)
    row = lax.broadcasted_iota(jnp.int32, (LANES, width), 0)
    vectors = jnp.zeros((LANES, width), F32)
    for place, vector in enumerate((g_gain1, g_bias1, g_gain2, g_bias2)):
        vectors = jnp.where(row == 32 + place, vector, vectors)
    gws_ref[...] = (g_router + vectors.T).astype(BF16)


def backward(tokens, cotangent, routes, wq, wp, ws, ln, kept, returned):
    rows, width = tokens.shape
    return pl.pallas_call(
        backward_kernel,
        out_shape=(
            jax.ShapeDtypeStruct((rows, width), BF16),
            jax.ShapeDtypeStruct((rows, width), F32),
            jax.ShapeDtypeStruct((2 * SIDE, width, width // 2), BF16),
            jax.ShapeDtypeStruct((width, LANES), BF16),
        ),
        scratch_shapes=[pltpu.VMEM((rows, 3 * width), BF16)],
        compiler_params=pltpu.CompilerParams(vmem_limit_bytes=48 * MIB),
        cost_estimate=pl.CostEstimate(
            flops=2 * rows * width * 14 * width, bytes_accessed=24 * MIB, transcendentals=rows * rows * 12
        ),
        name="attention_backward",
    )(tokens, cotangent, routes, wq, wp, ws, ln, *kept, returned)


def on_device(
    tokens, ln1_gain, ln1_bias, w_qkv, w_proj, ln2_gain, ln2_bias, w_router,
    expert_in, expert_out, routes, cotangent,
):
    rows, width = tokens.shape
    experts = w_router.shape[1]
    capacity = (5 * rows // 2 + 8 * experts - 1) // (8 * experts) * 8
    shard = w_qkv.shape[0]
    vectors = jnp.stack([ln1_gain, ln1_bias, ln2_gain, ln2_bias], 1)
    small = jnp.concatenate(
        [w_router, vectors, jnp.zeros((shard, LANES - experts - 4), BF16)], 1
    )
    wq, wp, ws, ln, *kept, arrived = forward(
        tokens, cotangent, routes, w_qkv, w_proj, small, experts, capacity
    )
    w1, w2 = expert_in[0], expert_out[0]
    active, d_hidden, g_first, g_second = expert_grads(arrived, w1, w2)
    g_first = lax.psum_scatter(g_first, "wshard", scatter_dimension=0, tiled=True)
    g_second = lax.psum_scatter(g_second, "wshard", scatter_dimension=0, tiled=True)
    back = expert_rows(active, d_hidden, w1, w2)
    returned = exchange(back, capacity, 2)
    mixed, grad_tokens, gw, gws = backward(
        tokens, cotangent, routes, wq, wp, ws, ln, kept, returned
    )
    gw, gws = reduce_all(gw, gws, 3)
    return (
        mixed,
        grad_tokens,
        gws[:, experts],
        gws[:, experts + 1],
        jnp.concatenate([gw[0], gw[1], gw[2], gw[4], gw[5], gw[6]], 1),
        jnp.concatenate([gw[3], gw[7]], 1),
        gws[:, experts + 2],
        gws[:, experts + 3],
        gws[:, :experts],
        g_first.astype(F32)[None],
        g_second.astype(F32)[None],
    )


def solution(mesh):
    in_specs = (
        P(("expert", "wshard"), None),
        P("wshard"),
        P("wshard"),
        P("wshard", None),
        P("wshard", None),
        P("wshard"),
        P("wshard"),
        P("wshard", None),
        P("expert", None, None),
        P("expert", None, None),
        P(("expert", "wshard"), None),
        P(("expert", "wshard"), None),
    )
    out_specs = (
        P(("expert", "wshard"), None),
        P(("expert", "wshard"), None),
        P("wshard"),
        P("wshard"),
        P("wshard", None),
        P("wshard", None),
        P("wshard"),
        P("wshard"),
        P("wshard", None),
        P("expert", "wshard", None),
        P("expert", "wshard", None),
    )
    return jax.shard_map(
        on_device, mesh=mesh, in_specs=in_specs, out_specs=out_specs, check_vma=False
    )
```

time: 584 us -> 215 us (0.37); the launches traced: 575 us -> 214 us
  Pallas kernels: 0 us -> 169 us
  waiting for transfers between devices: 157 us -> 0.71 us
  blocking collectives: 150 us -> 0 us
  matrix products: 89.8 us -> 0 us
  local copies, waits for them, and re-layouts: 94.8 us -> 23.2 us
  starting transfers between devices: 32.2 us -> 0.08 us
  other arithmetic: 33.9 us -> 6.64 us
    pallas_call x0 -> x6, Pallas kernels: none -> 169 us  [the longest x1 58.9 us: forward(): pl.pallas_call(functools.partial(forward_kernel, experts, capacity), out_...]
    psum x1 -> x0, blocking collectives: 124 us -> none  [on_device(): lax.psum(grad_gain_one.astype(jnp.bfloat16), 'expert').astype(jnp.float32)]
    reduce_scatter x4 -> x2, waiting for transfers between devices: 122 us -> 0.01 us  [the longest x1 0.01 us: on_device(): lax.psum_scatter(g_second, 'wshard', scatter_dimension=0, tiled=True)]
    dot_general x21 -> x0, matrix products: 89.8 us -> none  [the longest x1 18.6 us: on_device(): jnp.einsum('rlf,rld->lfd', active, grad_arrived, preferred_element_type=j...]
    scatter x4 -> x0, local copies, waits for them, and re-layouts: 50.7 us -> none  [the longest x2 25.3 us: on_device(): outgoing.at[slot_index, route_flat].set(jnp.repeat(second_in, 2, axis=0))]
    all_gather x2 -> x0, waiting for transfers between devices: 33 us -> none  [the longest x1 19 us: on_device(): lax.all_gather(w_proj, 'wshard', axis=0, tiled=True)]
    all_to_all x4 -> x0, starting transfers between devices: 31.4 us -> none  [the longest x1 8.94 us: on_device(): lax.all_to_all(outgoing, 'expert', split_axis=1, concat_axis=0, tiled=True)]
    convert_element_type x20 -> x0, other arithmetic: 18.4 us -> none  [the longest x7 7.21 us: on_device(): owned = (lax.psum_scatter(summed[0].astype(jnp.bfloat16), 'wshard', scatt...]
  transfers between devices with their start and end apart: 12 -> 2, of which waited for: 6 -> 0; matrix products, arithmetic and copies ran while one was open for 28% -> 5% of each run, Pallas kernels for 0% -> 44%
where the time goes in v1:
time: 215 us; the launch traced here: 214 us
  Pallas kernels  169 us (79%)
  local copies, waits for them, and re-layouts  23.2 us (11%)
  between operations  14.4 us (7%)
  other arithmetic  6.64 us (3%)
    pallas_call x1, Pallas kernels, forward(): pl.pallas_call(functools.partial(forward_kernel, experts, capacity), out_...  58.9 us
    pallas_call x1, Pallas kernels, reduce_all(): pl.pallas_call(reduce_kernel, out_shape=(jax.ShapeDtypeStruct((2 * SIDE,...  47 us
    pallas_call x1, Pallas kernels, exchange(): pl.pallas_call(functools.partial(exchange_kernel, capacity), out_shape=ja...  24.3 us
    unnamed x60, local copies, waits for them, and re-layouts  18.3 us
    pallas_call x1, Pallas kernels, backward(): pl.pallas_call(backward_kernel, out_shape=(jax.ShapeDtypeStruct((rows, wi...  14.9 us
    pallas_call x1, Pallas kernels, expert_grads(): pl.pallas_call(expert_kernel, grid=(hidden // block,), in_specs=[pl.Block...  14.9 us
    pallas_call x1, Pallas kernels, expert_rows(): pl.pallas_call(expert_out_kernel, grid=(hidden // block,), in_specs=[pl.B...  8.88 us
  transfers between devices with their start and end apart: 2, of which 0 were waited for; matrix products, arithmetic and copies ran while one was open for 5% of the time, Pallas kernels for 44%

profile of v1, /device:TPU:1, one launch (start us, length us, event | category | flops | bytes accessed | tf_op | source)
XLA Modules:
  0.0 213.8 jit_solution(12281239463195781262)
XLA Ops:
  7.2 0.7 stack.16
  8.0 0.7 stack.17
  8.7 0.7 stack.18
  9.5 0.7 stack.19
  10.2 0.8 copy.27
  11.1 0.8 copy.33.routes_ref
  12.1 1.2 copy-done.1
  13.2 1.0 copy-done.2
  14.2 1.0 copy-done.4
  15.2 1.0 copy-done.6
  16.1 58.9 %attention_forward.1 = (bf16[768,2304]{1,0:T(8,128)(2,1)}, bf16[768,768]{1,0:T(8,128)(2,1)S(1)}, bf16[768,128]{1,0:T(8,128)(2,1)S(1)}, f32[8,768]{1,0:T(8,128)S(...) custom-call(bf16[197,768]{1,0:T(8,128)(2,1)S(1)} %copy-done.2, ...), custom_call_target="tpu_custom_call" | custom-call | flops 1394343936 | bytes 16777216 | tf_op jit(solution)/shard_map/attention_forward/pallas_call | solution.py:501
  75.2 2.6 %copy-done.11 = bf16[512,1536]{1,0:T(8,128)(2,1)S(1)} copy-done((bf16[512,1536]{1,0:T(8,128)(2,1)S(1)}, bf16[512,1536]{1,0:T(8,128)(2,1)}, u32[]{:S(2)}) %copy-start.11) | copy-done | bytes 1572888
  77.7 14.9 %expert_grads.1 = (bf16[512,3072]{1,0:T(8,128)(2,1)S(1)}, bf16[512,3072]{1,0:T(8,128)(2,1)}, bf16[768,3072]{1,0:T(8,128)(2,1)}, bf16[3072,768]{1,0:T(8,128)(2,1)}) custom-call(bf16[512,1536]{1,0:T(8,128)(2,1)S(1)} %copy-done.11, bf16[768,3072]{1,0:T(8,128)(2,1)} %bitcast.28, bf16[3072,768]{1,0:T(8,128)(2,1)} %bitcast.30), custom_call_target="tpu_custom_call" | custom-call | flops 9663676416 | bytes 25165824 | tf_op jit(solution)/shard_map/expert_grads/pallas_call | solution.py:560
  93.4 8.9 %expert_rows.1.source_ref = bf16[512,1536]{1,0:T(8,128)(2,1)S(1)} custom-call(bf16[512,3072]{1,0:T(8,128)(2,1)S(1)} %get-tuple-element.45.a_ref, bf16[512,3072]{1,0:T(8,128)(2,1)} %get-tuple-element.46.du_ref, bf16[768,3072]{1,0:T(8,128)(2,1)} %bitcast.29, bf16[3072,768]{1,0:T(8,128)(2,1)} %bitcast.31), custom_call_target="tpu_custom_call" | custom-call | flops 4831838208 | bytes 18874368 | tf_op jit(solution)/shard_map/expert_rows/pallas_call | solution.py:608
  102.3 1.1 copy-done
  103.5 24.3 %exchange_rows.1.ret_ref = bf16[512,1536]{1,0:T(8,128)(2,1)} custom-call(bf16[512,1536]{1,0:T(8,128)(2,1)} %copy-done), custom_call_target="tpu_custom_call" | custom-call | bytes 4194304 | tf_op jit(solution)/shard_map/exchange_rows/pallas_call | solution.py:187
  127.9 1.1 copy-done.13
  128.9 0.9 copy-done.19
  129.9 0.9 copy-done.21
  130.8 0.9 copy-done.23
  131.6 0.7 copy-done.25
  132.4 14.9 %attention_backward.1 = (bf16[197,768]{1,0:T(8,128)(2,1)}, f32[197,768]{1,0:T(8,128)}, bf16[8,768,384]{2,1,0:T(8,128)(2,1)}, bf16[768,128]{1,0:T(8,128)(2,1)S(1)}) custom-call(bf16[197,768]{1,0:T(8,128)(2,1)S(1)} %copy-done.3, bf16[197,768]{1,0:T(8,128)(2,1)S(1)} %copy-done.5, s32[197,2]{1,0:T(8,128)S(1)} %copy.33.routes_ref, ...), custom_call_target="tpu_custom_call" | custom-call | flops 3253469184 | bytes 25165824 | tf_op jit(solution)/shard_map/attention_backward/pallas_call | solution.py:702
  147.3 47.0 %reduce_all.1 = (f32[8,192,384]{2,1,0:T(8,128)S(1)}, f32[192,128]{1,0:T(8,128)S(1)}) custom-call(bf16[8,768,384]{2,1,0:T(8,128)(2,1)} %get-tuple-element.49.g_ref, bf16[4,192,128]{2,1,0:T(8,128)(2,1)S(1)} %bitcast.27), custom_call_target="tpu_custom_call" | custom-call | bytes 33554432 | tf_op jit(solution)/shard_map/reduce_all/pallas_call | solution.py:361
  195.0 0.9 slice_reduce_fusion
  195.9 0.9 pad_maximum_fusion
  196.8 0.7 bitcast_dynamic-update-slice_fusion.5
  197.5 0.7 bitcast_dynamic-update-slice_fusion.4
  198.3 0.7 bitcast_dynamic-update-slice_fusion.3
  199.0 0.7 bitcast_dynamic-update-slice_fusion.2
  200.5 0.7 bitcast_dynamic-update-slice_fusion
  201.2 2.8 %bitcast_convert_fusion = f32[1,768,768]{2,1,0:T(8,128)} fusion(bf16[768,768]{1,0:T(8,128)(2,1)} %reduce-scatter.5.cloned.1.call-done), kind=kLoop, calls=%fused_computation | loop fusion | flops 589824 | bytes 3538944 | tf_op jit(solution)/shard_map/broadcast_in_dim | solution.py:755
  204.0 2.9 %bitcast_convert_fusion.1 = f32[1,192,3072]{2,1,0:T(8,128)} fusion(bf16[192,3072]{1,0:T(8,128)(2,1)} %reduce-scatter.3.cloned.1.call-done), kind=kLoop, calls=%fused_computation.1 | loop fusion | flops 589824 | bytes 3538944 | tf_op jit(solution)/shard_map/broadcast_in_dim | solution.py:754
  (52 shorter events, 2.5 us)
Async XLA Ops:
  7.2 194.0 %reduce-scatter.5.cloned.1.call-start = ((), (), s32[]{:S(2)}) async-start(), calls=%async_computation.3 | async-start | bytes 5898240 | tf_op jit(solution)/shard_map/reduce_scatter | solution.py:737
  12.1 1.2 copy-start.1
  13.2 1.0 copy-start.2
  14.2 1.0 copy-start.4
  15.2 1.0 copy-start.6
  75.0 17.5 %copy-start.7 = (bf16[768,768]{1,0:T(8,128)(2,1)}, bf16[768,768]{1,0:T(8,128)(2,1)S(1)}, u32[]{:S(2)}) copy-start(bf16[768,768]{1,0:T(8,128)(2,1)S(1)} %get-tuple-element.34.wp_ref) | copy-start | bytes 3538948
  75.1 17.5 %copy-start.9 = (bf16[197,2304]{1,0:T(8,128)(2,1)}, bf16[197,2304]{1,0:T(8,128)(2,1)S(1)}, u32[]{:S(2)}) copy-start(bf16[197,2304]{1,0:T(8,128)(2,1)S(1)} %get-tuple-element.37.qkv_ref) | copy-start | bytes 2723332
  75.1 17.5 %copy-start.12 = (f32[197,768]{1,0:T(8,128)}, f32[197,768]{1,0:T(8,128)S(1)}, u32[]{:S(2)}) copy-start(f32[197,768]{1,0:T(8,128)S(1)} %get-tuple-element.40.x2_ref) | copy-start | bytes 1815556
  75.1 17.5 %copy-start.14 = (bf16[197,512]{1,0:T(8,128)(2,1)}, bf16[197,512]{1,0:T(8,128)(2,1)S(1)}, u32[]{:S(2)}) copy-start(bf16[197,512]{1,0:T(8,128)(2,1)S(1)} %get-tuple-element.42.pick0_ref) | copy-start | bytes 605188
  75.1 17.5 %copy-start.16 = (bf16[197,512]{1,0:T(8,128)(2,1)}, bf16[197,512]{1,0:T(8,128)(2,1)S(1)}, u32[]{:S(2)}) copy-start(bf16[197,512]{1,0:T(8,128)(2,1)S(1)} %get-tuple-element.43.pick1_ref) | copy-start | bytes 605188
  75.1 17.5 %copy-start.18 = (bf16[768,128]{1,0:T(8,128)(2,1)}, bf16[768,128]{1,0:T(8,128)(2,1)S(1)}, u32[]{:S(2)}) copy-start(bf16[768,128]{1,0:T(8,128)(2,1)S(1)} %get-tuple-element.35.ws_ref) | copy-start | bytes 589828
  75.1 17.5 %copy-start.20 = (f32[197,128]{1,0:T(8,128)}, f32[197,128]{1,0:T(8,128)S(1)}, u32[]{:S(2)}) copy-start(f32[197,128]{1,0:T(8,128)S(1)} %get-tuple-element.38.lse_ref) | copy-start | bytes 302596
  75.1 17.5 %copy-start.22 = (f32[197,128]{1,0:T(8,128)}, f32[197,128]{1,0:T(8,128)S(1)}, u32[]{:S(2)}) copy-start(f32[197,128]{1,0:T(8,128)S(1)} %get-tuple-element.41.gates_ref) | copy-start | bytes 302596
  75.1 17.5 %copy-start.24 = (f32[8,768]{1,0:T(8,128)}, f32[8,768]{1,0:T(8,128)S(1)}, u32[]{:S(2)}) copy-start(f32[8,768]{1,0:T(8,128)S(1)} %get-tuple-element.36.ln_ref) | copy-start | bytes 73732
  75.1 2.6 %copy-start.11 = (bf16[512,1536]{1,0:T(8,128)(2,1)S(1)}, bf16[512,1536]{1,0:T(8,128)(2,1)}, u32[]{:S(2)}) copy-start(bf16[512,1536]{1,0:T(8,128)(2,1)} %get-tuple-element.44.arrived_ref) | copy-start | bytes 4718596
  92.7 111.4 %reduce-scatter.3.cloned.1.call-start = ((), (), s32[]{:S(2)}) async-start(), calls=%async_computation.2 | async-start | bytes 5898240 | tf_op jit(solution)/shard_map/reduce_scatter | solution.py:736
  102.3 1.1 copy-start
  103.5 24.3 %copy-start.3 = (bf16[197,768]{1,0:T(8,128)(2,1)S(1)}, bf16[197,768]{1,0:T(8,128)(2,1)}, u32[]{:S(2)}) copy-start(bf16[197,768]{1,0:T(8,128)(2,1)} %x_ref.3) | copy-start | bytes 907780
  103.5 24.3 %copy-start.5 = (bf16[197,768]{1,0:T(8,128)(2,1)S(1)}, bf16[197,768]{1,0:T(8,128)(2,1)}, u32[]{:S(2)}) copy-start(bf16[197,768]{1,0:T(8,128)(2,1)} %g_ref.3) | copy-start | bytes 907780
  103.5 24.3 %copy-start.8 = (bf16[768,768]{1,0:T(8,128)(2,1)S(1)}, bf16[768,768]{1,0:T(8,128)(2,1)}, u32[]{:S(2)}) copy-start(bf16[768,768]{1,0:T(8,128)(2,1)} %copy-done.7) | copy-start | bytes 3538948
  103.5 24.3 %copy-start.10 = (bf16[197,2304]{1,0:T(8,128)(2,1)S(1)}, bf16[197,2304]{1,0:T(8,128)(2,1)}, u32[]{:S(2)}) copy-start(bf16[197,2304]{1,0:T(8,128)(2,1)} %copy-done.9) | copy-start | bytes 2723332
  103.5 24.3 %copy-start.15 = (bf16[197,512]{1,0:T(8,128)(2,1)S(1)}, bf16[197,512]{1,0:T(8,128)(2,1)}, u32[]{:S(2)}) copy-start(bf16[197,512]{1,0:T(8,128)(2,1)} %copy-done.14) | copy-start | bytes 605188
  103.5 24.3 %copy-start.17 = (bf16[197,512]{1,0:T(8,128)(2,1)S(1)}, bf16[197,512]{1,0:T(8,128)(2,1)}, u32[]{:S(2)}) copy-start(bf16[197,512]{1,0:T(8,128)(2,1)} %copy-done.16) | copy-start | bytes 605188
  127.8 1.1 copy-start.13
  128.9 0.9 copy-start.19
  129.9 0.9 copy-start.21
  130.7 0.9 copy-start.23
  131.6 0.7 copy-start.25
Sparse Core Ops, SparseCore 0:
  92.8 49.7 reduce-scatter.4
  145.0 53.4 reduce-scatter.2

commit v2 on v1

v2 whole, which is shorter than its diff:
```python
import functools

import jax
import jax.numpy as jnp
from jax import lax
from jax.experimental import pallas as pl
from jax.experimental.pallas import tpu as pltpu
from jax.sharding import PartitionSpec as P

HEAD_DIM = 64
EPSILON = 1e-06
F32 = jnp.float32
BF16 = jnp.bfloat16
LANES = 128
MIB = 1 << 20


def mm(left, right, left_dim=1, right_dim=0):
    return lax.dot_general(
        left, right, (((left_dim,), (right_dim,)), ((), ())), preferred_element_type=F32
    )


def normalize(values):
    centered = values - jnp.mean(values, -1, keepdims=True)
    inverse = lax.rsqrt(jnp.mean(centered * centered, -1, keepdims=True) + EPSILON)
    return centered * inverse, inverse


def norm_back(upstream, normed, inverse, gain):
    scaled = upstream * gain
    return inverse * (
        scaled
        - jnp.mean(scaled, -1, keepdims=True)
        - normed * jnp.mean(scaled * normed, -1, keepdims=True)
    )


def lane_iota(rows, columns=LANES):
    return lax.broadcasted_iota(jnp.int32, (rows, columns), 1)


MESH = pl.DeviceIdType.MESH
SIDE = 4


def remote(source, target, send, receive, expert, shard):
    return pltpu.make_async_remote_copy(
        src_ref=source, dst_ref=target, send_sem=send, recv_sem=receive,
        device_id=(expert, shard), device_id_type=MESH,
    )


def greet(devices):
    barrier = pltpu.get_barrier_semaphore()
    for expert, shard in devices:
        pl.semaphore_signal(barrier, inc=1, device_id=(expert, shard), device_id_type=MESH)
    pl.semaphore_wait(barrier, len(devices))


class RowGather:
    def __init__(self, shard_ref, full_ref, send, receive, expert, shard):
        self.rows, columns = shard_ref.shape
        self.shard_ref, self.full_ref = shard_ref, full_ref
        self.send, self.receive = send, receive
        self.expert, self.shard = expert, shard
        core = lax.rem(expert, 2)
        self.sibling = expert + 1 - 2 * core
        self.after, self.before = lax.rem(shard + 1, SIDE), lax.rem(shard + 3, SIDE)
        self.across = lax.rem(shard + 2, SIDE)
        half = columns // 2
        self.columns = pl.ds(pl.multiple_of(core * half, LANES), half)

    def at(self, shard, start, count, columns):
        place = pl.multiple_of(shard * self.rows + start, 16)
        return self.full_ref.at[pl.ds(place, count), columns]

    def ring(self, number, source, target, shard):
        return remote(
            source, target, self.send.at[number], self.receive.at[number], self.expert, shard
        )

    def first(self):
        target = self.at(self.shard, 0, self.rows, self.columns)
        source = self.shard_ref.at[:, self.columns]
        self.to_after = self.ring(0, source, target, self.after)
        self.to_before = self.ring(1, source, target, self.before)
        self.own = pltpu.make_async_copy(
            self.shard_ref, self.at(self.shard, 0, self.rows, pl.ds(0, self.shard_ref.shape[1])),
            self.send.at[8],
        )
        self.to_after.start()
        self.to_before.start()
        self.own.start()

    def hand(self, number, shard, start, count):
        block = self.at(shard, start, count, self.columns)
        copy = remote(
            block, block, self.send.at[number], self.receive.at[number], self.sibling, self.shard
        )
        copy.start()
        return copy

    def second(self):
        half = self.rows // 2
        self.to_after.wait_recv()
        top = self.at(self.before, 0, half, self.columns)
        self.pass_after = self.ring(2, top, top, self.after)
        self.pass_after.start()
        self.to_before.wait_recv()
        bottom = self.at(self.after, half, half, self.columns)
        self.pass_before = self.ring(3, bottom, bottom, self.before)
        self.pass_before.start()
        self.handed = [
            self.hand(4, self.before, 0, self.rows),
            self.hand(5, self.after, 0, self.rows),
        ]

    def third(self):
        half = self.rows // 2
        self.pass_after.wait_recv()
        self.handed.append(self.hand(6, self.across, 0, half))
        self.pass_before.wait_recv()
        self.handed.append(self.hand(7, self.across, half, half))

    def finish(self):
        self.own.wait()
        for copy in self.handed:
            copy.wait_recv()

    def drain(self):
        for copy in (self.to_after, self.to_before, self.pass_after, self.pass_before, *self.handed):
            copy.wait_send()


def exchange_peers(expert):
    return [
        lax.rem(expert // 8 + dz, SIDE) * 8 + lax.rem(lax.rem(expert // 2, SIDE) + dx, SIDE) * 2
        + lax.rem(expert + dc, 2)
        for dz, dx, dc in exchange_order()
    ]


def exchange_order():
    reach = [0, 1, 2, 1]
    steps = [(dz, dx, dc) for dz in range(SIDE) for dx in range(SIDE) for dc in range(2)]
    return sorted(steps[1:], key=lambda step: -reach[step[0]] - reach[step[1]])


def exchange_start(source_ref, target_ref, send, receive, local, expert, shard, capacity):
    own = pl.ds(pl.multiple_of(expert * capacity, 16), capacity)
    copies = []
    for number, peer in enumerate(exchange_peers(expert)):
        block = pl.ds(pl.multiple_of(peer * capacity, 16), capacity)
        copy = remote(
            source_ref.at[block, :], target_ref.at[own, :], send.at[number], receive.at[number], peer, shard
        )
        copy.start()
        copies.append(copy)
    keep = pltpu.make_async_copy(source_ref.at[own, :], target_ref.at[own, :], local)
    keep.start()
    return copies, keep


def exchange_wait(copies, keep):
    keep.wait()
    for copy in copies:
        copy.wait()


def forward_kernel(
    experts, capacity, x_in, g_in, routes_ref, wq_shard, wp_shard, router_ref, gain1_ref, bias1_ref, gain2_ref, bias2_ref,
    routes_out, wq_out, wp_out, ws_ref, ln_ref, qkv_ref, lse_ref, o_ref, x2_ref, gates_ref, pick0_ref, pick1_ref, arrived_ref,
    x_ref, g_ref, own_ref, small_ref, wq_ref, wp_ref, send_ref, sends, receives, s_send, s_receive, ex_send, ex_receive, local,
):
    rows, width = x_ref.shape
    load_x = pltpu.make_async_copy(x_in, x_ref, local.at[3])
    load_x.start()
    load_g = pltpu.make_async_copy(g_in, g_ref, local.at[4])
    load_g.start()
    expert, shard = lax.axis_index("expert"), lax.axis_index("wshard")
    core = lax.rem(expert, 2)
    pad = jnp.zeros((own_ref.shape[0] - experts - 4, width // SIDE), F32)
    mini = [router_ref[...].astype(F32)] + [
        ref[...].astype(F32).reshape(1, width // SIDE) for ref in (gain1_ref, bias1_ref, gain2_ref, bias2_ref)
    ]
    own_ref[:, : width // SIDE] = jnp.concatenate(mini + [pad], 0).astype(BF16)
    own_ref[:, width // SIDE :] = jnp.zeros((own_ref.shape[0], own_ref.shape[1] - width // SIDE), BF16)
    greet(
        [(expert, lax.rem(shard + by, SIDE)) for by in (1, 2, 3)]
        + [(peer, shard) for peer in exchange_peers(expert)]
    )
    small = []
    for by in (1, 2, 3):
        copy = remote(
            own_ref, small_ref.at[by - 1], s_send.at[by - 1], s_receive.at[by - 1], expert, lax.rem(shard + by, SIDE)
        )
        copy.start()
        small.append(copy)
    first_w, second_w = [
        RowGather(shard_ref, full_ref, sends.at[number], receives.at[number], expert, shard)
        for number, (shard_ref, full_ref) in enumerate(((wq_shard, wq_ref), (wp_shard, wp_ref)))
    ]
    first_w.first()
    load_x.wait()
    x = x_ref[...].astype(F32)
    normed, _ = normalize(x)
    first_w.second()
    second_w.first()
    for copy in small:
        copy.wait_recv()
    pieces = []
    for place in range(SIDE):
        piece = own_ref[...].astype(F32)
        for by in (1, 2, 3):
            piece = jnp.where(lax.rem(shard + SIDE - by, SIDE) == place, small_ref[by - 1].astype(F32), piece)
        pieces.append(piece[:, : width // SIDE])
    lane = lane_iota(rows)
    both = jnp.concatenate(pieces, 1)
    vectors = both[experts : experts + 8, :]
    ln_ref[...] = vectors
    ws_ref[...] = jnp.concatenate([both[:experts], jnp.zeros((LANES - experts, width), F32)], 0).astype(BF16)
    h1 = (normed * vectors[0:1, :] + vectors[1:2, :]).astype(BF16)
    first_w.third()
    second_w.second()
    first_w.finish()
    keep_first = pltpu.make_async_copy(wq_ref, wq_out, local.at[1])
    keep_first.start()
    qkv_ref[...] = mm(h1, wq_ref[...]).astype(BF16)
    scale = HEAD_DIM ** (-0.5)
    lse_all = jnp.zeros((rows, LANES), F32)
    for pair in range(width // LANES):
        if pair == 2:
            second_w.third()
        at = pair * LANES
        q = qkv_ref[:, at : at + LANES]
        k = qkv_ref[:, width + at : width + at + LANES]
        v = qkv_ref[:, 2 * width + at : 2 * width + at + LANES]
        halves = []
        for half in range(2):
            own = (lane // HEAD_DIM) == half
            s = mm(jnp.where(own, q, jnp.zeros_like(q)), k, 1, 1) * scale
            top = jnp.max(s, -1, keepdims=True)
            e = jnp.exp(s - top)
            total = jnp.sum(e, -1, keepdims=True)
            lse_all = jnp.where(lane == 2 * pair + half, top + jnp.log(total), lse_all)
            halves.append(mm((e / total).astype(BF16), v))
        o_ref[:, at : at + LANES] = jnp.where(lane < HEAD_DIM, halves[0], halves[1]).astype(BF16)
    lse_ref[...] = lse_all
    second_w.finish()
    keep_second = pltpu.make_async_copy(wp_ref, wp_out, local.at[2])
    keep_second.start()
    x2 = x + mm(o_ref[...], wp_ref[...])
    x2_ref[...] = x2
    normed2, _ = normalize(x2)
    h2 = (normed2 * vectors[2:3, :] + vectors[3:4, :]).astype(BF16)
    logits = jnp.where(lane < experts, mm(h2, ws_ref[...], 1, 1), -jnp.inf)
    e = jnp.exp(logits - jnp.max(logits, -1, keepdims=True))
    gates = e / jnp.sum(e, -1, keepdims=True)
    gates_ref[...] = gates
    diagonal = lax.broadcasted_iota(jnp.int32, (rows, rows), 0) == lane_iota(rows, rows)
    routes = mm(diagonal.astype(F32).astype(BF16), routes_ref[...].astype(F32).astype(BF16), 1, 1)
    lane_number = lane.astype(F32)
    match = [lane_number == routes[:, k : k + 1] for k in range(2)]
    routes_out[...] = jnp.where(lane == 0, routes[:, 0:1], routes[:, 1:2])
    hits = (match[0] | match[1]).astype(F32).astype(BF16)
    earlier = lax.broadcasted_iota(jnp.int32, (rows, rows), 0) > lane_iota(rows, rows)
    before = mm(earlier.astype(F32).astype(BF16), hits)
    slots = lane_iota(rows, experts * capacity).astype(F32)
    load_g.wait()
    g = g_ref[...].astype(F32)
    picks, grads = [], []
    for k in range(2):
        slot = jnp.sum(jnp.where(match[k], before, 0.0), -1, keepdims=True)
        place = routes[:, k : k + 1] * capacity + slot
        picks.append((slots == place).astype(F32).astype(BF16))
        chosen = jnp.sum(jnp.where(match[k], gates, 0.0), -1, keepdims=True)
        grads.append((chosen * g).astype(BF16))
    pick0_ref[...] = picks[0]
    pick1_ref[...] = picks[1]
    send_ref[:, :width] = mm(picks[0] + picks[1], h2, 0, 0).astype(BF16)
    send_ref[:, width:] = (mm(picks[0], grads[0], 0, 0) + mm(picks[1], grads[1], 0, 0)).astype(BF16)
    copies, keep = exchange_start(
        send_ref, arrived_ref, ex_send, ex_receive, local.at[0], expert, shard, capacity
    )
    for copy in small:
        copy.wait_send()
    for gather in (first_w, second_w):
        gather.drain()
    keep_first.wait()
    keep_second.wait()
    exchange_wait(copies, keep)


def forward(tokens, cotangent, routes, wq, wp, router, vectors, experts, capacity):
    rows, width = tokens.shape
    slots = experts * capacity
    vmem, anywhere = pl.BlockSpec(memory_space=pltpu.VMEM), pl.BlockSpec(memory_space=pl.ANY)
    return pl.pallas_call(
        functools.partial(forward_kernel, experts, capacity),
        out_shape=(
            jax.ShapeDtypeStruct((rows, LANES), F32),
            jax.ShapeDtypeStruct((width, 3 * width), BF16),
            jax.ShapeDtypeStruct((width, width), BF16),
            jax.ShapeDtypeStruct((LANES, width), BF16),
            jax.ShapeDtypeStruct((8, width), F32),
            jax.ShapeDtypeStruct((rows, 3 * width), BF16),
            jax.ShapeDtypeStruct((rows, LANES), F32),
            jax.ShapeDtypeStruct((rows, width), BF16),
            jax.ShapeDtypeStruct((rows, width), F32),
            jax.ShapeDtypeStruct((rows, LANES), F32),
            jax.ShapeDtypeStruct((rows, slots), BF16),
            jax.ShapeDtypeStruct((rows, slots), BF16),
            jax.ShapeDtypeStruct((slots, 2 * width), BF16),
        ),
        in_specs=[anywhere] * 2 + [vmem] + [anywhere] * 2 + [vmem] * 5,
        out_specs=[vmem] + [anywhere] * 2 + [vmem] * 9 + [anywhere],
        scratch_shapes=[
            pltpu.VMEM((rows, width), BF16),
            pltpu.VMEM((rows, width), BF16),
            pltpu.VMEM((48, 256), BF16),
            pltpu.VMEM((3, 48, 256), BF16),
            pltpu.VMEM((width, 3 * width), BF16),
            pltpu.VMEM((width, width), BF16),
            pltpu.VMEM((slots, 2 * width), BF16),
            pltpu.SemaphoreType.DMA((2, 9)),
            pltpu.SemaphoreType.DMA((2, 8)),
            pltpu.SemaphoreType.DMA((3,)),
            pltpu.SemaphoreType.DMA((3,)),
            pltpu.SemaphoreType.DMA((31,)),
            pltpu.SemaphoreType.DMA((31,)),
            pltpu.SemaphoreType.DMA((5,)),
        ],
        compiler_params=pltpu.CompilerParams(
            vmem_limit_bytes=58 * MIB, collective_id=1, has_side_effects=True
        ),
        cost_estimate=pl.CostEstimate(
            flops=2 * rows * width * 6 * width, bytes_accessed=16 * MIB, transcendentals=rows * rows * 12
        ),
        name="attention_forward",
    )(tokens, cotangent, routes, wq, wp, router, *vectors)


def expert_kernel(arrived_ref, w1_ref, w2_ref, a_ref, du_ref, gw1_ref, gw2_ref):
    width = w1_ref.shape[0]
    z = arrived_ref[:, :width]
    dy = arrived_ref[:, width:]
    u = mm(z, w1_ref[...])
    da = mm(dy, w2_ref[...], 1, 1)
    phi = 0.5 * (1.0 + lax.erf(u * (2.0**-0.5)))
    density = jnp.exp(-0.5 * u * u) * 0.3989422804014327
    a = (u * phi).astype(BF16)
    du = (da * (phi + u * density)).astype(BF16)
    a_ref[...] = a
    du_ref[...] = du
    gw2_ref[...] = mm(a, dy, 0, 0).astype(BF16)
    gw1_ref[...] = mm(z, du, 0, 0).astype(BF16)


def expert_grads(arrived, w1, w2):
    rows = arrived.shape[0]
    width, hidden = w1.shape
    block = 512
    return pl.pallas_call(
        expert_kernel,
        grid=(hidden // block,),
        in_specs=[
            pl.BlockSpec((rows, 2 * width), lambda f: (0, 0)),
            pl.BlockSpec((width, block), lambda f: (0, f)),
            pl.BlockSpec((block, width), lambda f: (f, 0)),
        ],
        out_specs=[
            pl.BlockSpec((rows, block), lambda f: (0, f)),
            pl.BlockSpec((rows, block), lambda f: (0, f)),
            pl.BlockSpec((width, block), lambda f: (0, f)),
            pl.BlockSpec((block, width), lambda f: (f, 0)),
        ],
        out_shape=(
            jax.ShapeDtypeStruct((rows, hidden), BF16),
            jax.ShapeDtypeStruct((rows, hidden), BF16),
            jax.ShapeDtypeStruct((width, hidden), BF16),
            jax.ShapeDtypeStruct((hidden, width), BF16),
        ),
        compiler_params=pltpu.CompilerParams(vmem_limit_bytes=58 * MIB),
        cost_estimate=pl.CostEstimate(
            flops=8 * rows * width * hidden, bytes_accessed=24 * MIB, transcendentals=2 * rows * hidden
        ),
        name="expert_grads",
    )(arrived, w1, w2)


def rows_kernel(
    capacity, a_ref, du_ref, w1_ref, w2_ref, gw1_ref, gw2_ref, y_ref, dz_ref, side1_ref, side2_ref,
    a_buf, du_buf, w1_buf, w2_buf, y_buf, dz_buf, total, loads, sends, receives, half_send, half_receive,
):
    expert, shard = lax.axis_index("expert"), lax.axis_index("wshard")
    width, hidden = w1_ref.shape
    block = hidden // SIDE
    after, before, across = [lax.rem(shard + by, SIDE) for by in (1, 3, 2)]
    queue = []
    for number in range(SIDE):
        at = pl.ds(number * block, block)
        for place, (source, target) in enumerate(
            ((a_ref.at[:, at], a_buf.at[:, at]), (w2_ref.at[at, :], w2_buf.at[at, :]))
        ):
            queue.append(pltpu.make_async_copy(source, target, loads.at[place, number]))
    for number in range(SIDE):
        at = pl.ds(number * block, block)
        for place, (source, target) in enumerate(
            ((du_ref.at[:, at], du_buf.at[:, at]), (w1_ref.at[:, at], w1_buf.at[:, at]))
        ):
            queue.append(pltpu.make_async_copy(source, target, loads.at[2 + place, number]))
    for copy in queue:
        copy.start()
    greet([(peer, shard) for peer in exchange_peers(expert)] + [(expert, after), (expert, before)])
    halves = []
    for place, (source, target, rows) in enumerate(
        ((gw1_ref, side1_ref, width // SIDE), (gw2_ref, side2_ref, hidden // SIDE))
    ):
        for number, peer in enumerate((after, before)):
            start = pl.multiple_of(across * rows + number * (rows // 2), 16)
            copy = remote(
                source.at[pl.ds(start, rows // 2), :], target.at[number],
                half_send.at[place, number], half_receive.at[place, number], expert, peer,
            )
            copy.start()
            halves.append(copy)
    moves = []
    for number in range(SIDE):
        queue[2 * number].wait()
        queue[2 * number + 1].wait()
        at = slice(number * block, (number + 1) * block)
        term = mm(a_buf[:, at], w2_buf[at, :])
        total[...] = term if number == 0 else total[...] + term
    y_buf[...] = total[...].astype(BF16)
    moves.append(
        exchange_start(y_buf, y_ref, sends.at[0], receives.at[0], loads.at[4, 0], expert, shard, capacity)
    )
    for number in range(SIDE):
        queue[2 * SIDE + 2 * number].wait()
        queue[2 * SIDE + 2 * number + 1].wait()
        at = slice(number * block, (number + 1) * block)
        term = mm(du_buf[:, at], w1_buf[:, at], 1, 1)
        total[...] = term if number == 0 else total[...] + term
    dz_buf[...] = total[...].astype(BF16)
    moves.append(
        exchange_start(dz_buf, dz_ref, sends.at[1], receives.at[1], loads.at[4, 1], expert, shard, capacity)
    )
    for copies, keep in moves:
        exchange_wait(copies, keep)
    for copy in halves:
        copy.wait()


def expert_rows(a, du, w1, w2, gw1, gw2, capacity, collective_id):
    rows, hidden = a.shape
    width = w1.shape[0]
    vmem, semaphores = pltpu.VMEM, pltpu.SemaphoreType.DMA
    anywhere = pl.BlockSpec(memory_space=pl.ANY)
    return pl.pallas_call(
        functools.partial(rows_kernel, capacity),
        out_shape=(
            jax.ShapeDtypeStruct((rows, width), BF16),
            jax.ShapeDtypeStruct((rows, width), BF16),
            jax.ShapeDtypeStruct((2, width // 8, hidden), BF16),
            jax.ShapeDtypeStruct((2, hidden // 8, width), BF16),
        ),
        in_specs=[anywhere] * 6,
        out_specs=[anywhere] * 4,
        scratch_shapes=[
            vmem((rows, hidden), BF16), vmem((rows, hidden), BF16),
            vmem((width, hidden), BF16), vmem((hidden, width), BF16),
            vmem((rows, width), BF16), vmem((rows, width), BF16), vmem((rows, width), F32),
            semaphores((5, SIDE)), semaphores((2, 31)), semaphores((2, 31)),
            semaphores((2, 2)), semaphores((2, 2)),
        ],
        compiler_params=pltpu.CompilerParams(
            vmem_limit_bytes=58 * MIB, collective_id=collective_id, has_side_effects=True
        ),
        cost_estimate=pl.CostEstimate(
            flops=4 * rows * width * hidden, bytes_accessed=24 * MIB, transcendentals=0
        ),
        name="expert_rows",
    )(a, du, w1, w2, gw1, gw2)


def tail_kernel(
    x_in, g_in, routes_in, wq_in, wp_in, ws_in, ln_in, qkv_in, lse_in, o_in, x2_in, gates_in, pick0_in, pick1_in,
    y_in, dz_in, gw1_in, gw2_in, side1_in, side2_in,
    mixed_ref, dx_ref, gwq_ref, gwp_ref, small_ref, gw1_ref, gw2_ref,
    x_ref, g_ref, routes_ref, wq_ref, wp_ref, ws_ref, ln_ref, qkv_ref, lse_ref, o_ref, x2_ref, gates_ref,
    pick0_ref, pick1_ref, y_ref, dz_ref, side1, side2, part1, part2, came1, came2, do_ref, dqkv_ref, h1_ref,
    theirs, ours, paired, summed, side, first_in, second, second_in, third_in, piece, line, plane, gathered,
    s_ref, s_pair, s_sum, s_in, s_out, s_other,
    loads, send, receive, s_send, s_receive, g_send, g_receive,
):
    expert, shard = lax.axis_index("expert"), lax.axis_index("wshard")
    core = lax.rem(expert, 2)
    x_at, z_at = lax.rem(expert // 2, SIDE), expert // 8
    sibling = expert + 1 - 2 * core
    first, second_at = x_at * (1 - core) + z_at * core, z_at * (1 - core) + x_at * core
    first_step, second_step = 2 + 6 * core, 8 - 6 * core

    def turn(place, by):
        return lax.rem(place + by, SIDE)

    def on_first(by):
        return expert + (turn(first, by) - first) * first_step

    def on_second(by):
        return expert + (turn(second_at, by) - second_at) * second_step

    load_count = [0]

    def load(source, target):
        copy = pltpu.make_async_copy(source, target, loads.at[load_count[0]])
        load_count[0] += 1
        copy.start()
        return copy

    rows1, rows2 = part1.shape[1], part2.shape[1]

    def shard_rows(ref, by, rows):
        return ref.at[pl.ds(pl.multiple_of(turn(shard, by) * rows, 16), rows), :]

    load_first = [load(side1_in, side1)] + [
        load(shard_rows(gw1_in, by, rows1), part1.at[number]) for number, by in enumerate((1, 3))
    ]
    load_out = [
        load(*pair) for pair in (
            (y_in, y_ref), (pick0_in, pick0_ref), (pick1_in, pick1_ref), (x2_in, x2_ref), (g_in, g_ref),
            (gates_in, gates_ref), (routes_in, routes_ref),
        )
    ]
    load_gates = [
        load(*pair) for pair in (
            (dz_in, dz_ref), (ws_in, ws_ref), (ln_in, ln_ref), (wp_in, wp_ref), (o_in, o_ref), (x_in, x_ref),
        )
    ]
    load_heads = [load(qkv_in, qkv_ref), load(lse_in, lse_ref)]
    load_second = [load(side2_in, side2)] + [
        load(shard_rows(gw2_in, by, rows2), part2.at[number]) for number, by in enumerate((1, 3))
    ]
    load_last = [load(wq_in, wq_ref)]
    load_own = [
        load(shard_rows(gw1_in, 0, rows1), part1.at[2]), load(shard_rows(gw2_in, 0, rows2), part2.at[2])
    ]

    greet(
        [(sibling, shard)]
        + [(on_first(by), shard) for by in (1, 2, 3)]
        + [(on_second(by), shard) for by in (1, 2, 3)]
        + [(expert, turn(shard, by)) for by in (1, 2, 3)]
    )
    started = []
    counts = {}

    def go(source, target, to_expert, to_shard, sends=send, receives=receive, kind="wide"):
        number = counts.get(kind, 0)
        counts[kind] = number + 1
        copy = remote(source, target, sends.at[number], receives.at[number], to_expert, to_shard)
        copy.start()
        started.append(copy)
        return copy

    def go_small(*args):
        return go(*args, sends=s_send, receives=s_receive, kind="small")

    def add(left, right):
        return (left.astype(F32) + right.astype(F32)).astype(BF16)

    def join(part, came_half):
        half = part.shape[1] // 2
        part[0, :half] = add(part[0, :half], came_half[0])
        part[1, half:] = add(part[1, half:], came_half[1])

    def pass_on(part, came, start, count):
        at = pl.ds(start, count)
        return [
            go(
                part.at[number, at], came.at[number, at], expert, turn(shard, by), g_send, g_receive, "expert"
            )
            for number, by in enumerate((1, 3))
        ]

    for copy in load_first:
        copy.wait()
    join(part1, side1)
    grads_first = pass_on(part1, came1, 0, rows1)

    for copy in load_out:
        copy.wait()
    rows, width = x_ref.shape
    lane = lane_iota(rows)
    g = g_ref[...].astype(F32)
    x2 = x2_ref[...]
    gates = gates_ref[...]
    routes = routes_ref[...]
    out = x2
    dgates = jnp.zeros((rows, LANES), F32)
    for k, pick_ref in enumerate((pick0_ref, pick1_ref)):
        match = lane.astype(F32) == routes[:, k : k + 1]
        picked = mm(pick_ref[...], y_ref[...])
        chosen = jnp.sum(jnp.where(match, gates, 0.0), -1, keepdims=True)
        out = out + chosen * picked
        dgates = jnp.where(match, jnp.sum(g * picked, -1, keepdims=True), dgates)
    mixed_ref[...] = out.astype(BF16)
    dl = (gates * (dgates - jnp.sum(gates * dgates, -1, keepdims=True))).astype(BF16)
    for copy in load_gates:
        copy.wait()
    dh2 = mm(pick0_ref[...] + pick1_ref[...], dz_ref[...]) + mm(dl, ws_ref[...])
    gain1, bias1 = ln_ref[0:1, :], ln_ref[1:2, :]
    gain2, bias2 = ln_ref[2:3, :], ln_ref[3:4, :]
    n2, r2 = normalize(x2)
    h2 = (n2 * gain2 + bias2).astype(BF16)
    g_router = mm(dl, h2, 0, 0)
    g_gain2 = jnp.sum(dh2 * n2, 0, keepdims=True)
    g_bias2 = jnp.sum(dh2, 0, keepdims=True)
    dx2 = g + norm_back(dh2, n2, r2, gain2)
    dx_ref[...] = dx2
    dx2b = dx2.astype(BF16)
    do_ref[...] = dx2b
    block = width // 2
    mine = pl.ds(pl.multiple_of(core * block, LANES), block)
    others = pl.ds(pl.multiple_of((1 - core) * block, LANES), block)
    theirs[3] = mm(o_ref[...], do_ref[:, others], 0, 0).astype(BF16)
    pair = [None] * SIDE
    pair[3] = go(theirs.at[3], paired.at[3], sibling, shard)
    ours[3] = mm(o_ref[...], do_ref[:, mine], 0, 0).astype(BF16)
    do_ref[...] = mm(dx2b, wp_ref[...], 1, 1).astype(BF16)
    n1, r1 = normalize(x_ref[...].astype(F32))
    h1_ref[...] = (n1 * gain1 + bias1).astype(BF16)
    for copy in load_second:
        copy.wait()
    join(part2, side2)
    grads_second = pass_on(part2, came2, 0, rows2 // 2)
    for copy in load_heads:
        copy.wait()
    scale = HEAD_DIM ** (-0.5)
    low = lane < HEAD_DIM

    def heads(start):
        for step in range(block // LANES):
            at = [
                pl.ds(pl.multiple_of(third * width + start + step * LANES, LANES), LANES) for third in range(3)
            ]
            q, k, v = qkv_ref[:, at[0]], qkv_ref[:, at[1]], qkv_ref[:, at[2]]
            do = do_ref[:, at[0]]
            parts = []
            for half in range(2):
                own = (lane // HEAD_DIM) == half
                head = start // HEAD_DIM + 2 * step + half
                lse = jnp.sum(jnp.where(lane == head, lse_ref[...], 0.0), -1, keepdims=True)
                s = mm(jnp.where(own, q, jnp.zeros_like(q)), k, 1, 1) * scale
                p = jnp.exp(s - lse)
                dp = mm(jnp.where(own, do, jnp.zeros_like(do)), v, 1, 1)
                ds = (p * (dp - jnp.sum(dp * p, -1, keepdims=True))).astype(BF16)
                parts.append((mm(ds, k) * scale, mm(ds, q, 0, 0) * scale, mm(p.astype(BF16), do, 0, 0)))
            for third, (left, right) in enumerate(zip(*parts)):
                dqkv_ref[:, at[third]] = jnp.where(low, left, right).astype(BF16)

    def weight_grads(target, start):
        for third in range(3):
            columns = pl.ds(pl.multiple_of(third * width + start, LANES), block)
            target[third] = mm(h1_ref[...], dqkv_ref[:, columns], 0, 0).astype(BF16)

    heads((1 - core) * block)
    weight_grads(theirs, (1 - core) * block)
    for third in range(3):
        pair[third] = go(theirs.at[third], paired.at[third], sibling, shard)
    heads(core * block)
    weight_grads(ours, core * block)
    for copy in pair:
        copy.wait_recv()

    order = (2, 1, 3, 0)

    def add_pair(number):
        chunk = turn(first, order[number])
        summed[number] = add(ours[chunk], paired[chunk])

    wide = s_ref.shape[1]
    part, quarter, half = wide // 2, wide // 4, 2 * wide
    add_pair(0)
    relay_up = go(summed.at[0, pl.ds(0, half)], side.at[0], on_first(1), shard)
    relay_down = go(summed.at[0, pl.ds(half, half)], side.at[1], on_first(3), shard)
    add_pair(1)
    add_pair(2)

    for copy in load_last:
        copy.wait()
    dh1 = mm(dqkv_ref[...], wq_ref[...], 1, 1)
    g_gain1 = jnp.sum(dh1 * n1, 0, keepdims=True)
    g_bias1 = jnp.sum(dh1, 0, keepdims=True)
    row = lax.broadcasted_iota(jnp.int32, (LANES, width), 0)
    vectors = g_router
    for place, vector in enumerate((g_gain1, g_bias1, g_gain2, g_bias2)):
        vectors = jnp.where(row == 32 + place, vector, vectors)
    s_ref[...] = vectors.T.astype(BF16).reshape(s_ref.shape)
    small_pair = go_small(s_ref, s_pair, sibling, shard)

    relay_up.wait_recv()
    summed[1, :half] = add(summed[1, :half], side[0])
    up = go(summed.at[1], first_in.at[0], on_first(1), shard)
    relay_down.wait_recv()
    summed[2, half:] = add(summed[2, half:], side[1])
    down = go(summed.at[2], first_in.at[1], on_first(3), shard)
    add_pair(3)
    dx_ref[...] += norm_back(dh1, n1, r1, gain1)

    small_pair.wait_recv()
    s_sum[...] = add(s_ref[...], s_pair[...])
    s_mine = pl.ds(pl.multiple_of(core * part, 16), part)
    s_others = pl.ds(pl.multiple_of((1 - core) * part, 16), part)
    small_along = [
        go_small(s_sum.at[turn(shard, by), s_mine, :], s_in.at[by - 1], expert, turn(shard, by)) for by in (1, 2, 3)
    ]
    for copy in small_along:
        copy.wait_recv()

    def four(own, a, b, c):
        return own.astype(F32) + a.astype(F32) + b.astype(F32) + c.astype(F32)

    s_out[0] = four(s_sum[shard, s_mine, :], s_in[0], s_in[1], s_in[2]).astype(BF16)
    small_first = [go_small(s_out.at[0], s_in.at[2 + by], on_first(by), shard) for by in (1, 2, 3)]

    up.wait_recv()
    down.wait_recv()
    for own_shard in range(SIDE):
        for place in range(SIDE):
            at = pl.ds(own_shard * wide + place * quarter, quarter)
            second[place, own_shard] = (
                summed[3, at, :].astype(F32) + first_in[0, at, :].astype(F32) + first_in[1, at, :].astype(F32)
            ).astype(BF16)
    along_second = [
        go(second.at[turn(second_at, by)], second_in.at[by - 1], on_second(by), shard) for by in (2, 1, 3)
    ]
    for copy in small_first:
        copy.wait_recv()
    s_out[1] = four(s_out[0], s_in[3], s_in[4], s_in[5]).astype(BF16)
    small_second = [go_small(s_out.at[1], s_in.at[5 + by], on_second(by), shard) for by in (1, 2, 3)]
    for copy in along_second:
        copy.wait_recv()
    piece[...] = four(second[second_at], second_in[0], second_in[1], second_in[2]).astype(BF16)
    along_shard = [
        go(piece.at[turn(shard, by)], third_in.at[by - 1], expert, turn(shard, by)) for by in (2, 1, 3)
    ]
    grads_second += pass_on(part2, came2, rows2 // 2, rows2 // 2)
    for copy in small_second:
        copy.wait_recv()
    s_out[2] = four(s_out[1], s_in[6], s_in[7], s_in[8]).astype(BF16)
    small_back = go_small(s_out.at[2], s_other, sibling, shard)
    for copy in load_own:
        copy.wait()
    for copy in along_shard:
        copy.wait_recv()
    line[second_at] = four(piece[shard], third_in[0], third_in[1], third_in[2]).astype(BF16)
    back_second = [
        go(line.at[second_at], line.at[second_at], on_second(by), shard) for by in (2, 1, 3)
    ]
    small_back.wait_recv()
    small_ref[s_mine, :] = s_out[2].astype(F32)
    small_ref[s_others, :] = s_other[...].astype(F32)
    for copy in back_second:
        copy.wait_recv()
    plane[first] = line[...].reshape(wide, line.shape[-1])
    back_first = [
        go(plane.at[first], plane.at[first], on_first(by), shard) for by in (2, 1, 3)
    ]
    own_back = go(plane.at[first], gathered.at[first], sibling, shard)
    for copy in grads_first:
        copy.wait_recv()
    gw1_ref[...] = part1[2].astype(F32) + came1[0].astype(F32) + came1[1].astype(F32)
    hands = []
    for copy, by in zip(back_first, (2, 1, 3)):
        copy.wait_recv()
        came = turn(first, SIDE - by)
        hands.append(go(plane.at[came], gathered.at[came], sibling, shard))

    def put(source, start):
        for third in range(3):
            columns = pl.ds(pl.multiple_of(third * width + start, LANES), block)
            gwq_ref[:, columns] = source[third].astype(F32)
        gwp_ref[:, pl.ds(pl.multiple_of(start, LANES), block)] = source[3].astype(F32)

    put(plane, core * block)
    own_back.wait_recv()
    for copy in hands:
        copy.wait_recv()
    put(gathered, (1 - core) * block)
    for copy in grads_second:
        copy.wait_recv()
    gw2_ref[...] = part2[2].astype(F32) + came2[0].astype(F32) + came2[1].astype(F32)
    for copy in started:
        copy.wait_send()


def tail(operands, expert_operands, collective_id):
    tokens, width = operands[0].shape
    columns = width // 2
    rows = width // SIDE
    hidden = expert_operands[0].shape[1]
    quarter, part = rows // 4, rows // 2
    vmem, semaphores = pltpu.VMEM, pltpu.SemaphoreType.DMA
    anywhere = pl.BlockSpec(memory_space=pl.ANY)
    everything = (*operands, *expert_operands)
    return pl.pallas_call(
        tail_kernel,
        out_shape=(
            jax.ShapeDtypeStruct((tokens, width), BF16),
            jax.ShapeDtypeStruct((tokens, width), F32),
            jax.ShapeDtypeStruct((rows, 3 * width), F32),
            jax.ShapeDtypeStruct((rows, width), F32),
            jax.ShapeDtypeStruct((rows, LANES), F32),
            jax.ShapeDtypeStruct((rows, hidden), F32),
            jax.ShapeDtypeStruct((hidden // SIDE, width), F32),
        ),
        in_specs=[anywhere] * len(everything),
        out_specs=[pl.BlockSpec(memory_space=vmem)] * 7,
        scratch_shapes=[vmem(array.shape, array.dtype) for array in operands] + [
            vmem((2, rows // 2, hidden), BF16),
            vmem((2, hidden // 8, width), BF16),
            vmem((3, rows, hidden), BF16),
            vmem((3, hidden // SIDE, width), BF16),
            vmem((2, rows, hidden), BF16),
            vmem((2, hidden // SIDE, width), BF16),
            vmem((tokens, width), BF16),
            vmem((tokens, 3 * width), BF16),
            vmem((tokens, width), BF16),
            vmem((SIDE, width, columns), BF16),
            vmem((SIDE, width, columns), BF16),
            vmem((SIDE, width, columns), BF16),
            vmem((SIDE, width, columns), BF16),
            vmem((2, 2 * rows, columns), BF16),
            vmem((2, width, columns), BF16),
            vmem((SIDE, SIDE, quarter, columns), BF16),
            vmem((3, SIDE, quarter, columns), BF16),
            vmem((3, quarter, columns), BF16),
            vmem((SIDE, quarter, columns), BF16),
            vmem((SIDE, quarter, columns), BF16),
            vmem((SIDE, rows, columns), BF16),
            vmem((SIDE, rows, columns), BF16),
            vmem((SIDE, rows, LANES), BF16),
            vmem((SIDE, rows, LANES), BF16),
            vmem((SIDE, rows, LANES), BF16),
            vmem((9, part, LANES), BF16),
            vmem((3, part, LANES), BF16),
            vmem((part, LANES), BF16),
            semaphores((24,)),
            semaphores((24,)),
            semaphores((24,)),
            semaphores((11,)),
            semaphores((11,)),
            semaphores((6,)),
            semaphores((6,)),
        ],
        compiler_params=pltpu.CompilerParams(
            vmem_limit_bytes=58 * MIB, collective_id=collective_id, has_side_effects=True
        ),
        cost_estimate=pl.CostEstimate(
            flops=2 * tokens * width * 14 * width, bytes_accessed=48 * MIB, transcendentals=tokens * tokens * 12
        ),
        name="backward_and_sums",
    )(*everything)


def on_device(
    tokens, ln1_gain, ln1_bias, w_qkv, w_proj, ln2_gain, ln2_bias, w_router,
    expert_in, expert_out, routes, cotangent,
):
    rows, width = tokens.shape
    experts = w_router.shape[1]
    capacity = (5 * rows // 2 + 8 * experts - 1) // (8 * experts) * 8
    routes, wq, wp, ws, ln, *kept, arrived = forward(
        tokens, cotangent, routes.T, w_qkv, w_proj, w_router.T, (ln1_gain, ln1_bias, ln2_gain, ln2_bias),
        experts, capacity,
    )
    w1, w2 = expert_in[0], expert_out[0]
    active, d_hidden, g_first, g_second = expert_grads(arrived, w1, w2)
    y, dz, side_first, side_second = expert_rows(active, d_hidden, w1, w2, g_first, g_second, capacity, 2)
    mixed, grad_tokens, gwq, gwp, gws, g_first, g_second = tail(
        (tokens, cotangent, routes, wq, wp, ws, ln, *kept, y, dz), (g_first, g_second, side_first, side_second), 3
    )
    return (
        mixed,
        grad_tokens,
        gws[:, experts],
        gws[:, experts + 1],
        gwq,
        gwp,
        gws[:, experts + 2],
        gws[:, experts + 3],
        gws[:, :experts],
        g_first[None],
        g_second[None],
    )


def solution(mesh):
    in_specs = (
        P(("expert", "wshard"), None),
        P("wshard"),
        P("wshard"),
        P("wshard", None),
        P("wshard", None),
        P("wshard"),
        P("wshard"),
        P("wshard", None),
        P("expert", None, None),
        P("expert", None, None),
        P(("expert", "wshard"), None),
        P(("expert", "wshard"), None),
    )
    out_specs = (
        P(("expert", "wshard"), None),
        P(("expert", "wshard"), None),
        P("wshard"),
        P("wshard"),
        P("wshard", None),
        P("wshard", None),
        P("wshard"),
        P("wshard"),
        P("wshard", None),
        P("expert", "wshard", None),
        P("expert", "wshard", None),
    )
    return jax.shard_map(
        on_device, mesh=mesh, in_specs=in_specs, out_specs=out_specs, check_vma=False
    )
```

time: 215 us -> 195 us (0.907)
  between operations: 14.4 us -> 0.69 us
  Pallas kernels: 169 us -> 180 us
  local copies, waits for them, and re-layouts: 23.2 us -> 13.8 us
  other arithmetic: 6.64 us -> 0 us
    pallas_call x4 -> x2, Pallas kernels: 95 us -> 105 us  [the longest x1 72.3 us: tail(): pl.pallas_call(tail_kernel, out_shape=(jax.ShapeDtypeStruct((tokens, widt...]
    unnamed x60 -> x15, local copies, waits for them, and re-layouts: 18.3 us -> 11.7 us
    broadcast_in_dim x2 -> x0, other arithmetic: 5.78 us -> none  [the longest x1 2.94 us: on_device(): g_first.astype(F32)[None]]
    another operation x4 -> x0, local copies, waits for them, and re-layouts: 2.97 us -> none  [on_device(): vectors = jnp.stack([ln1_gain, ln1_bias, ln2_gain, ln2_bias], 1)]
  transfers between devices with their start and end apart: 2 -> 0, of which waited for: 0 -> 0; matrix products, arithmetic and copies ran while one was open for 5% -> 0% of each run, Pallas kernels for 44% -> 0%
where the time goes in v2:
time: 195 us
  Pallas kernels  180 us (92%)
  local copies, waits for them, and re-layouts  13.8 us (7%)
    pallas_call x1, Pallas kernels, tail(): pl.pallas_call(tail_kernel, out_shape=(jax.ShapeDtypeStruct((tokens, widt...  72.3 us
    pallas_call x1, Pallas kernels, forward(): pl.pallas_call(functools.partial(forward_kernel, experts, capacity), out_...  61 us
    pallas_call x1, Pallas kernels, expert_rows(): pl.pallas_call(functools.partial(rows_kernel, capacity), out_shape=(jax.S...  32.9 us
    pallas_call x1, Pallas kernels, expert_grads(): pl.pallas_call(expert_kernel, grid=(hidden // block,), in_specs=[pl.Block...  14 us
    unnamed x15, local copies, waits for them, and re-layouts  11.7 us

profile of v2, /device:TPU:1, one launch (start us, length us, event | category | flops | bytes accessed | tf_op | source)
XLA Modules:
  0.0 194.7 jit_solution(12273389312810831271)
XLA Ops:
  0.6 61.0 %attention_forward.1 = (f32[197,128]{1,0:T(8,128)}, bf16[768,2304]{1,0:T(8,128)(2,1)}, bf16[768,768]{1,0:T(8,128)(2,1)}, bf16[128,768]{1,0:T(8,128)(2,1)}, f32[8...) custom-call(bf16[197,768]{1,0:T(8,128)(2,1)} %x_in.3, ...), custom_call_target="tpu_custom_call" | custom-call | flops 1394343936 | bytes 16777216 | tf_op jit(solution)/shard_map/attention_forward/pallas_call | solution.py:299
  61.7 14.0 %expert_grads.1 = (bf16[512,3072]{1,0:T(8,128)(2,1)}, bf16[512,3072]{1,0:T(8,128)(2,1)}, bf16[768,3072]{1,0:T(8,128)(2,1)}, bf16[3072,768]{1,0:T(8,128)(2,1)}) custom-call(bf16[512,1536]{1,0:T(8,128)(2,1)} %get-tuple-element.51.arrived_ref, bf16[768,3072]{1,0:T(8,128)(2,1)} %bitcast.7, bf16[3072,768]{1,0:T(8,128)(2,1)} %bitcast.9), custom_call_target="tpu_custom_call" | custom-call | flops 9663676416 | bytes 25165824 | tf_op jit(solution)/shard_map/expert_grads/pallas_call | solution.py:364
  75.7 32.9 %expert_rows.1 = (bf16[512,768]{1,0:T(8,128)(2,1)}, bf16[512,768]{1,0:T(8,128)(2,1)}, bf16[2,96,3072]{2,1,0:T(8,128)(2,1)}, bf16[2,384,768]{2,1,0:T(8,128)(2,1)}) custom-call(bf16[512,3072]{1,0:T(8,128)(2,1)} %get-tuple-element.52.a_ref, bf16[512,3072]{1,0:T(8,128)(2,1)} %get-tuple-element.53.du_ref, bf16[768,3072]{1,0:T(8,128)(2,1)} %bitcast.8, ...), custom_call_target="tpu_custom_call" | custom-call | flops 4831838208 | bytes 25165824 | tf_op jit(solution)/shard_map/expert_rows/pallas_call | solution.py:460
  108.6 72.3 %backward_and_sums.1 = (bf16[197,768]{1,0:T(8,128)(2,1)}, f32[197,768]{1,0:T(8,128)}, f32[192,2304]{1,0:T(8,128)}, f32[192,768]{1,0:T(8,128)}, f32[192,128]{1,0:...) custom-call(bf16[197,768]{1,0:T(8,128)(2,1)} %x_in.3, bf16[197,768]{1,0:T(8,128)(2,1)} %g_in.3, ...), custom_call_target="tpu_custom_call" | custom-call | flops 3253469184 | bytes 50331648 | tf_op jit(solution)/shard_map/backward_and_sums/pallas_call | solution.py:807
  180.9 0.0 copy-start.2
  180.9 2.1 %slice_reduce_fusion = (f32[192]{0:T(256)}, f32[192]{0:T(256)}, f32[192]{0:T(256)}, f32[192]{0:T(256)}) fusion(f32[192,128]{1,0:T(8,128)} %get-tuple-element.62), kind=kLoop, calls=%fused_computation | loop fusion | bytes 6144 | tf_op jit(solution)/shard_map/slice | solution.py:892
  183.0 1.6 copy.24
  184.6 1.7 copy.31
  186.3 0.0 copy-start.3
  186.3 2.0 %copy.32 = f32[197,768]{1,0:T(8,128)} copy(f32[197,768]{1,0:T(8,128)} %get-tuple-element.105) | data formatting | bytes 1210368
  188.3 0.0 copy-done.2
  188.3 0.0 copy-start.1
  188.3 1.2 copy.33
  189.5 0.0 copy-done.3
  189.5 0.8 copy.34
  190.3 0.5 copy-done.1
  190.8 0.0 copy-start
  190.8 1.4 copy.35
  192.2 1.1 copy-done
  193.3 1.4 copy.36
Async XLA Ops:
  180.9 7.4 %copy-start.2 = (f32[192,2304]{1,0:T(8,128)S(1)}, f32[192,2304]{1,0:T(8,128)}, u32[]{:S(2)}) copy-start(f32[192,2304]{1,0:T(8,128)} %get-tuple-element.108) | copy-start | bytes 5308420
  186.3 3.2 %copy-start.3 = (f32[192,768]{1,0:T(8,128)S(1)}, f32[192,768]{1,0:T(8,128)}, u32[]{:S(2)}) copy-start(f32[192,768]{1,0:T(8,128)} %get-tuple-element.109) | copy-start | bytes 1769476
  188.3 2.5 %copy-start.1 = (f32[192,3072]{1,0:T(8,128)S(1)}, f32[192,3072]{1,0:T(8,128)}, u32[]{:S(2)}) copy-start(f32[192,3072]{1,0:T(8,128)} %get-tuple-element.65) | copy-start | bytes 7077892
  190.8 2.5 %copy-start = (f32[768,768]{1,0:T(8,128)S(1)}, f32[768,768]{1,0:T(8,128)}, u32[]{:S(2)}) copy-start(f32[768,768]{1,0:T(8,128)} %get-tuple-element.66) | copy-start | bytes 7077892

commit v3 on v2

--- a/solution.py
+++ b/solution.py
@@ -168,10 +168,14 @@
         copy.wait()
 
 
-def forward_kernel(
+def main_kernel(
     experts, capacity, x_in, g_in, routes_ref, wq_shard, wp_shard, router_ref, gain1_ref, bias1_ref, gain2_ref, bias2_ref,
-    routes_out, wq_out, wp_out, ws_ref, ln_ref, qkv_ref, lse_ref, o_ref, x2_ref, gates_ref, pick0_ref, pick1_ref, arrived_ref,
-    x_ref, g_ref, own_ref, small_ref, wq_ref, wp_ref, send_ref, sends, receives, s_send, s_receive, ex_send, ex_receive, local,
+    w1_in, w2_in,
+    routes_out, wq_out, wp_out, ws_ref, ln_ref, qkv_ref, lse_ref, o_ref, x2_ref, gates_ref, pick0_ref, pick1_ref,
+    y_out, dz_out, gw1_out, gw2_out, side1_out, side2_out,
+    x_ref, g_ref, own_ref, small_ref, wq_ref, wp_ref, send_z, send_dy, z_ref, dy_ref,
+    w1_ref, w2_ref, a_ref, slope_ref, gw1_ref, gw2_ref, rows_ref, y_ref, dz_ref,
+    sends, receives, s_send, s_receive, ex_send, ex_receive, half_send, half_receive, local,
 ):
     rows, width = x_ref.shape
     load_x = pltpu.make_async_copy(x_in, x_ref, local.at[3])
@@ -202,6 +206,10 @@
         for number, (shard_ref, full_ref) in enumerate(((wq_shard, wq_ref), (wp_shard, wp_ref)))
     ]
     first_w.first()
+    load_w1 = pltpu.make_async_copy(w1_in, w1_ref, local.at[5])
+    load_w1.start()
+    load_w2 = pltpu.make_async_copy(w2_in, w2_ref, local.at[6])
+    load_w2.start()
     load_x.wait()
     x = x_ref[...].astype(F32)
     normed, _ = normalize(x)
@@ -278,26 +286,113 @@
         grads.append((chosen * g).astype(BF16))
     pick0_ref[...] = picks[0]
     pick1_ref[...] = picks[1]
-    send_ref[:, :width] = mm(picks[0] + picks[1], h2, 0, 0).astype(BF16)
-    send_ref[:, width:] = (mm(picks[0], grads[0], 0, 0) + mm(picks[1], grads[1], 0, 0)).astype(BF16)
-    copies, keep = exchange_start(
-        send_ref, arrived_ref, ex_send, ex_receive, local.at[0], expert, shard, capacity
-    )
+    moves = []
+
+    def move(source, target):
+        number = len(moves)
+        moves.append(
+            exchange_start(
+                source, target, ex_send.at[number], ex_receive.at[number], local.at[7 + number], expert, shard, capacity
+            )
+        )
+        return moves[-1]
+
+    send_z[...] = mm(picks[0] + picks[1], h2, 0, 0).astype(BF16)
+    z_move = move(send_z, z_ref)
+    send_dy[...] = (mm(picks[0], grads[0], 0, 0) + mm(picks[1], grads[1], 0, 0)).astype(BF16)
+    dy_move = move(send_dy, dy_ref)
     for copy in small:
         copy.wait_send()
     for gather in (first_w, second_w):
         gather.drain()
     keep_first.wait()
     keep_second.wait()
-    exchange_wait(copies, keep)
-
-
-def forward(tokens, cotangent, routes, wq, wp, router, vectors, experts, capacity):
+    load_w1.wait()
+    load_w2.wait()
+    block = width
+    blocks = w1_ref.shape[1] // block
+    exchange_wait(*z_move)
+
+    def columns(number):
+        return pl.ds(pl.multiple_of(number * block, block), block)
+
+    rows_ref[...] = jnp.zeros_like(rows_ref)
+
+    def activate(number, _):
+        at = columns(number)
+        u = mm(z_ref[...], w1_ref[:, at])
+        phi = 0.5 * (1.0 + lax.erf(u * (2.0**-0.5)))
+        density = jnp.exp(-0.5 * u * u) * 0.3989422804014327
+        slope_ref[:, at] = phi + u * density
+        a = (u * phi).astype(BF16)
+        a_ref[:, at] = a
+        rows_ref[...] += mm(a, w2_ref[at, :])
+        return 0
+
+    lax.fori_loop(0, blocks, activate, 0)
+    y_ref[...] = rows_ref[...].astype(BF16)
+    move(y_ref, y_out)
+    exchange_wait(*dy_move)
+
+    after, before, across = [lax.rem(shard + by, SIDE) for by in (1, 3, 2)]
+    halves = []
+
+    def pass_halves(place, source, target):
+        rows_each = source.shape[0] // SIDE
+        for number, peer in enumerate((after, before)):
+            start = pl.multiple_of(across * rows_each + number * (rows_each // 2), 16)
+            copy = remote(
+                source.at[pl.ds(start, rows_each // 2), :], target.at[number],
+                half_send.at[place, number], half_receive.at[place, number], expert, peer,
+            )
+            copy.start()
+            halves.append(copy)
+
+    def out_grads(number):
+        at = columns(number)
+        gw2_ref[at, :] = mm(a_ref[:, at], dy_ref[...], 0, 0).astype(BF16)
+
+    out_grads(across)
+    pass_halves(0, gw2_ref, side2_out)
+
+    def other_grads(step, _):
+        out_grads(lax.rem(across + step, SIDE))
+        return 0
+
+    lax.fori_loop(1, blocks, other_grads, 0)
+    keep_gw2 = pltpu.make_async_copy(gw2_ref, gw2_out, local.at[11])
+    keep_gw2.start()
+    rows_ref[...] = jnp.zeros_like(rows_ref)
+
+    def in_grads(number, _):
+        at = columns(number)
+        da = mm(dy_ref[...], w2_ref[at, :], 1, 1)
+        du = (da * slope_ref[:, at]).astype(BF16)
+        rows_ref[...] += mm(du, w1_ref[:, at], 1, 1)
+        gw1_ref[:, at] = mm(z_ref[...], du, 0, 0).astype(BF16)
+        return 0
+
+    lax.fori_loop(0, blocks, in_grads, 0)
+    dz_ref[...] = rows_ref[...].astype(BF16)
+    move(dz_ref, dz_out)
+    pass_halves(1, gw1_ref, side1_out)
+    keep_gw1 = pltpu.make_async_copy(gw1_ref, gw1_out, local.at[12])
+    keep_gw1.start()
+    keep_gw2.wait()
+    keep_gw1.wait()
+    for copies, keep in moves[2:]:
+        exchange_wait(copies, keep)
+    for copy in halves:
+        copy.wait()
+
+
+def forward(tokens, cotangent, routes, wq, wp, router, vectors, w1, w2, experts, capacity):
     rows, width = tokens.shape
+    hidden = w1.shape[1]
     slots = experts * capacity
     vmem, anywhere = pl.BlockSpec(memory_space=pltpu.VMEM), pl.BlockSpec(memory_space=pl.ANY)
     return pl.pallas_call(
-        functools.partial(forward_kernel, experts, capacity),
+        functools.partial(main_kernel, experts, capacity),
         out_shape=(
             jax.ShapeDtypeStruct((rows, LANES), F32),
             jax.ShapeDtypeStruct((width, 3 * width), BF16),
@@ -311,10 +406,15 @@
             jax.ShapeDtypeStruct((rows, LANES), F32),
             jax.ShapeDtypeStruct((rows, slots), BF16),
             jax.ShapeDtypeStruct((rows, slots), BF16),
-            jax.ShapeDtypeStruct((slots, 2 * width), BF16),
+            jax.ShapeDtypeStruct((slots, width), BF16),
+            jax.ShapeDtypeStruct((slots, width), BF16),
+            jax.ShapeDtypeStruct((width, hidden), BF16),
+            jax.ShapeDtypeStruct((hidden, width), BF16),
+            jax.ShapeDtypeStruct((2, width // 8, hidden), BF16),
+            jax.ShapeDtypeStruct((2, hidden // 8, width), BF16),
         ),
-        in_specs=[anywhere] * 2 + [vmem] + [anywhere] * 2 + [vmem] * 5,
-        out_specs=[vmem] + [anywhere] * 2 + [vmem] * 9 + [anywhere],
+        in_specs=[anywhere] * 2 + [vmem] + [anywhere] * 2 + [vmem] * 5 + [anywhere] * 2,
+        out_specs=[vmem] + [anywhere] * 2 + [vmem] * 9 + [anywhere] * 6,
         scratch_shapes=[
             pltpu.VMEM((rows, width), BF16),
             pltpu.VMEM((rows, width), BF16),
@@ -322,166 +422,34 @@
             pltpu.VMEM((3, 48, 256), BF16),
             pltpu.VMEM((width, 3 * width), BF16),
             pltpu.VMEM((width, width), BF16),
-            pltpu.VMEM((slots, 2 * width), BF16),
+            *[pltpu.VMEM((slots, width), BF16)] * 4,
+            pltpu.VMEM((width, hidden), BF16),
+            pltpu.VMEM((hidden, width), BF16),
+            pltpu.VMEM((slots, hidden), BF16),
+            pltpu.VMEM((slots, hidden), F32),
+            pltpu.VMEM((width, hidden), BF16),
+            pltpu.VMEM((hidden, width), BF16),
+            pltpu.VMEM((slots, width), F32),
+            pltpu.VMEM((slots, width), BF16),
+            pltpu.VMEM((slots, width), BF16),
             pltpu.SemaphoreType.DMA((2, 9)),
             pltpu.SemaphoreType.DMA((2, 8)),
             pltpu.SemaphoreType.DMA((3,)),
             pltpu.SemaphoreType.DMA((3,)),
-            pltpu.SemaphoreType.DMA((31,)),
-            pltpu.SemaphoreType.DMA((31,)),
-            pltpu.SemaphoreType.DMA((5,)),
+            pltpu.SemaphoreType.DMA((4, 31)),
+            pltpu.SemaphoreType.DMA((4, 31)),
+            pltpu.SemaphoreType.DMA((2, 2)),
+            pltpu.SemaphoreType.DMA((2, 2)),
+            pltpu.SemaphoreType.DMA((13,)),
         ],
         compiler_params=pltpu.CompilerParams(
             vmem_limit_bytes=58 * MIB, collective_id=1, has_side_effects=True
         ),
         cost_estimate=pl.CostEstimate(
-            flops=2 * rows * width * 6 * width, bytes_accessed=16 * MIB, transcendentals=rows * rows * 12
+            flops=12 * slots * width * hidden, bytes_accessed=48 * MIB, transcendentals=2 * slots * hidden
         ),
-        name="attention_forward",
-    )(tokens, cotangent, routes, wq, wp, router, *vectors)
-
-
-def expert_kernel(arrived_ref, w1_ref, w2_ref, a_ref, du_ref, gw1_ref, gw2_ref):
-    width = w1_ref.shape[0]
-    z = arrived_ref[:, :width]
-    dy = arrived_ref[:, width:]
-    u = mm(z, w1_ref[...])
-    da = mm(dy, w2_ref[...], 1, 1)
-    phi = 0.5 * (1.0 + lax.erf(u * (2.0**-0.5)))
-    density = jnp.exp(-0.5 * u * u) * 0.3989422804014327
-    a = (u * phi).astype(BF16)
-    du = (da * (phi + u * density)).astype(BF16)
-    a_ref[...] = a
-    du_ref[...] = du
-    gw2_ref[...] = mm(a, dy, 0, 0).astype(BF16)
-    gw1_ref[...] = mm(z, du, 0, 0).astype(BF16)
-
-
-def expert_grads(arrived, w1, w2):
-    rows = arrived.shape[0]
-    width, hidden = w1.shape
-    block = 512
-    return pl.pallas_call(
-        expert_kernel,
-        grid=(hidden // block,),
-        in_specs=[
-            pl.BlockSpec((rows, 2 * width), lambda f: (0, 0)),
-            pl.BlockSpec((width, block), lambda f: (0, f)),
-            pl.BlockSpec((block, width), lambda f: (f, 0)),
-        ],
-        out_specs=[
-            pl.BlockSpec((rows, block), lambda f: (0, f)),
-            pl.BlockSpec((rows, block), lambda f: (0, f)),
-            pl.BlockSpec((width, block), lambda f: (0, f)),
-            pl.BlockSpec((block, width), lambda f: (f, 0)),
-        ],
-        out_shape=(
-            jax.ShapeDtypeStruct((rows, hidden), BF16),
-            jax.ShapeDtypeStruct((rows, hidden), BF16),
-            jax.ShapeDtypeStruct((width, hidden), BF16),
-            jax.ShapeDtypeStruct((hidden, width), BF16),
-        ),
-        compiler_params=pltpu.CompilerParams(vmem_limit_bytes=58 * MIB),
-        cost_estimate=pl.CostEstimate(
-            flops=8 * rows * width * hidden, bytes_accessed=24 * MIB, transcendentals=2 * rows * hidden
-        ),
-        name="expert_grads",
-    )(arrived, w1, w2)
-
-
-def rows_kernel(
-    capacity, a_ref, du_ref, w1_ref, w2_ref, gw1_ref, gw2_ref, y_ref, dz_ref, side1_ref, side2_ref,
-    a_buf, du_buf, w1_buf, w2_buf, y_buf, dz_buf, total, loads, sends, receives, half_send, half_receive,
-):
-    expert, shard = lax.axis_index("expert"), lax.axis_index("wshard")
-    width, hidden = w1_ref.shape
-    block = hidden // SIDE
-    after, before, across = [lax.rem(shard + by, SIDE) for by in (1, 3, 2)]
-    queue = []
-    for number in range(SIDE):
-        at = pl.ds(number * block, block)
-        for place, (source, target) in enumerate(
-            ((a_ref.at[:, at], a_buf.at[:, at]), (w2_ref.at[at, :], w2_buf.at[at, :]))
-        ):
-            queue.append(pltpu.make_async_copy(source, target, loads.at[place, number]))
-    for number in range(SIDE):
-        at = pl.ds(number * block, block)
-        for place, (source, target) in enumerate(
-            ((du_ref.at[:, at], du_buf.at[:, at]), (w1_ref.at[:, at], w1_buf.at[:, at]))
-        ):
-            queue.append(pltpu.make_async_copy(source, target, loads.at[2 + place, number]))
-    for copy in queue:
-        copy.start()
-    greet([(peer, shard) for peer in exchange_peers(expert)] + [(expert, after), (expert, before)])
-    halves = []
-    for place, (source, target, rows) in enumerate(
-        ((gw1_ref, side1_ref, width // SIDE), (gw2_ref, side2_ref, hidden // SIDE))
-    ):
-        for number, peer in enumerate((after, before)):
-            start = pl.multiple_of(across * rows + number * (rows // 2), 16)
-            copy = remote(
-                source.at[pl.ds(start, rows // 2), :], target.at[number],
-                half_send.at[place, number], half_receive.at[place, number], expert, peer,
-            )
-            copy.start()
-            halves.append(copy)
-    moves = []
-    for number in range(SIDE):
-        queue[2 * number].wait()
-        queue[2 * number + 1].wait()
-        at = slice(number * block, (number + 1) * block)
-        term = mm(a_buf[:, at], w2_buf[at, :])
-        total[...] = term if number == 0 else total[...] + term
-    y_buf[...] = total[...].astype(BF16)
-    moves.append(
-        exchange_start(y_buf, y_ref, sends.at[0], receives.at[0], loads.at[4, 0], expert, shard, capacity)
-    )
-    for number in range(SIDE):
-        queue[2 * SIDE + 2 * number].wait()
-        queue[2 * SIDE + 2 * number + 1].wait()
-        at = slice(number * block, (number + 1) * block)
-        term = mm(du_buf[:, at], w1_buf[:, at], 1, 1)
-        total[...] = term if number == 0 else total[...] + term
-    dz_buf[...] = total[...].astype(BF16)
-    moves.append(
-        exchange_start(dz_buf, dz_ref, sends.at[1], receives.at[1], loads.at[4, 1], expert, shard, capacity)
-    )
-    for copies, keep in moves:
-        exchange_wait(copies, keep)
-    for copy in halves:
-        copy.wait()
-
-
-def expert_rows(a, du, w1, w2, gw1, gw2, capacity, collective_id):
-    rows, hidden = a.shape
-    width = w1.shape[0]
-    vmem, semaphores = pltpu.VMEM, pltpu.SemaphoreType.DMA
-    anywhere = pl.BlockSpec(memory_space=pl.ANY)
-    return pl.pallas_call(
-        functools.partial(rows_kernel, capacity),
-        out_shape=(
-            jax.ShapeDtypeStruct((rows, width), BF16),
-            jax.ShapeDtypeStruct((rows, width), BF16),
-            jax.ShapeDtypeStruct((2, width // 8, hidden), BF16),
-            jax.ShapeDtypeStruct((2, hidden // 8, width), BF16),
-        ),
-        in_specs=[anywhere] * 6,
-        out_specs=[anywhere] * 4,
-        scratch_shapes=[
-            vmem((rows, hidden), BF16), vmem((rows, hidden), BF16),
-            vmem((width, hidden), BF16), vmem((hidden, width), BF16),
-            vmem((rows, width), BF16), vmem((rows, width), BF16), vmem((rows, width), F32),
-            semaphores((5, SIDE)), semaphores((2, 31)), semaphores((2, 31)),
-            semaphores((2, 2)), semaphores((2, 2)),
-        ],
-        compiler_params=pltpu.CompilerParams(
-            vmem_limit_bytes=58 * MIB, collective_id=collective_id, has_side_effects=True
-        ),
-        cost_estimate=pl.CostEstimate(
-            flops=4 * rows * width * hidden, bytes_accessed=24 * MIB, transcendentals=0
-        ),
-        name="expert_rows",
-    )(a, du, w1, w2, gw1, gw2)
+        name="forward_and_experts",
+    )(tokens, cotangent, routes, wq, wp, router, *vectors, w1, w2)
 
 
 def tail_kernel(
@@ -770,7 +738,7 @@
     own_back = go(plane.at[first], gathered.at[first], sibling, shard)
     for copy in grads_first:
         copy.wait_recv()
-    gw1_ref[...] = part1[2].astype(F32) + came1[0].astype(F32) + came1[1].astype(F32)
+    gw1_ref[...] = (part1[2].astype(F32) + came1[0].astype(F32) + came1[1].astype(F32)).astype(BF16)
     hands = []
     for copy, by in zip(back_first, (2, 1, 3)):
         copy.wait_recv()
@@ -780,8 +748,8 @@
     def put(source, start):
         for third in range(3):
             columns = pl.ds(pl.multiple_of(third * width + start, LANES), block)
-            gwq_ref[:, columns] = source[third].astype(F32)
-        gwp_ref[:, pl.ds(pl.multiple_of(start, LANES), block)] = source[3].astype(F32)
+            gwq_ref[:, columns] = source[third]
+        gwp_ref[:, pl.ds(pl.multiple_of(start, LANES), block)] = source[3]
 
     put(plane, core * block)
     own_back.wait_recv()
@@ -790,7 +758,7 @@
     put(gathered, (1 - core) * block)
     for copy in grads_second:
         copy.wait_recv()
-    gw2_ref[...] = part2[2].astype(F32) + came2[0].astype(F32) + came2[1].astype(F32)
+    gw2_ref[...] = (part2[2].astype(F32) + came2[0].astype(F32) + came2[1].astype(F32)).astype(BF16)
     for copy in started:
         copy.wait_send()
 
@@ -809,11 +777,11 @@
         out_shape=(
             jax.ShapeDtypeStruct((tokens, width), BF16),
             jax.ShapeDtypeStruct((tokens, width), F32),
-            jax.ShapeDtypeStruct((rows, 3 * width), F32),
-            jax.ShapeDtypeStruct((rows, width), F32),
+            jax.ShapeDtypeStruct((rows, 3 * width), BF16),
+            jax.ShapeDtypeStruct((rows, width), BF16),
             jax.ShapeDtypeStruct((rows, LANES), F32),
-            jax.ShapeDtypeStruct((rows, hidden), F32),
-            jax.ShapeDtypeStruct((hidden // SIDE, width), F32),
+            jax.ShapeDtypeStruct((rows, hidden), BF16),
+            jax.ShapeDtypeStruct((hidden // SIDE, width), BF16),
         ),
         in_specs=[anywhere] * len(everything),
         out_specs=[pl.BlockSpec(memory_space=vmem)] * 7,
@@ -864,36 +832,77 @@
     )(*everything)
 
 
+def widen_kernel(experts, *refs):
+    ins, outs, buffers, wide, loads, stores = refs[:7], refs[7:18], refs[18:25], refs[25:32], refs[32], refs[33]
+    small_in, small_buffer = ins[4], buffers[4]
+    incoming = []
+    for number, (source, target) in enumerate(zip(ins, buffers)):
+        copy = pltpu.make_async_copy(source, target, loads.at[number])
+        copy.start()
+        incoming.append(copy)
+    outgoing = []
+
+    def store(source, target):
+        copy = pltpu.make_async_copy(source, target, stores.at[len(outgoing)])
+        copy.start()
+        outgoing.append(copy)
+
+    places = (0, 1, 4, 5, None, 9, 10)
+    for number in (0, 1, 5, 6, 2, 3):
+        incoming[number].wait()
+        if number < 2:
+            store(buffers[number], outs[places[number]])
+        else:
+            wide[number][...] = buffers[number][...].astype(F32)
+            target = outs[places[number]]
+            store(wide[number], target.at[0] if number > 4 else target)
+    incoming[4].wait()
+    rows = small_buffer.shape[0]
+    padded = jnp.concatenate([small_buffer[...], jnp.zeros((256 - rows, LANES), F32)], 0).T
+    outs[8][...] = padded[:experts, :rows]
+    for place, output in enumerate((2, 3, 6, 7)):
+        outs[output][...] = padded[experts + place : experts + place + 1, :rows].reshape(rows)
+    for copy in outgoing:
+        copy.wait()
+
+
+def widen(mixed, grad_tokens, gwq, gwp, small, gw1, gw2, experts):
+    ins = (mixed, grad_tokens, gwq, gwp, small, gw1, gw2)
+    rows = small.shape[0]
+    anywhere, vmem = pl.BlockSpec(memory_space=pl.ANY), pl.BlockSpec(memory_space=pltpu.VMEM)
+    shapes = [
+        (mixed.shape, BF16), (grad_tokens.shape, F32), ((rows,), F32), ((rows,), F32), (gwq.shape, F32), (gwp.shape, F32),
+        ((rows,), F32), ((rows,), F32), ((experts, rows), F32), ((1, *gw1.shape), F32), ((1, *gw2.shape), F32),
+    ]
+    return pl.pallas_call(
+        functools.partial(widen_kernel, experts),
+        out_shape=[jax.ShapeDtypeStruct(*shape) for shape in shapes],
+        in_specs=[anywhere] * 7,
+        out_specs=[anywhere if place in (0, 1, 4, 5, 9, 10) else vmem for place in range(11)],
+        scratch_shapes=[pltpu.VMEM(array.shape, array.dtype) for array in ins]
+        + [pltpu.VMEM(array.shape, F32) for array in ins]
+        + [pltpu.SemaphoreType.DMA((7,)), pltpu.SemaphoreType.DMA((6,))],
+        compiler_params=pltpu.CompilerParams(vmem_limit_bytes=58 * MIB),
+        cost_estimate=pl.CostEstimate(flops=0, bytes_accessed=13 * MIB, transcendentals=0),
+        name="widen_outputs",
+    )(*ins)
+
+
 def on_device(
     tokens, ln1_gain, ln1_bias, w_qkv, w_proj, ln2_gain, ln2_bias, w_router,
     expert_in, expert_out, routes, cotangent,
 ):
-    rows, width = tokens.shape
+    rows = tokens.shape[0]
     experts = w_router.shape[1]
     capacity = (5 * rows // 2 + 8 * experts - 1) // (8 * experts) * 8
-    routes, wq, wp, ws, ln, *kept, arrived = forward(
+    *kept, g_first, g_second, side_first, side_second = forward(
         tokens, cotangent, routes.T, w_qkv, w_proj, w_router.T, (ln1_gain, ln1_bias, ln2_gain, ln2_bias),
-        experts, capacity,
+        expert_in[0], expert_out[0], experts, capacity,
     )
-    w1, w2 = expert_in[0], expert_out[0]
-    active, d_hidden, g_first, g_second = expert_grads(arrived, w1, w2)
-    y, dz, side_first, side_second = expert_rows(active, d_hidden, w1, w2, g_first, g_second, capacity, 2)
-    mixed, grad_tokens, gwq, gwp, gws, g_first, g_second = tail(
-        (tokens, cotangent, routes, wq, wp, ws, ln, *kept, y, dz), (g_first, g_second, side_first, side_second), 3
-    )
-    return (
-        mixed,
-        grad_tokens,
-        gws[:, experts],
-        gws[:, experts + 1],
-        gwq,
-        gwp,
-        gws[:, experts + 2],
-        gws[:, experts + 3],
-        gws[:, :experts],
-        g_first[None],
-        g_second[None],
-    )
+    sums = tail((tokens, cotangent, *kept), (g_first, g_second, side_first, side_second), 3)
+    outputs = list(widen(*sums, experts))
+    outputs[8] = outputs[8].T
+    return tuple(outputs)
 
 
 def solution(mesh):

time: 195 us -> 170 us (0.87)
  local copies, waits for them, and re-layouts: 13.8 us -> 0 us
  Pallas kernels: 180 us -> 169 us
    unnamed x15 -> x0, local copies, waits for them, and re-layouts: 11.7 us -> none
    pallas_call x3 -> x2, Pallas kernels: 108 us -> 97.4 us  [the longest x1 91.6 us: forward(): pl.pallas_call(functools.partial(main_kernel, experts, capacity), out_sha...]
    slice x1 -> x0, local copies, waits for them, and re-layouts: 2.1 us -> none  [on_device(): gws[:, experts + 3]]
where the time goes in v3:
time: 170 us
  Pallas kernels  169 us (99%)
    pallas_call x1, Pallas kernels, forward(): pl.pallas_call(functools.partial(main_kernel, experts, capacity), out_sha...  91.6 us
    pallas_call x1, Pallas kernels, tail(): pl.pallas_call(tail_kernel, out_shape=(jax.ShapeDtypeStruct((tokens, widt...  71.4 us
    pallas_call x1, Pallas kernels, widen(): pl.pallas_call(functools.partial(widen_kernel, experts), out_shape=[jax.S...  5.84 us

profile of v3, /device:TPU:1, one launch (start us, length us, event | category | flops | bytes accessed | tf_op | source)
XLA Modules:
  0.0 169.7 jit_solution(1709265747029269082)
XLA Ops:
  0.6 91.6 %forward_and_experts.1 = (f32[197,128]{1,0:T(8,128)}, bf16[768,2304]{1,0:T(8,128)(2,1)}, bf16[768,768]{1,0:T(8,128)(2,1)}, bf16[128,768]{1,0:T(8,128)(2,1)}, f32...) custom-call(bf16[197,768]{1,0:T(8,128)(2,1)} %x_in.3, ...), custom_call_target="tpu_custom_call" | custom-call | flops 14495514624 | bytes 50331648 | tf_op jit(solution)/shard_map/forward_and_experts/pallas_call | solution.py:394
  92.2 71.4 %backward_and_sums.1 = (bf16[197,768]{1,0:T(8,128)(2,1)}, f32[197,768]{1,0:T(8,128)}, bf16[192,2304]{1,0:T(8,128)(2,1)}, bf16[192,768]{1,0:T(8,128)(2,1)}, f32[1...) custom-call(bf16[197,768]{1,0:T(8,128)(2,1)} %x_in.3, bf16[197,768]{1,0:T(8,128)(2,1)} %g_in.3, ...), custom_call_target="tpu_custom_call" | custom-call | flops 3253469184 | bytes 50331648 | tf_op jit(solution)/shard_map/backward_and_sums/pallas_call | solution.py:775
  163.7 5.8 %widen_outputs.1 = (bf16[197,768]{1,0:T(8,128)(2,1)}, f32[197,768]{1,0:T(8,128)}, f32[192]{0:T(256)}, f32[192]{0:T(256)}, f32[192,2304]{1,0:T(8,128)}, /*index=5...) custom-call(bf16[197,768]{1,0:T(8,128)(2,1)} %get-tuple-element.65.r, ...), custom_call_target="tpu_custom_call" | custom-call | bytes 13631488 | tf_op jit(solution)/shard_map/widen_outputs/pallas_call | solution.py:877

commit v4 on v3

--- a/solution.py
+++ b/solution.py
@@ -59,8 +59,9 @@
 
 
 class RowGather:
-    def __init__(self, shard_ref, full_ref, send, receive, expert, shard):
-        self.rows, columns = shard_ref.shape
+    def __init__(self, shard_ref, full_ref, columns, send, receive, expert, shard):
+        self.rows = shard_ref.shape[0]
+        self.columns = columns
         self.shard_ref, self.full_ref = shard_ref, full_ref
         self.send, self.receive = send, receive
         self.expert, self.shard = expert, shard
@@ -68,8 +69,6 @@
         self.sibling = expert + 1 - 2 * core
         self.after, self.before = lax.rem(shard + 1, SIDE), lax.rem(shard + 3, SIDE)
         self.across = lax.rem(shard + 2, SIDE)
-        half = columns // 2
-        self.columns = pl.ds(pl.multiple_of(core * half, LANES), half)
 
     def at(self, shard, start, count, columns):
         place = pl.multiple_of(shard * self.rows + start, 16)
@@ -133,6 +132,95 @@
             copy.wait_send()
 
 
+class PlaneGather:
+    def __init__(self, shard_ref, full_ref, columns, stride, send, receive, expert, shard):
+        self.rows = shard_ref.shape[0]
+        self.shard_ref, self.full_ref, self.columns = shard_ref, full_ref, columns
+        self.send, self.receive = send, receive
+        self.expert, self.shard, self.stride = expert, shard, stride
+        self.place = lax.rem(expert // stride, SIDE)
+        self.sibling = expert + 1 - 2 * lax.rem(expert, 2)
+        self.sent = []
+
+    def at(self, shard, start, count):
+        return self.full_ref.at[pl.ds(pl.multiple_of(shard * self.rows + start, 16), count), self.columns]
+
+    def go(self, number, source, target, expert, shard):
+        copy = remote(source, target, self.send.at[number], self.receive.at[number], expert, shard)
+        copy.start()
+        self.sent.append(copy)
+        return copy
+
+    def first(self):
+        quarter = self.rows // SIDE
+        start = pl.multiple_of(self.place * quarter, 16)
+        source = self.shard_ref.at[pl.ds(start, quarter), self.columns]
+        self.pieces = [
+            self.go(
+                by - 1, source, self.at(self.shard, start, quarter), self.expert, lax.rem(self.shard + by, SIDE)
+            )
+            for by in (2, 1, 3)
+        ]
+
+    def second(self):
+        quarter = self.rows // SIDE
+        self.shares = []
+        for copy, by in zip(self.pieces, (2, 1, 3)):
+            copy.wait_recv()
+            piece = self.at(lax.rem(self.shard + SIDE - by, SIDE), self.place * quarter, quarter)
+            for step in (2, 1, 3):
+                peer = self.expert + (lax.rem(self.place + step, SIDE) - self.place) * self.stride
+                self.shares.append(self.go(3 * by + step - 1, piece, piece, peer, self.shard))
+
+    def third(self):
+        for copy in self.shares:
+            copy.wait_recv()
+        self.handed = []
+        for by in (1, 2, 3):
+            block = self.at(lax.rem(self.shard + by, SIDE), 0, self.rows)
+            self.handed.append(self.go(11 + by, block, block, self.sibling, self.shard))
+
+    def finish(self):
+        for copy in self.handed:
+            copy.wait_recv()
+
+    def drain(self):
+        for copy in self.sent:
+            copy.wait_send()
+
+
+class Gather:
+    def __init__(self, shard_ref, full_ref, send, receive, expert, shard):
+        third = shard_ref.shape[1] // 6
+        start = lax.rem(expert, 2) * 3 * third
+        parts = [pl.ds(pl.multiple_of(start + number * third, LANES), third) for number in range(3)]
+        self.parts = [
+            PlaneGather(shard_ref, full_ref, parts[1], 2, send.at[1], receive.at[1], expert, shard),
+            PlaneGather(shard_ref, full_ref, parts[2], 8, send.at[2], receive.at[2], expert, shard),
+            RowGather(shard_ref, full_ref, parts[0], send.at[0], receive.at[0], expert, shard),
+        ]
+
+    def first(self):
+        for part in self.parts:
+            part.first()
+
+    def second(self):
+        for part in self.parts:
+            part.second()
+
+    def third(self):
+        for part in self.parts:
+            part.third()
+
+    def finish(self):
+        for part in self.parts:
+            part.finish()
+
+    def drain(self):
+        for part in self.parts:
+            part.drain()
+
+
 def exchange_peers(expert):
     return [
         lax.rem(expert // 8 + dz, SIDE) * 8 + lax.rem(lax.rem(expert // 2, SIDE) + dx, SIDE) * 2
@@ -173,7 +261,7 @@
     w1_in, w2_in,
     routes_out, wq_out, wp_out, ws_ref, ln_ref, qkv_ref, lse_ref, o_ref, x2_ref, gates_ref, pick0_ref, pick1_ref,
     y_out, dz_out, gw1_out, gw2_out, side1_out, side2_out,
-    x_ref, g_ref, own_ref, small_ref, wq_ref, wp_ref, send_z, send_dy, z_ref, dy_ref,
+    x_ref, g_ref, own_ref, small_ref, wq_ref, wp_ref, send_z, send_dy, z_ref, g_rows_ref, dy_ref,
     w1_ref, w2_ref, a_ref, slope_ref, gw1_ref, gw2_ref, rows_ref, y_ref, dz_ref,
     sends, receives, s_send, s_receive, ex_send, ex_receive, half_send, half_receive, local,
 ):
@@ -202,7 +290,7 @@
         copy.start()
         small.append(copy)
     first_w, second_w = [
-        RowGather(shard_ref, full_ref, sends.at[number], receives.at[number], expert, shard)
+        Gather(shard_ref, full_ref, sends.at[number], receives.at[number], expert, shard)
         for number, (shard_ref, full_ref) in enumerate(((wq_shard, wq_ref), (wp_shard, wp_ref)))
     ]
     first_w.first()
@@ -213,6 +301,33 @@
     load_x.wait()
     x = x_ref[...].astype(F32)
     normed, _ = normalize(x)
+    lane = lane_iota(rows)
+    diagonal = lax.broadcasted_iota(jnp.int32, (rows, rows), 0) == lane_iota(rows, rows)
+    routes = mm(diagonal.astype(F32).astype(BF16), routes_ref[...].astype(F32).astype(BF16), 1, 1)
+    lane_number = lane.astype(F32)
+    match = [lane_number == routes[:, k : k + 1] for k in range(2)]
+    routes_out[...] = jnp.where(lane == 0, routes[:, 0:1], routes[:, 1:2])
+    hits = (match[0] | match[1]).astype(F32).astype(BF16)
+    earlier = lax.broadcasted_iota(jnp.int32, (rows, rows), 0) > lane_iota(rows, rows)
+    before = mm(earlier.astype(F32).astype(BF16), hits)
+    slots = lane_iota(rows, experts * capacity).astype(F32)
+    for k, pick_ref in enumerate((pick0_ref, pick1_ref)):
+        slot = jnp.sum(jnp.where(match[k], before, 0.0), -1, keepdims=True)
+        place = routes[:, k : k + 1] * capacity + slot
+        pick_ref[...] = (slots == place).astype(F32).astype(BF16)
+    load_g.wait()
+    send_dy[...] = mm(pick0_ref[...] + pick1_ref[...], g_ref[...], 0, 0).astype(BF16)
+    moves = []
+
+    def move(source, target):
+        number = len(moves)
+        moves.append(
+            exchange_start(
+                source, target, ex_send.at[number], ex_receive.at[number], local.at[7 + number], expert, shard, capacity
+            )
+        )
+        return moves[-1]
+
     first_w.second()
     second_w.first()
     for copy in small:
@@ -223,7 +338,6 @@
         for by in (1, 2, 3):
             piece = jnp.where(lax.rem(shard + SIDE - by, SIDE) == place, small_ref[by - 1].astype(F32), piece)
         pieces.append(piece[:, : width // SIDE])
-    lane = lane_iota(rows)
     both = jnp.concatenate(pieces, 1)
     vectors = both[experts : experts + 8, :]
     ln_ref[...] = vectors
@@ -232,6 +346,7 @@
     first_w.third()
     second_w.second()
     first_w.finish()
+    dy_move = move(send_dy, g_rows_ref)
     keep_first = pltpu.make_async_copy(wq_ref, wq_out, local.at[1])
     keep_first.start()
     qkv_ref[...] = mm(h1, wq_ref[...]).astype(BF16)
@@ -266,41 +381,19 @@
     e = jnp.exp(logits - jnp.max(logits, -1, keepdims=True))
     gates = e / jnp.sum(e, -1, keepdims=True)
     gates_ref[...] = gates
-    diagonal = lax.broadcasted_iota(jnp.int32, (rows, rows), 0) == lane_iota(rows, rows)
-    routes = mm(diagonal.astype(F32).astype(BF16), routes_ref[...].astype(F32).astype(BF16), 1, 1)
-    lane_number = lane.astype(F32)
-    match = [lane_number == routes[:, k : k + 1] for k in range(2)]
-    routes_out[...] = jnp.where(lane == 0, routes[:, 0:1], routes[:, 1:2])
-    hits = (match[0] | match[1]).astype(F32).astype(BF16)
-    earlier = lax.broadcasted_iota(jnp.int32, (rows, rows), 0) > lane_iota(rows, rows)
-    before = mm(earlier.astype(F32).astype(BF16), hits)
-    slots = lane_iota(rows, experts * capacity).astype(F32)
-    load_g.wait()
-    g = g_ref[...].astype(F32)
-    picks, grads = [], []
+    shares = []
     for k in range(2):
-        slot = jnp.sum(jnp.where(match[k], before, 0.0), -1, keepdims=True)
-        place = routes[:, k : k + 1] * capacity + slot
-        picks.append((slots == place).astype(F32).astype(BF16))
         chosen = jnp.sum(jnp.where(match[k], gates, 0.0), -1, keepdims=True)
-        grads.append((chosen * g).astype(BF16))
-    pick0_ref[...] = picks[0]
-    pick1_ref[...] = picks[1]
-    moves = []
-
-    def move(source, target):
-        number = len(moves)
-        moves.append(
-            exchange_start(
-                source, target, ex_send.at[number], ex_receive.at[number], local.at[7 + number], expert, shard, capacity
-            )
-        )
-        return moves[-1]
-
-    send_z[...] = mm(picks[0] + picks[1], h2, 0, 0).astype(BF16)
+        high = chosen.astype(BF16)
+        rest = chosen - high.astype(F32)
+        middle = rest.astype(BF16)
+        rest = rest - middle.astype(F32)
+        share = jnp.where(lane == 0, high.astype(F32), jnp.where(lane == 1, middle.astype(F32), rest))
+        shares.append(jnp.where(lane < 3, share, 0.0).astype(BF16))
+    both_picks = pick0_ref[...] + pick1_ref[...]
+    send_z[:, :width] = mm(both_picks, h2, 0, 0).astype(BF16)
+    send_z[:, width:] = (mm(pick0_ref[...], shares[0], 0, 0) + mm(pick1_ref[...], shares[1], 0, 0)).astype(BF16)
     z_move = move(send_z, z_ref)
-    send_dy[...] = (mm(picks[0], grads[0], 0, 0) + mm(picks[1], grads[1], 0, 0)).astype(BF16)
-    dy_move = move(send_dy, dy_ref)
     for copy in small:
         copy.wait_send()
     for gather in (first_w, second_w):
@@ -318,64 +411,60 @@
 
     rows_ref[...] = jnp.zeros_like(rows_ref)
 
-    def activate(number, _):
+    z = z_ref.at[:, pl.ds(0, width)]
+    exchange_wait(*dy_move)
+    share = z_ref[:, width:].astype(F32)
+    dy_ref[...] = (g_rows_ref[...].astype(F32) * (share[:, 0:1] + share[:, 1:2] + share[:, 2:3])).astype(BF16)
+    after, before, across = [lax.rem(shard + by, SIDE) for by in (1, 3, 2)]
+    halves = []
+
+    def pass_halves(place, source, target, at=slice(None)):
+        rows_each = source.shape[0] // SIDE
+        for number, peer in enumerate((after, before)):
+            start = pl.multiple_of(across * rows_each + number * (rows_each // 2), 16)
+            copy = remote(
+                source.at[pl.ds(start, rows_each // 2), at], target.at[number, :, at],
+                half_send.at[place, number], half_receive.at[place, number], expert, peer,
+            )
+            copy.start()
+            halves.append(copy)
+
+    def activate(number):
         at = columns(number)
-        u = mm(z_ref[...], w1_ref[:, at])
+        u = mm(z[...], w1_ref[:, at])
         phi = 0.5 * (1.0 + lax.erf(u * (2.0**-0.5)))
         density = jnp.exp(-0.5 * u * u) * 0.3989422804014327
         slope_ref[:, at] = phi + u * density
         a = (u * phi).astype(BF16)
         a_ref[:, at] = a
         rows_ref[...] += mm(a, w2_ref[at, :])
+        gw2_ref[at, :] = mm(a, dy_ref[...], 0, 0).astype(BF16)
+
+    activate(across)
+    pass_halves(0, gw2_ref, side2_out)
+
+    def activate_others(step, _):
+        activate(lax.rem(across + step, SIDE))
         return 0
 
-    lax.fori_loop(0, blocks, activate, 0)
+    lax.fori_loop(1, blocks, activate_others, 0)
     y_ref[...] = rows_ref[...].astype(BF16)
     move(y_ref, y_out)
-    exchange_wait(*dy_move)
-
-    after, before, across = [lax.rem(shard + by, SIDE) for by in (1, 3, 2)]
-    halves = []
-
-    def pass_halves(place, source, target):
-        rows_each = source.shape[0] // SIDE
-        for number, peer in enumerate((after, before)):
-            start = pl.multiple_of(across * rows_each + number * (rows_each // 2), 16)
-            copy = remote(
-                source.at[pl.ds(start, rows_each // 2), :], target.at[number],
-                half_send.at[place, number], half_receive.at[place, number], expert, peer,
-            )
-            copy.start()
-            halves.append(copy)
-
-    def out_grads(number):
-        at = columns(number)
-        gw2_ref[at, :] = mm(a_ref[:, at], dy_ref[...], 0, 0).astype(BF16)
-
-    out_grads(across)
-    pass_halves(0, gw2_ref, side2_out)
-
-    def other_grads(step, _):
-        out_grads(lax.rem(across + step, SIDE))
-        return 0
-
-    lax.fori_loop(1, blocks, other_grads, 0)
+
     keep_gw2 = pltpu.make_async_copy(gw2_ref, gw2_out, local.at[11])
     keep_gw2.start()
     rows_ref[...] = jnp.zeros_like(rows_ref)
 
-    def in_grads(number, _):
-        at = columns(number)
+    for number in range(blocks):
+        at = slice(number * block, (number + 1) * block)
         da = mm(dy_ref[...], w2_ref[at, :], 1, 1)
         du = (da * slope_ref[:, at]).astype(BF16)
         rows_ref[...] += mm(du, w1_ref[:, at], 1, 1)
-        gw1_ref[:, at] = mm(z_ref[...], du, 0, 0).astype(BF16)
-        return 0
-
-    lax.fori_loop(0, blocks, in_grads, 0)
+        gw1_ref[:, at] = mm(z[...], du, 0, 0).astype(BF16)
+        pass_halves(1 + number, gw1_ref, side1_out, at)
+
     dz_ref[...] = rows_ref[...].astype(BF16)
     move(dz_ref, dz_out)
-    pass_halves(1, gw1_ref, side1_out)
     keep_gw1 = pltpu.make_async_copy(gw1_ref, gw1_out, local.at[12])
     keep_gw1.start()
     keep_gw2.wait()
@@ -422,7 +511,11 @@
             pltpu.VMEM((3, 48, 256), BF16),
             pltpu.VMEM((width, 3 * width), BF16),
             pltpu.VMEM((width, width), BF16),
-            *[pltpu.VMEM((slots, width), BF16)] * 4,
+            pltpu.VMEM((slots, width + LANES), BF16),
+            pltpu.VMEM((slots, width), BF16),
+            pltpu.VMEM((slots, width + LANES), BF16),
+            pltpu.VMEM((slots, width), BF16),
+            pltpu.VMEM((slots, width), BF16),
             pltpu.VMEM((width, hidden), BF16),
             pltpu.VMEM((hidden, width), BF16),
             pltpu.VMEM((slots, hidden), BF16),
@@ -432,14 +525,14 @@
             pltpu.VMEM((slots, width), F32),
             pltpu.VMEM((slots, width), BF16),
             pltpu.VMEM((slots, width), BF16),
-            pltpu.SemaphoreType.DMA((2, 9)),
-            pltpu.SemaphoreType.DMA((2, 8)),
+            pltpu.SemaphoreType.DMA((2, 3, 15)),
+            pltpu.SemaphoreType.DMA((2, 3, 15)),
             pltpu.SemaphoreType.DMA((3,)),
             pltpu.SemaphoreType.DMA((3,)),
             pltpu.SemaphoreType.DMA((4, 31)),
             pltpu.SemaphoreType.DMA((4, 31)),
-            pltpu.SemaphoreType.DMA((2, 2)),
-            pltpu.SemaphoreType.DMA((2, 2)),
+            pltpu.SemaphoreType.DMA((5, 2)),
+            pltpu.SemaphoreType.DMA((5, 2)),
             pltpu.SemaphoreType.DMA((13,)),
         ],
         compiler_params=pltpu.CompilerParams(
@@ -601,7 +694,8 @@
     for copy in load_second:
         copy.wait()
     join(part2, side2)
-    grads_second = pass_on(part2, came2, 0, rows2 // 2)
+    early = rows2 // 4
+    grads_second = pass_on(part2, came2, 0, early)
     for copy in load_heads:
         copy.wait()
     scale = HEAD_DIM ** (-0.5)
@@ -713,7 +807,7 @@
     along_shard = [
         go(piece.at[turn(shard, by)], third_in.at[by - 1], expert, turn(shard, by)) for by in (2, 1, 3)
     ]
-    grads_second += pass_on(part2, came2, rows2 // 2, rows2 // 2)
+    grads_second += pass_on(part2, came2, early, rows2 - early)
     for copy in small_second:
         copy.wait_recv()
     s_out[2] = four(s_out[1], s_in[6], s_in[7], s_in[8]).astype(BF16)

time: 170 us -> 161 us (0.947)
  Pallas kernels: 169 us -> 159 us
    pallas_call x1, Pallas kernels: 91.6 us -> 85.3 us  [forward(): pl.pallas_call(functools.partial(main_kernel, experts, capacity), out_sha...]
    pallas_call x1, Pallas kernels: 71.4 us -> 68.2 us  [tail(): pl.pallas_call(tail_kernel, out_shape=(jax.ShapeDtypeStruct((tokens, widt...]
where the time goes in v4:
time: 161 us; the launch traced here: 160 us
  Pallas kernels  159 us (99%)
    pallas_call x1, Pallas kernels, forward(): pl.pallas_call(functools.partial(main_kernel, experts, capacity), out_sha...  85.3 us
    pallas_call x1, Pallas kernels, tail(): pl.pallas_call(tail_kernel, out_shape=(jax.ShapeDtypeStruct((tokens, widt...  68.2 us
    pallas_call x1, Pallas kernels, widen(): pl.pallas_call(functools.partial(widen_kernel, experts), out_shape=[jax.S...  5.84 us

profile of v4, /device:TPU:1, one launch (start us, length us, event | category | flops | bytes accessed | tf_op | source)
XLA Modules:
  0.0 160.2 jit_solution(15893315277797248870)
XLA Ops:
  0.6 85.3 %forward_and_experts.1 = (f32[197,128]{1,0:T(8,128)}, bf16[768,2304]{1,0:T(8,128)(2,1)}, bf16[768,768]{1,0:T(8,128)(2,1)}, bf16[128,768]{1,0:T(8,128)(2,1)}, f32...) custom-call(bf16[197,768]{1,0:T(8,128)(2,1)} %x_in.3, ...), custom_call_target="tpu_custom_call" | custom-call | flops 14495514624 | bytes 50331648 | tf_op jit(solution)/shard_map/forward_and_experts/pallas_call | solution.py:483
  86.0 68.2 %backward_and_sums.1 = (bf16[197,768]{1,0:T(8,128)(2,1)}, f32[197,768]{1,0:T(8,128)}, bf16[192,2304]{1,0:T(8,128)(2,1)}, bf16[192,768]{1,0:T(8,128)(2,1)}, f32[1...) custom-call(bf16[197,768]{1,0:T(8,128)(2,1)} %x_in.3, bf16[197,768]{1,0:T(8,128)(2,1)} %g_in.3, ...), custom_call_target="tpu_custom_call" | custom-call | flops 3253469184 | bytes 50331648 | tf_op jit(solution)/shard_map/backward_and_sums/pallas_call | solution.py:869
  154.2 5.8 %widen_outputs.1 = (bf16[197,768]{1,0:T(8,128)(2,1)}, f32[197,768]{1,0:T(8,128)}, f32[192]{0:T(256)}, f32[192]{0:T(256)}, f32[192,2304]{1,0:T(8,128)}, /*index=5...) custom-call(bf16[197,768]{1,0:T(8,128)(2,1)} %get-tuple-element.65.r, ...), custom_call_target="tpu_custom_call" | custom-call | bytes 13631488 | tf_op jit(solution)/shard_map/widen_outputs/pallas_call | solution.py:971

commit v5 on v4

--- a/solution.py
+++ b/solution.py
@@ -259,11 +259,14 @@
 def main_kernel(
     experts, capacity, x_in, g_in, routes_ref, wq_shard, wp_shard, router_ref, gain1_ref, bias1_ref, gain2_ref, bias2_ref,
     w1_in, w2_in,
-    routes_out, wq_out, wp_out, ws_ref, ln_ref, qkv_ref, lse_ref, o_ref, x2_ref, gates_ref, pick0_ref, pick1_ref,
-    y_out, dz_out, gw1_out, gw2_out, side1_out, side2_out,
+    mixed_ref, dx_ref, gwq_ref, gwp_ref, small_out, gw1_out, gw2_out, y_out, dz_out,
+    routes_out, ws_ref, ln_ref, qkv_ref, lse_ref, o_ref, x2_ref, gates_ref, pick0_ref, pick1_ref,
     x_ref, g_ref, own_ref, small_ref, wq_ref, wp_ref, send_z, send_dy, z_ref, g_rows_ref, dy_ref,
-    w1_ref, w2_ref, a_ref, slope_ref, gw1_ref, gw2_ref, rows_ref, y_ref, dz_ref,
-    sends, receives, s_send, s_receive, ex_send, ex_receive, half_send, half_receive, local,
+    w1_ref, w2_ref, a_ref, slope_ref, gw1_ref, gw2_ref, side1_ref, side2_ref, rows_ref,
+    do_ref, dqkv_ref, h1_ref, summed, side, first_in, second, second_in, third_in, piece, line, plane, gathered,
+    s_ref, s_pair, s_sum, s_in, s_out, s_other,
+    sends, receives, mini_send, mini_receive, ex_send, ex_receive, half_send, half_receive, local,
+    send, receive, s_send, s_receive, g_send, g_receive,
 ):
     rows, width = x_ref.shape
     load_x = pltpu.make_async_copy(x_in, x_ref, local.at[3])
@@ -285,7 +288,7 @@
     small = []
     for by in (1, 2, 3):
         copy = remote(
-            own_ref, small_ref.at[by - 1], s_send.at[by - 1], s_receive.at[by - 1], expert, lax.rem(shard + by, SIDE)
+            own_ref, small_ref.at[by - 1], mini_send.at[by - 1], mini_receive.at[by - 1], expert, lax.rem(shard + by, SIDE)
         )
         copy.start()
         small.append(copy)
@@ -334,10 +337,10 @@
         copy.wait_recv()
     pieces = []
     for place in range(SIDE):
-        piece = own_ref[...].astype(F32)
+        strip = own_ref[...].astype(F32)
         for by in (1, 2, 3):
-            piece = jnp.where(lax.rem(shard + SIDE - by, SIDE) == place, small_ref[by - 1].astype(F32), piece)
-        pieces.append(piece[:, : width // SIDE])
+            strip = jnp.where(lax.rem(shard + SIDE - by, SIDE) == place, small_ref[by - 1].astype(F32), strip)
+        pieces.append(strip[:, : width // SIDE])
     both = jnp.concatenate(pieces, 1)
     vectors = both[experts : experts + 8, :]
     ln_ref[...] = vectors
@@ -347,32 +350,29 @@
     second_w.second()
     first_w.finish()
     dy_move = move(send_dy, g_rows_ref)
-    keep_first = pltpu.make_async_copy(wq_ref, wq_out, local.at[1])
-    keep_first.start()
     qkv_ref[...] = mm(h1, wq_ref[...]).astype(BF16)
     scale = HEAD_DIM ** (-0.5)
-    lse_all = jnp.zeros((rows, LANES), F32)
-    for pair in range(width // LANES):
-        if pair == 2:
-            second_w.third()
-        at = pair * LANES
-        q = qkv_ref[:, at : at + LANES]
-        k = qkv_ref[:, width + at : width + at + LANES]
-        v = qkv_ref[:, 2 * width + at : 2 * width + at + LANES]
-        halves = []
+    lse_ref[...] = jnp.zeros((rows, LANES), F32)
+
+    def attend(pair, _):
+        at = [pl.ds(pl.multiple_of(third * width + pair * LANES, LANES), LANES) for third in range(3)]
+        q, k, v = qkv_ref[:, at[0]], qkv_ref[:, at[1]], qkv_ref[:, at[2]]
+        parts = []
         for half in range(2):
             own = (lane // HEAD_DIM) == half
             s = mm(jnp.where(own, q, jnp.zeros_like(q)), k, 1, 1) * scale
             top = jnp.max(s, -1, keepdims=True)
             e = jnp.exp(s - top)
             total = jnp.sum(e, -1, keepdims=True)
-            lse_all = jnp.where(lane == 2 * pair + half, top + jnp.log(total), lse_all)
-            halves.append(mm((e / total).astype(BF16), v))
-        o_ref[:, at : at + LANES] = jnp.where(lane < HEAD_DIM, halves[0], halves[1]).astype(BF16)
-    lse_ref[...] = lse_all
+            lse_ref[...] = jnp.where(lane == 2 * pair + half, top + jnp.log(total), lse_ref[...])
+            parts.append(mm((e / total).astype(BF16), v))
+        o_ref[:, at[0]] = jnp.where(lane < HEAD_DIM, parts[0], parts[1]).astype(BF16)
+        return 0
+
+    lax.fori_loop(0, 2, attend, 0)
+    second_w.third()
+    lax.fori_loop(2, width // LANES, attend, 0)
     second_w.finish()
-    keep_second = pltpu.make_async_copy(wp_ref, wp_out, local.at[2])
-    keep_second.start()
     x2 = x + mm(o_ref[...], wp_ref[...])
     x2_ref[...] = x2
     normed2, _ = normalize(x2)
@@ -398,8 +398,6 @@
         copy.wait_send()
     for gather in (first_w, second_w):
         gather.drain()
-    keep_first.wait()
-    keep_second.wait()
     load_w1.wait()
     load_w2.wait()
     block = width
@@ -434,129 +432,39 @@
         u = mm(z[...], w1_ref[:, at])
         phi = 0.5 * (1.0 + lax.erf(u * (2.0**-0.5)))
         density = jnp.exp(-0.5 * u * u) * 0.3989422804014327
-        slope_ref[:, at] = phi + u * density
+        slope_ref[:, at] = (phi + u * density).astype(BF16)
         a = (u * phi).astype(BF16)
         a_ref[:, at] = a
         rows_ref[...] += mm(a, w2_ref[at, :])
         gw2_ref[at, :] = mm(a, dy_ref[...], 0, 0).astype(BF16)
 
-    activate(across)
-    pass_halves(0, gw2_ref, side2_out)
-
-    def activate_others(step, _):
+    def activate_one(step, _):
         activate(lax.rem(across + step, SIDE))
         return 0
 
-    lax.fori_loop(1, blocks, activate_others, 0)
-    y_ref[...] = rows_ref[...].astype(BF16)
-    move(y_ref, y_out)
-
-    keep_gw2 = pltpu.make_async_copy(gw2_ref, gw2_out, local.at[11])
-    keep_gw2.start()
+    lax.fori_loop(0, 1, activate_one, 0)
+    pass_halves(0, gw2_ref, side2_ref)
+    lax.fori_loop(1, blocks, activate_one, 0)
+    send_dy[...] = rows_ref[...].astype(BF16)
+    move(send_dy, y_out)
+
     rows_ref[...] = jnp.zeros_like(rows_ref)
 
-    for number in range(blocks):
-        at = slice(number * block, (number + 1) * block)
+    def in_grads(number, _):
+        at = columns(number)
         da = mm(dy_ref[...], w2_ref[at, :], 1, 1)
-        du = (da * slope_ref[:, at]).astype(BF16)
+        du = (da * slope_ref[:, at].astype(F32)).astype(BF16)
         rows_ref[...] += mm(du, w1_ref[:, at], 1, 1)
         gw1_ref[:, at] = mm(z[...], du, 0, 0).astype(BF16)
-        pass_halves(1 + number, gw1_ref, side1_out, at)
-
+        return 0
+
+    lax.fori_loop(0, blocks, in_grads, 0)
+    pass_halves(1, gw1_ref, side1_ref)
+
+    dz_ref = send_z.at[:, pl.ds(0, width)]
     dz_ref[...] = rows_ref[...].astype(BF16)
     move(dz_ref, dz_out)
-    keep_gw1 = pltpu.make_async_copy(gw1_ref, gw1_out, local.at[12])
-    keep_gw1.start()
-    keep_gw2.wait()
-    keep_gw1.wait()
-    for copies, keep in moves[2:]:
-        exchange_wait(copies, keep)
-    for copy in halves:
-        copy.wait()
-
-
-def forward(tokens, cotangent, routes, wq, wp, router, vectors, w1, w2, experts, capacity):
-    rows, width = tokens.shape
-    hidden = w1.shape[1]
-    slots = experts * capacity
-    vmem, anywhere = pl.BlockSpec(memory_space=pltpu.VMEM), pl.BlockSpec(memory_space=pl.ANY)
-    return pl.pallas_call(
-        functools.partial(main_kernel, experts, capacity),
-        out_shape=(
-            jax.ShapeDtypeStruct((rows, LANES), F32),
-            jax.ShapeDtypeStruct((width, 3 * width), BF16),
-            jax.ShapeDtypeStruct((width, width), BF16),
-            jax.ShapeDtypeStruct((LANES, width), BF16),
-            jax.ShapeDtypeStruct((8, width), F32),
-            jax.ShapeDtypeStruct((rows, 3 * width), BF16),
-            jax.ShapeDtypeStruct((rows, LANES), F32),
-            jax.ShapeDtypeStruct((rows, width), BF16),
-            jax.ShapeDtypeStruct((rows, width), F32),
-            jax.ShapeDtypeStruct((rows, LANES), F32),
-            jax.ShapeDtypeStruct((rows, slots), BF16),
-            jax.ShapeDtypeStruct((rows, slots), BF16),
-            jax.ShapeDtypeStruct((slots, width), BF16),
-            jax.ShapeDtypeStruct((slots, width), BF16),
-            jax.ShapeDtypeStruct((width, hidden), BF16),
-            jax.ShapeDtypeStruct((hidden, width), BF16),
-            jax.ShapeDtypeStruct((2, width // 8, hidden), BF16),
-            jax.ShapeDtypeStruct((2, hidden // 8, width), BF16),
-        ),
-        in_specs=[anywhere] * 2 + [vmem] + [anywhere] * 2 + [vmem] * 5 + [anywhere] * 2,
-        out_specs=[vmem] + [anywhere] * 2 + [vmem] * 9 + [anywhere] * 6,
-        scratch_shapes=[
-            pltpu.VMEM((rows, width), BF16),
-            pltpu.VMEM((rows, width), BF16),
-            pltpu.VMEM((48, 256), BF16),
-            pltpu.VMEM((3, 48, 256), BF16),
-            pltpu.VMEM((width, 3 * width), BF16),
-            pltpu.VMEM((width, width), BF16),
-            pltpu.VMEM((slots, width + LANES), BF16),
-            pltpu.VMEM((slots, width), BF16),
-            pltpu.VMEM((slots, width + LANES), BF16),
-            pltpu.VMEM((slots, width), BF16),
-            pltpu.VMEM((slots, width), BF16),
-            pltpu.VMEM((width, hidden), BF16),
-            pltpu.VMEM((hidden, width), BF16),
-            pltpu.VMEM((slots, hidden), BF16),
-            pltpu.VMEM((slots, hidden), F32),
-            pltpu.VMEM((width, hidden), BF16),
-            pltpu.VMEM((hidden, width), BF16),
-            pltpu.VMEM((slots, width), F32),
-            pltpu.VMEM((slots, width), BF16),
-            pltpu.VMEM((slots, width), BF16),
-            pltpu.SemaphoreType.DMA((2, 3, 15)),
-            pltpu.SemaphoreType.DMA((2, 3, 15)),
-            pltpu.SemaphoreType.DMA((3,)),
-            pltpu.SemaphoreType.DMA((3,)),
-            pltpu.SemaphoreType.DMA((4, 31)),
-            pltpu.SemaphoreType.DMA((4, 31)),
-            pltpu.SemaphoreType.DMA((5, 2)),
-            pltpu.SemaphoreType.DMA((5, 2)),
-            pltpu.SemaphoreType.DMA((13,)),
-        ],
-        compiler_params=pltpu.CompilerParams(
-            vmem_limit_bytes=58 * MIB, collective_id=1, has_side_effects=True
-        ),
-        cost_estimate=pl.CostEstimate(
-            flops=12 * slots * width * hidden, bytes_accessed=48 * MIB, transcendentals=2 * slots * hidden
-        ),
-        name="forward_and_experts",
-    )(tokens, cotangent, routes, wq, wp, router, *vectors, w1, w2)
-
-
-def tail_kernel(
-    x_in, g_in, routes_in, wq_in, wp_in, ws_in, ln_in, qkv_in, lse_in, o_in, x2_in, gates_in, pick0_in, pick1_in,
-    y_in, dz_in, gw1_in, gw2_in, side1_in, side2_in,
-    mixed_ref, dx_ref, gwq_ref, gwp_ref, small_ref, gw1_ref, gw2_ref,
-    x_ref, g_ref, routes_ref, wq_ref, wp_ref, ws_ref, ln_ref, qkv_ref, lse_ref, o_ref, x2_ref, gates_ref,
-    pick0_ref, pick1_ref, y_ref, dz_ref, side1, side2, part1, part2, came1, came2, do_ref, dqkv_ref, h1_ref,
-    theirs, ours, paired, summed, side, first_in, second, second_in, third_in, piece, line, plane, gathered,
-    s_ref, s_pair, s_sum, s_in, s_out, s_other,
-    loads, send, receive, s_send, s_receive, g_send, g_receive,
-):
-    expert, shard = lax.axis_index("expert"), lax.axis_index("wshard")
-    core = lax.rem(expert, 2)
+
     x_at, z_at = lax.rem(expert // 2, SIDE), expert // 8
     sibling = expert + 1 - 2 * core
     first, second_at = x_at * (1 - core) + z_at * core, z_at * (1 - core) + x_at * core
@@ -571,48 +479,7 @@
     def on_second(by):
         return expert + (turn(second_at, by) - second_at) * second_step
 
-    load_count = [0]
-
-    def load(source, target):
-        copy = pltpu.make_async_copy(source, target, loads.at[load_count[0]])
-        load_count[0] += 1
-        copy.start()
-        return copy
-
-    rows1, rows2 = part1.shape[1], part2.shape[1]
-
-    def shard_rows(ref, by, rows):
-        return ref.at[pl.ds(pl.multiple_of(turn(shard, by) * rows, 16), rows), :]
-
-    load_first = [load(side1_in, side1)] + [
-        load(shard_rows(gw1_in, by, rows1), part1.at[number]) for number, by in enumerate((1, 3))
-    ]
-    load_out = [
-        load(*pair) for pair in (
-            (y_in, y_ref), (pick0_in, pick0_ref), (pick1_in, pick1_ref), (x2_in, x2_ref), (g_in, g_ref),
-            (gates_in, gates_ref), (routes_in, routes_ref),
-        )
-    ]
-    load_gates = [
-        load(*pair) for pair in (
-            (dz_in, dz_ref), (ws_in, ws_ref), (ln_in, ln_ref), (wp_in, wp_ref), (o_in, o_ref), (x_in, x_ref),
-        )
-    ]
-    load_heads = [load(qkv_in, qkv_ref), load(lse_in, lse_ref)]
-    load_second = [load(side2_in, side2)] + [
-        load(shard_rows(gw2_in, by, rows2), part2.at[number]) for number, by in enumerate((1, 3))
-    ]
-    load_last = [load(wq_in, wq_ref)]
-    load_own = [
-        load(shard_rows(gw1_in, 0, rows1), part1.at[2]), load(shard_rows(gw2_in, 0, rows2), part2.at[2])
-    ]
-
-    greet(
-        [(sibling, shard)]
-        + [(on_first(by), shard) for by in (1, 2, 3)]
-        + [(on_second(by), shard) for by in (1, 2, 3)]
-        + [(expert, turn(shard, by)) for by in (1, 2, 3)]
-    )
+    rows1, rows2 = width // SIDE, w1_ref.shape[1] // SIDE
     started = []
     counts = {}
 
@@ -630,46 +497,80 @@
     def add(left, right):
         return (left.astype(F32) + right.astype(F32)).astype(BF16)
 
-    def join(part, came_half):
-        half = part.shape[1] // 2
-        part[0, :half] = add(part[0, :half], came_half[0])
-        part[1, half:] = add(part[1, half:], came_half[1])
-
-    def pass_on(part, came, start, count):
-        at = pl.ds(start, count)
-        return [
-            go(
-                part.at[number, at], came.at[number, at], expert, turn(shard, by), g_send, g_receive, "expert"
+    def shard_rows(by, each, start, count):
+        return pl.ds(pl.multiple_of(turn(shard, by) * each + start, 16), count)
+
+    def join(ref, came_half, each):
+        for number, by in enumerate((1, 3)):
+            at = shard_rows(by, each, number * (each // 2), each // 2)
+            ref[at, :] = add(ref[at, :], came_half[number])
+
+    def pass_on(ref, came, each, start, count):
+        copies = []
+        for number, by in enumerate((1, 3)):
+            landing = pl.ds(number * each + start, count)
+            copies.append(
+                go(
+                    ref.at[shard_rows(by, each, start, count), :], came.at[landing, :], expert, turn(shard, by),
+                    g_send, g_receive, "expert",
+                )
             )
-            for number, by in enumerate((1, 3))
-        ]
-
-    for copy in load_first:
-        copy.wait()
-    join(part1, side1)
-    grads_first = pass_on(part1, came1, 0, rows1)
-
-    for copy in load_out:
-        copy.wait()
+        return copies
+
+    def final_sum(ref, came, each, target, number):
+        own = shard_rows(0, each, 0, each)
+        ref[own, :] = (
+            ref[own, :].astype(F32) + came[:each, :].astype(F32) + came[each : 2 * each, :].astype(F32)
+        ).astype(BF16)
+        copy = pltpu.make_async_copy(ref.at[own, :], target, local.at[number])
+        copy.start()
+        return copy
+
+    def their(chunk):
+        return w1_ref.at[:, pl.ds(chunk * block, block)]
+
+    def our(chunk):
+        return w1_ref.at[:, pl.ds(pl.multiple_of((SIDE + chunk) * block, LANES), block)]
+
+    def paired(chunk):
+        start = 2 * width + chunk // 2 * width
+        return w2_ref.at[pl.ds(pl.multiple_of(start, 16), width), pl.ds(pl.multiple_of(chunk % 2 * block, LANES), block)]
+
+    block = width // 2
+    for copy in halves[2:]:
+        copy.wait_recv()
+    join(gw1_ref, side1_ref, rows1)
+    grads_first = pass_on(gw1_ref, a_ref, rows1, 0, rows1)
+    exchange_wait(*moves[2])
+    load_y = pltpu.make_async_copy(y_out, g_rows_ref, local.at[1])
+    load_y.start()
+    for copy in halves[:2]:
+        copy.wait_recv()
+    join(gw2_ref, side2_ref, rows2)
+    early = rows2 // 4
+    grads_second = pass_on(gw2_ref, w2_ref, rows2, 0, early)
+    load_y.wait()
     rows, width = x_ref.shape
     lane = lane_iota(rows)
     g = g_ref[...].astype(F32)
     x2 = x2_ref[...]
     gates = gates_ref[...]
-    routes = routes_ref[...]
+    routes = routes_out[...]
     out = x2
     dgates = jnp.zeros((rows, LANES), F32)
     for k, pick_ref in enumerate((pick0_ref, pick1_ref)):
         match = lane.astype(F32) == routes[:, k : k + 1]
-        picked = mm(pick_ref[...], y_ref[...])
+        picked = mm(pick_ref[...], g_rows_ref[...])
         chosen = jnp.sum(jnp.where(match, gates, 0.0), -1, keepdims=True)
         out = out + chosen * picked
         dgates = jnp.where(match, jnp.sum(g * picked, -1, keepdims=True), dgates)
     mixed_ref[...] = out.astype(BF16)
     dl = (gates * (dgates - jnp.sum(gates * dgates, -1, keepdims=True))).astype(BF16)
-    for copy in load_gates:
-        copy.wait()
-    dh2 = mm(pick0_ref[...] + pick1_ref[...], dz_ref[...]) + mm(dl, ws_ref[...])
+    exchange_wait(*moves[3])
+    load_dz = pltpu.make_async_copy(dz_out, dy_ref, local.at[2])
+    load_dz.start()
+    load_dz.wait()
+    dh2 = mm(pick0_ref[...] + pick1_ref[...], dy_ref[...]) + mm(dl, ws_ref[...])
     gain1, bias1 = ln_ref[0:1, :], ln_ref[1:2, :]
     gain2, bias2 = ln_ref[2:3, :], ln_ref[3:4, :]
     n2, r2 = normalize(x2)
@@ -684,25 +585,18 @@
     block = width // 2
     mine = pl.ds(pl.multiple_of(core * block, LANES), block)
     others = pl.ds(pl.multiple_of((1 - core) * block, LANES), block)
-    theirs[3] = mm(o_ref[...], do_ref[:, others], 0, 0).astype(BF16)
+    their(3)[...] = mm(o_ref[...], do_ref[:, others], 0, 0).astype(BF16)
     pair = [None] * SIDE
-    pair[3] = go(theirs.at[3], paired.at[3], sibling, shard)
-    ours[3] = mm(o_ref[...], do_ref[:, mine], 0, 0).astype(BF16)
+    pair[3] = go(their(3), paired(3), sibling, shard)
+    our(3)[...] = mm(o_ref[...], do_ref[:, mine], 0, 0).astype(BF16)
     do_ref[...] = mm(dx2b, wp_ref[...], 1, 1).astype(BF16)
     n1, r1 = normalize(x_ref[...].astype(F32))
     h1_ref[...] = (n1 * gain1 + bias1).astype(BF16)
-    for copy in load_second:
-        copy.wait()
-    join(part2, side2)
-    early = rows2 // 4
-    grads_second = pass_on(part2, came2, 0, early)
-    for copy in load_heads:
-        copy.wait()
     scale = HEAD_DIM ** (-0.5)
     low = lane < HEAD_DIM
 
     def heads(start):
-        for step in range(block // LANES):
+        def one(step, _):
             at = [
                 pl.ds(pl.multiple_of(third * width + start + step * LANES, LANES), LANES) for third in range(3)
             ]
@@ -720,18 +614,21 @@
                 parts.append((mm(ds, k) * scale, mm(ds, q, 0, 0) * scale, mm(p.astype(BF16), do, 0, 0)))
             for third, (left, right) in enumerate(zip(*parts)):
                 dqkv_ref[:, at[third]] = jnp.where(low, left, right).astype(BF16)
+            return 0
+
+        lax.fori_loop(0, block // LANES, one, 0)
 
     def weight_grads(target, start):
         for third in range(3):
             columns = pl.ds(pl.multiple_of(third * width + start, LANES), block)
-            target[third] = mm(h1_ref[...], dqkv_ref[:, columns], 0, 0).astype(BF16)
+            target(third)[...] = mm(h1_ref[...], dqkv_ref[:, columns], 0, 0).astype(BF16)
 
     heads((1 - core) * block)
-    weight_grads(theirs, (1 - core) * block)
+    weight_grads(their, (1 - core) * block)
     for third in range(3):
-        pair[third] = go(theirs.at[third], paired.at[third], sibling, shard)
+        pair[third] = go(their(third), paired(third), sibling, shard)
     heads(core * block)
-    weight_grads(ours, core * block)
+    weight_grads(our, core * block)
     for copy in pair:
         copy.wait_recv()
 
@@ -739,7 +636,7 @@
 
     def add_pair(number):
         chunk = turn(first, order[number])
-        summed[number] = add(ours[chunk], paired[chunk])
+        summed[number] = add(our(chunk)[...], paired(chunk)[...])
 
     wide = s_ref.shape[1]
     part, quarter, half = wide // 2, wide // 4, 2 * wide
@@ -749,8 +646,6 @@
     add_pair(1)
     add_pair(2)
 
-    for copy in load_last:
-        copy.wait()
     dh1 = mm(dqkv_ref[...], wq_ref[...], 1, 1)
     g_gain1 = jnp.sum(dh1 * n1, 0, keepdims=True)
     g_bias1 = jnp.sum(dh1, 0, keepdims=True)
@@ -807,13 +702,11 @@
     along_shard = [
         go(piece.at[turn(shard, by)], third_in.at[by - 1], expert, turn(shard, by)) for by in (2, 1, 3)
     ]
-    grads_second += pass_on(part2, came2, early, rows2 - early)
+    grads_second += pass_on(gw2_ref, w2_ref, rows2, early, rows2 - early)
     for copy in small_second:
         copy.wait_recv()
     s_out[2] = four(s_out[1], s_in[6], s_in[7], s_in[8]).astype(BF16)
     small_back = go_small(s_out.at[2], s_other, sibling, shard)
-    for copy in load_own:
-        copy.wait()
     for copy in along_shard:
         copy.wait_recv()
     line[second_at] = four(piece[shard], third_in[0], third_in[1], third_in[2]).astype(BF16)
@@ -821,8 +714,8 @@
         go(line.at[second_at], line.at[second_at], on_second(by), shard) for by in (2, 1, 3)
     ]
     small_back.wait_recv()
-    small_ref[s_mine, :] = s_out[2].astype(F32)
-    small_ref[s_others, :] = s_other[...].astype(F32)
+    small_out[s_mine, :] = s_out[2].astype(F32)
+    small_out[s_others, :] = s_other[...].astype(F32)
     for copy in back_second:
         copy.wait_recv()
     plane[first] = line[...].reshape(wide, line.shape[-1])
@@ -832,7 +725,7 @@
     own_back = go(plane.at[first], gathered.at[first], sibling, shard)
     for copy in grads_first:
         copy.wait_recv()
-    gw1_ref[...] = (part1[2].astype(F32) + came1[0].astype(F32) + came1[1].astype(F32)).astype(BF16)
+    write_first = final_sum(gw1_ref, a_ref, rows1, gw1_out, 11)
     hands = []
     for copy, by in zip(back_first, (2, 1, 3)):
         copy.wait_recv()
@@ -852,78 +745,111 @@
     put(gathered, (1 - core) * block)
     for copy in grads_second:
         copy.wait_recv()
-    gw2_ref[...] = (part2[2].astype(F32) + came2[0].astype(F32) + came2[1].astype(F32)).astype(BF16)
+    write_second = final_sum(gw2_ref, w2_ref, rows2, gw2_out, 12)
+    write_first.wait()
+    write_second.wait()
+    for copy in halves:
+        copy.wait_send()
     for copy in started:
         copy.wait_send()
 
 
-def tail(operands, expert_operands, collective_id):
-    tokens, width = operands[0].shape
-    columns = width // 2
-    rows = width // SIDE
-    hidden = expert_operands[0].shape[1]
-    quarter, part = rows // 4, rows // 2
-    vmem, semaphores = pltpu.VMEM, pltpu.SemaphoreType.DMA
-    anywhere = pl.BlockSpec(memory_space=pl.ANY)
-    everything = (*operands, *expert_operands)
+def block_step(tokens, cotangent, routes, wq, wp, router, vectors, w1, w2, experts, capacity):
+    rows, width = tokens.shape
+    hidden = w1.shape[1]
+    each, block = width // SIDE, width // 2
+    quarter, part = each // 4, each // 2
+    slots = experts * capacity
+    vmem, anywhere = pl.BlockSpec(memory_space=pltpu.VMEM), pl.BlockSpec(memory_space=pl.ANY)
     return pl.pallas_call(
-        tail_kernel,
+        functools.partial(main_kernel, experts, capacity),
         out_shape=(
-            jax.ShapeDtypeStruct((tokens, width), BF16),
-            jax.ShapeDtypeStruct((tokens, width), F32),
-            jax.ShapeDtypeStruct((rows, 3 * width), BF16),
             jax.ShapeDtypeStruct((rows, width), BF16),
-            jax.ShapeDtypeStruct((rows, LANES), F32),
-            jax.ShapeDtypeStruct((rows, hidden), BF16),
+            jax.ShapeDtypeStruct((rows, width), F32),
+            jax.ShapeDtypeStruct((each, 3 * width), BF16),
+            jax.ShapeDtypeStruct((each, width), BF16),
+            jax.ShapeDtypeStruct((each, LANES), F32),
+            jax.ShapeDtypeStruct((each, hidden), BF16),
             jax.ShapeDtypeStruct((hidden // SIDE, width), BF16),
+            jax.ShapeDtypeStruct((slots, width), BF16),
+            jax.ShapeDtypeStruct((slots, width), BF16),
         ),
-        in_specs=[anywhere] * len(everything),
-        out_specs=[pl.BlockSpec(memory_space=vmem)] * 7,
-        scratch_shapes=[vmem(array.shape, array.dtype) for array in operands] + [
-            vmem((2, rows // 2, hidden), BF16),
-            vmem((2, hidden // 8, width), BF16),
-            vmem((3, rows, hidden), BF16),
-            vmem((3, hidden // SIDE, width), BF16),
-            vmem((2, rows, hidden), BF16),
-            vmem((2, hidden // SIDE, width), BF16),
-            vmem((tokens, width), BF16),
-            vmem((tokens, 3 * width), BF16),
-            vmem((tokens, width), BF16),
-            vmem((SIDE, width, columns), BF16),
-            vmem((SIDE, width, columns), BF16),
-            vmem((SIDE, width, columns), BF16),
-            vmem((SIDE, width, columns), BF16),
-            vmem((2, 2 * rows, columns), BF16),
-            vmem((2, width, columns), BF16),
-            vmem((SIDE, SIDE, quarter, columns), BF16),
-            vmem((3, SIDE, quarter, columns), BF16),
-            vmem((3, quarter, columns), BF16),
-            vmem((SIDE, quarter, columns), BF16),
-            vmem((SIDE, quarter, columns), BF16),
-            vmem((SIDE, rows, columns), BF16),
-            vmem((SIDE, rows, columns), BF16),
-            vmem((SIDE, rows, LANES), BF16),
-            vmem((SIDE, rows, LANES), BF16),
-            vmem((SIDE, rows, LANES), BF16),
-            vmem((9, part, LANES), BF16),
-            vmem((3, part, LANES), BF16),
-            vmem((part, LANES), BF16),
-            semaphores((24,)),
-            semaphores((24,)),
-            semaphores((24,)),
-            semaphores((11,)),
-            semaphores((11,)),
-            semaphores((6,)),
-            semaphores((6,)),
+        in_specs=[anywhere] * 2 + [vmem] + [anywhere] * 2 + [vmem] * 5 + [anywhere] * 2,
+        out_specs=[vmem] * 5 + [anywhere] * 4,
+        scratch_shapes=[
+            pltpu.VMEM((rows, LANES), F32),
+            pltpu.VMEM((LANES, width), BF16),
+            pltpu.VMEM((8, width), F32),
+            pltpu.VMEM((rows, 3 * width), BF16),
+            pltpu.VMEM((rows, LANES), F32),
+            pltpu.VMEM((rows, width), BF16),
+            pltpu.VMEM((rows, width), F32),
+            pltpu.VMEM((rows, LANES), F32),
+            pltpu.VMEM((rows, slots), BF16),
+            pltpu.VMEM((rows, slots), BF16),
+            pltpu.VMEM((rows, width), BF16),
+            pltpu.VMEM((rows, width), BF16),
+            pltpu.VMEM((48, 256), BF16),
+            pltpu.VMEM((3, 48, 256), BF16),
+            pltpu.VMEM((width, 3 * width), BF16),
+            pltpu.VMEM((width, width), BF16),
+            pltpu.VMEM((slots, width + LANES), BF16),
+            pltpu.VMEM((slots, width), BF16),
+            pltpu.VMEM((slots, width + LANES), BF16),
+            pltpu.VMEM((slots, width), BF16),
+            pltpu.VMEM((slots, width), BF16),
+            pltpu.VMEM((width, hidden), BF16),
+            pltpu.VMEM((hidden, width), BF16),
+            pltpu.VMEM((slots, hidden), BF16),
+            pltpu.VMEM((slots, hidden), BF16),
+            pltpu.VMEM((width, hidden), BF16),
+            pltpu.VMEM((hidden, width), BF16),
+            pltpu.VMEM((2, width // 8, hidden), BF16),
+            pltpu.VMEM((2, hidden // 8, width), BF16),
+            pltpu.VMEM((slots, width), F32),
+            pltpu.VMEM((rows, width), BF16),
+            pltpu.VMEM((rows, 3 * width), BF16),
+            pltpu.VMEM((rows, width), BF16),
+            pltpu.VMEM((SIDE, width, block), BF16),
+            pltpu.VMEM((2, 2 * each, block), BF16),
+            pltpu.VMEM((2, width, block), BF16),
+            pltpu.VMEM((SIDE, SIDE, quarter, block), BF16),
+            pltpu.VMEM((3, SIDE, quarter, block), BF16),
+            pltpu.VMEM((3, quarter, block), BF16),
+            pltpu.VMEM((SIDE, quarter, block), BF16),
+            pltpu.VMEM((SIDE, quarter, block), BF16),
+            pltpu.VMEM((SIDE, each, block), BF16),
+            pltpu.VMEM((SIDE, each, block), BF16),
+            pltpu.VMEM((SIDE, each, LANES), BF16),
+            pltpu.VMEM((SIDE, each, LANES), BF16),
+            pltpu.VMEM((SIDE, each, LANES), BF16),
+            pltpu.VMEM((9, part, LANES), BF16),
+            pltpu.VMEM((3, part, LANES), BF16),
+            pltpu.VMEM((part, LANES), BF16),
+            pltpu.SemaphoreType.DMA((2, 3, 15)),
+            pltpu.SemaphoreType.DMA((2, 3, 15)),
+            pltpu.SemaphoreType.DMA((3,)),
+            pltpu.SemaphoreType.DMA((3,)),
+            pltpu.SemaphoreType.DMA((4, 31)),
+            pltpu.SemaphoreType.DMA((4, 31)),
+            pltpu.SemaphoreType.DMA((2, 2)),
+            pltpu.SemaphoreType.DMA((2, 2)),
+            pltpu.SemaphoreType.DMA((13,)),
+            pltpu.SemaphoreType.DMA((24,)),
+            pltpu.SemaphoreType.DMA((24,)),
+            pltpu.SemaphoreType.DMA((11,)),
+            pltpu.SemaphoreType.DMA((11,)),
+            pltpu.SemaphoreType.DMA((6,)),
+            pltpu.SemaphoreType.DMA((6,)),
         ],
         compiler_params=pltpu.CompilerParams(
-            vmem_limit_bytes=58 * MIB, collective_id=collective_id, has_side_effects=True
+            vmem_limit_bytes=62 * MIB, collective_id=1, has_side_effects=True
         ),
         cost_estimate=pl.CostEstimate(
-            flops=2 * tokens * width * 14 * width, bytes_accessed=48 * MIB, transcendentals=tokens * tokens * 12
+            flops=12 * slots * width * hidden, bytes_accessed=48 * MIB, transcendentals=2 * slots * hidden
         ),
-        name="backward_and_sums",
-    )(*everything)
+        name="whole_block",
+    )(tokens, cotangent, routes, wq, wp, router, *vectors, w1, w2)
 
 
 def widen_kernel(experts, *refs):
@@ -989,11 +915,10 @@
     rows = tokens.shape[0]
     experts = w_router.shape[1]
     capacity = (5 * rows // 2 + 8 * experts - 1) // (8 * experts) * 8
-    *kept, g_first, g_second, side_first, side_second = forward(
+    *sums, _, _ = block_step(
         tokens, cotangent, routes.T, w_qkv, w_proj, w_router.T, (ln1_gain, ln1_bias, ln2_gain, ln2_bias),
         expert_in[0], expert_out[0], experts, capacity,
     )
-    sums = tail((tokens, cotangent, *kept), (g_first, g_second, side_first, side_second), 3)
     outputs = list(widen(*sums, experts))
     outputs[8] = outputs[8].T
     return tuple(outputs)

time: 161 us -> 160 us (level)
    pallas_call x2 -> x1, Pallas kernels: 154 us -> 153 us  [block_step(): pl.pallas_call(functools.partial(main_kernel, experts, capacity), out_sha...]
where the time goes in v5:
time: 160 us; the launch traced here: 159 us
  Pallas kernels  159 us (99%)
    pallas_call x1, Pallas kernels, block_step(): pl.pallas_call(functools.partial(main_kernel, experts, capacity), out_sha...  153 us
    pallas_call x1, Pallas kernels, widen(): pl.pallas_call(functools.partial(widen_kernel, experts), out_shape=[jax.S...  5.84 us

profile of v5, /device:TPU:1, one launch (start us, length us, event | category | flops | bytes accessed | tf_op | source)
XLA Modules:
  0.0 159.4 jit_solution(14712358557565610586)
XLA Ops:
  0.6 152.7 %whole_block.1 = (bf16[197,768]{1,0:T(8,128)(2,1)}, f32[197,768]{1,0:T(8,128)}, bf16[192,2304]{1,0:T(8,128)(2,1)}, bf16[192,768]{1,0:T(8,128)(2,1)}, f32[192,128...) custom-call(bf16[197,768]{1,0:T(8,128)(2,1)} %x_in.1, ...), custom_call_target="tpu_custom_call" | custom-call | flops 14495514624 | bytes 50331648 | tf_op jit(solution)/shard_map/whole_block/pallas_call | solution.py:764
  153.4 5.8 %widen_outputs.1 = (bf16[197,768]{1,0:T(8,128)(2,1)}, f32[197,768]{1,0:T(8,128)}, f32[192]{0:T(256)}, f32[192]{0:T(256)}, f32[192,2304]{1,0:T(8,128)}, /*index=5...) custom-call(bf16[197,768]{1,0:T(8,128)(2,1)} %get-tuple-element.29.r, ...), custom_call_target="tpu_custom_call" | custom-call | bytes 13631488 | tf_op jit(solution)/shard_map/widen_outputs/pallas_call | solution.py:897
